TPU v7x, 32 devices: a whole 2x2x4 slice. The times are simulated.
32 devices in a mesh: feat: 8 (over y, x, core), dom: 4 (over z).
Axes of the slice: x: 2, y: 2, z: 4, core: 2. Of those that a mesh axis runs over, the one named last changes fastest.
Arguments:
- features: bfloat16 [768, 4096], P('feat', 'dom'), may hold values from -6 to 6
- neigh_one: int32 [4, 15, 512], P('dom'), may hold values from 0 to 1023
- boundary: int32 [4, 8, 128], P('dom', 'feat'), may hold values from 0 to 63
- neigh_two: int32 [4, 256, 10], P('dom', 'feat'), may hold values from 0 to 191
- weight_one: bfloat16 [2, 768, 256], P(None, 'feat'), may hold values from -0.21875 to 0.21875
- weight_two: bfloat16 [2, 256, 256], replicated, may hold values from -0.375 to 0.375
Outputs:
- hidden_two: bfloat16 [4, 256, 256], P('dom', 'feat')
Inputs may be any that keep to these rules, and one draw needn't show every extreme that they name: `neigh_one`: source node of a partition. `boundary`: local layer-one output row of the sending device. `neigh_two`: row of the device's table.
All inputs are finite; a program needn't handle non-finite values.
Results may differ from a plain program's by a relative error of at most 0.0051.
Values may be sent and summed in bfloat16 or wider, within the bound.
No kernel may reach another device: no remote copies, remote signals or barrier semaphores. Data moves between devices by JAX's collectives and lax.ppermute only.
A program may use at most 64 MiB of HBM per device.

v0:
```python
import math

import jax
import jax.numpy as jnp
from jax import lax
from jax.sharding import PartitionSpec as P

FAN1 = 15
FAN2 = 10


def count_matrix(index, width):
    slots = lax.broadcasted_iota(jnp.int32, (index.shape[0], width), 1)
    counts = jnp.zeros((index.shape[0], width), jnp.bfloat16)
    for k in range(index.shape[1]):
        counts = counts + (index[:, k][:, None] == slots).astype(jnp.bfloat16)
    return counts


def on_device(features, neigh_one, boundary, neigh_two, weight_one, weight_two):
    neigh = neigh_one[0]
    fan_count = neigh.shape[0]
    dst_count = neigh.shape[1]
    src_count = features.shape[1]
    block = math.gcd(dst_count, 256)
    blocks = dst_count // block
    neigh_blocks = neigh.reshape(fan_count, blocks, block).transpose(1, 2, 0)

    def block_sum(index):
        counts = count_matrix(index, src_count)
        return lax.dot_general(
            features, counts, (((1,), (1,)), ((), ())), preferred_element_type=jnp.float32
        )

    sums = lax.map(block_sum, neigh_blocks)
    summed = sums.transpose(1, 0, 2).reshape(features.shape[0], dst_count)
    agg = (summed / FAN1).astype(jnp.bfloat16)
    own = features[:, :dst_count]
    dims = (((0,), (0,)), ((), ()))
    term = lax.dot_general(own, weight_one[0], dims, preferred_element_type=jnp.float32)
    pre = lax.psum_scatter(
        term + lax.dot_general(agg, weight_one[1], dims, preferred_element_type=jnp.float32),
        "feat",
        scatter_dimension=0,
        tiled=True,
    )
    hidden = jax.nn.relu(pre).astype(jnp.bfloat16)
    dom_count = lax.axis_size("dom")
    width = hidden.shape[1]
    chosen = count_matrix(boundary[0, 0][:, None], hidden.shape[0])
    picked = jnp.dot(chosen, hidden, preferred_element_type=jnp.float32).astype(jnp.bfloat16)
    outgoing = picked.reshape(dom_count, -1, width)
    incoming = lax.all_to_all(outgoing, "dom", split_axis=0, concat_axis=0, tiled=True)
    table = jnp.concatenate([hidden, incoming.reshape(-1, width)], axis=0)
    index_two = neigh_two[0]
    out_rows = index_two.shape[0]
    counts_two = count_matrix(index_two, table.shape[0])
    gathered = jnp.dot(counts_two, table, preferred_element_type=jnp.float32)
    agg_two = (gathered / FAN2).astype(jnp.bfloat16)
    result = jnp.dot(hidden[:out_rows], weight_two[0], preferred_element_type=jnp.float32)
    result = result + jnp.dot(agg_two, weight_two[1], preferred_element_type=jnp.float32)
    return jax.nn.relu(result).astype(jnp.bfloat16)[None]


def solution(mesh):
    placed = (
        P("feat", "dom"),
        P("dom", None, None),
        P("dom", "feat", None),
        P("dom", "feat", None),
        P(None, "feat", None),
        P(),
    )
    return jax.shard_map(
        on_device, mesh=mesh, in_specs=placed, out_specs=P("dom", "feat", None), check_vma=False
    )
```

profile of v0, /device:TPU:0, one launch (start us, length us, event | category | flops | bytes accessed | tf_op | source)
XLA Modules:
  0.0 72.9 jit_solution(1305397367065341876)
XLA Ops:
  6.5 0.0 reduce-scatter.2.cloned.1.call-start
  6.5 0.8 %reduce = s32[15,512]{1,0:T(8,128)S(1)} reduce(s32[1,15,512]{2,0,1:T(1,128)} %param.9, s32[]{:T(128)} %copy.27), dimensions={0}, to_apply=%param.9.reduce_sub_computation | reduce | bytes 61444 | tf_op args[1]
  7.4 6.4 %while.10 = (s32[]{:T(128)}, f32[2,96,256]{2,1,0:T(8,128)S(1)}, s32[2,256,15]{1,0,2:T(2,128)S(1)}, bf16[96,1024]{1,0:T(8,128)(2,1)}, s32[]{:T(128)}) while((s32[]{:T(128)}, f32[2,96,256]{2,1,0:T(8,128)S(1)}, s32[2,256,15]{1,0,2:T(2,128)S(1)}, bf16[96,1024]{1,0:T(8,128)(2,1)}, s32[]{:T(128)}) %tuple.49), condition=%wide.region_1.2_spmd, body=%wide.region_0.1_spmd.sunk | while | flops 66060288 | bytes 402509 | solution.py:35
  7.5 3.1 %fusion.158 = f32[2,96,256]{2,1,0:T(8,128)S(1)} fusion(f32[2,96,256]{2,1,0:T(8,128)S(1)} %get-tuple-element.126, s32[]{:T(128)S(6)} %copy.22, bf16[96,1024]{1,0:T(8,128)(2,1)} %get-tuple-element.133, s32[256]{0:T(256)S(1)} %bitcast.113, s32[256]{0:T(256)S(1)} %bitcast.114, s32[256]{0:T(256)S(1)} %bitcast.115, s32[256]{0:T(256)S(1)} %bitcast.116, ...), kind=kOutput, calls=%fused_computation.1.clone.1 | convolution fusion | flops 66060288 | bytes 310276 | tf_op jit(solution)/shard_map/while/body/eval_jaxpr/dot_general | solution.py:31
  10.7 3.1 %fusion.158 = f32[2,96,256]{2,1,0:T(8,128)S(1)} fusion(f32[2,96,256]{2,1,0:T(8,128)S(1)} %get-tuple-element.126, s32[]{:T(128)S(6)} %copy.22, bf16[96,1024]{1,0:T(8,128)(2,1)} %get-tuple-element.133, s32[256]{0:T(256)S(1)} %bitcast.113, s32[256]{0:T(256)S(1)} %bitcast.114, s32[256]{0:T(256)S(1)} %bitcast.115, s32[256]{0:T(256)S(1)} %bitcast.116, ...), kind=kOutput, calls=%fused_computation.1.clone.1 | convolution fusion | flops 66060288 | bytes 310276 | tf_op jit(solution)/shard_map/while/body/eval_jaxpr/dot_general | solution.py:31
  13.8 0.0 copy-start.2
  13.8 0.0 copy-start
  13.8 0.9 %copy-done.2 = bf16[96,1024]{1,0:T(8,128)(2,1)S(1)} copy-done((bf16[96,1024]{1,0:T(8,128)(2,1)S(1)}, bf16[96,1024]{1,0:T(8,128)(2,1)}, u32[]{:S(2)}) %copy-start.2) | copy-done | bytes 196632
  14.7 0.1 copy-done
  14.8 0.2 fusion.76
  15.0 1.0 %convolution_add_fusion = f32[512,256]{1,0:T(8,128)} fusion(f32[512,256]{1,0:T(8,128)S(1)} %fusion.76, bf16[96,512]{1,0:T(8,128)(2,1)S(1)} %bitcast.109, bf16[2,96,256]{2,1,0:T(8,128)(2,1)S(1)} %copy-done), kind=kOutput, calls=%fused_computation.63 | convolution fusion | flops 25296896 | bytes 1196032 | tf_op jit(solution)/shard_map/dot_general | solution.py:42
  16.1 0.0 copy-start.3
  16.1 0.0 copy-start.4
  16.1 0.0 reduce-scatter.2.cloned.1.call-update
  16.1 0.7 copy-done.3
  16.8 0.0 copy-start.1
  16.8 36.3 %reduce-scatter.2.cloned.1.call-done = f32[64,256]{1,0:T(8,128)} async-done(((f32[512,256]{1,0:T(8,128)}), f32[64,256]{1,0:T(8,128)}) %reduce-scatter.2.cloned.1.call-update) | async-done | bytes 65552 | tf_op jit(solution)/shard_map/reduce_scatter | solution.py:41
  53.1 0.8 %maximum_convert_fusion = bf16[64,256]{1,0:T(8,128)(2,1)S(1)} fusion(f32[64,256]{1,0:T(8,128)} %reduce-scatter.2.cloned.1.call-done), kind=kLoop, calls=%fused_computation.84 | loop fusion | flops 32768 | bytes 98304 | tf_op jit(solution)/shard_map/convert_element_type | solution.py:47
  53.9 0.0 copy-done.4
  53.9 0.8 %convolution_convert_fusion = bf16[128,256]{1,0:T(8,128)(2,1)} fusion(bf16[64,256]{1,0:T(8,128)(2,1)S(1)} %maximum_convert_fusion, s32[128]{0:T(128)S(1)} %bitcast.128), kind=kOutput, calls=%fused_computation.64 | convolution fusion | flops 4235264 | bytes 98816 | tf_op jit(solution)/shard_map/dot_general | solution.py:51
  54.7 4.6 %all-to-all-start = ((bf16[4,32,256]{2,1,0:T(8,128)(2,1)}), bf16[4,32,256]{2,1,0:T(8,128)(2,1)S(1)}, u32[]{:S(2)}, u32[]{:S(2)}) async-start(bf16[4,32,256]{2,1,0:T(8,128)(2,1)} %bitcast.34), calls=%async_computation.1 | async-start | bytes 131072 | tf_op jit(solution)/shard_map/all_to_all | solution.py:53
  59.4 0.0 copy-done.1
  59.4 0.1 fusion.65
  59.5 5.6 %all-to-all-done = bf16[4,32,256]{2,1,0:T(8,128)(2,1)S(1)} async-done(((bf16[4,32,256]{2,1,0:T(8,128)(2,1)}), bf16[4,32,256]{2,1,0:T(8,128)(2,1)S(1)}, u32[]{:S(2)}, u32[]{:S(2)}) %all-to-all-start) | async-done | bytes 65568 | tf_op jit(solution)/shard_map/all_to_all | solution.py:53
  65.1 1.0 %fusion.63 = bf16[1,32,256]{2,1,0:T(8,128)(2,1)} fusion(f32[32,256]{1,0:T(8,128)S(1)} %fusion.65, bf16[2,256,256]{2,1,0:T(8,128)(2,1)S(1)} %copy-done.1, bf16[128,256]{1,0:T(8,128)(2,1)S(1)} %bitcast.111, bf16[64,256]{1,0:T(8,128)(2,1)S(1)} %maximum_convert_fusion, s32[32]{0:T(128)S(1)} %get-tuple-element.56, s32[32]{0:T(128)S(1)} %get-tuple-element.57, ...), kind=kOutput, calls=%fused_computation.70 | convolution fusion | flops 7823360 | bytes 283648 | tf_op jit(solution)/shard_map/dot_general | solution.py:61
  (12 shorter events, 0.1 us)
Async XLA Ops:
  6.5 46.5 %reduce-scatter.2.cloned.1.call-start = ((), (), s32[]{:S(2)}) async-start(), calls=%async_computation.2 | async-start | bytes 589824 | tf_op jit(solution)/shard_map/reduce_scatter | solution.py:41
  13.8 0.9 %copy-start.2 = (bf16[96,1024]{1,0:T(8,128)(2,1)S(1)}, bf16[96,1024]{1,0:T(8,128)(2,1)}, u32[]{:S(2)}) copy-start(bf16[96,1024]{1,0:T(8,128)(2,1)} %get-tuple-element.140) | copy-start | bytes 589828
  13.8 1.0 %copy-start = (bf16[2,96,256]{2,1,0:T(8,128)(2,1)S(1)}, bf16[2,96,256]{2,1,0:T(8,128)(2,1)}, u32[]{:S(2)}) copy-start(bf16[2,96,256]{2,1,0:T(8,128)(2,1)} %param.12) | copy-start | bytes 294916
  16.1 0.7 copy-start.3
  16.1 37.8 %copy-start.4 = (s32[1,1,128]{2,1,0:T(1,128)S(1)}, s32[1,1,128]{2,1,0:T(1,128)}, u32[]{:S(2)}) copy-start(s32[1,1,128]{2,1,0:T(1,128)} %param.10) | copy-start | bytes 1540
  16.8 42.6 %copy-start.1 = (bf16[2,256,256]{2,1,0:T(8,128)(2,1)S(1)}, bf16[2,256,256]{2,1,0:T(8,128)(2,1)}, u32[]{:S(2)}) copy-start(bf16[2,256,256]{2,1,0:T(8,128)(2,1)} %param.13) | copy-start | bytes 786436
  54.7 10.4 %all-to-all-start = ((bf16[4,32,256]{2,1,0:T(8,128)(2,1)}), bf16[4,32,256]{2,1,0:T(8,128)(2,1)S(1)}, u32[]{:S(2)}, u32[]{:S(2)}) async-start(bf16[4,32,256]{2,1,0:T(8,128)(2,1)} %bitcast.34), calls=%async_computation.1 | async-start | bytes 131072 | tf_op jit(solution)/shard_map/all_to_all | solution.py:53
Sparse Core Ops, SparseCore 0:
  16.2 36.7 reduce-scatter.1
where the time goes:
time: 73.3 us; the launch traced here: 72.9 us
  waiting for transfers between devices  41.9 us (57%)
  between operations  13.5 us (18%)
  matrix products  9.42 us (13%)
  starting transfers between devices  4.62 us (6%)
  local copies, waits for them, and re-layouts  1.72 us (2%)
  other arithmetic  1.69 us (2%)
    reduce_scatter x1, waiting for transfers between devices, on_device(): lax.psum_scatter(term + lax.dot_general(agg, weight_one[1], dims, preferr...  36.3 us
    dot_general x2, matrix products, block_sum(): lax.dot_general(features, counts, (((1,), (1,)), ((), ())), preferred_ele...  6.22 us
    all_to_all x1, waiting for transfers between devices, on_device(): lax.all_to_all(outgoing, 'dom', split_axis=0, concat_axis=0, tiled=True)  5.61 us
    all_to_all x1, starting transfers between devices, on_device(): lax.all_to_all(outgoing, 'dom', split_axis=0, concat_axis=0, tiled=True)  4.62 us
    unnamed x11, local copies, waits for them, and re-layouts  1.61 us
  transfers between devices with their start and end apart: 2, of which 2 were waited for; matrix products, arithmetic and copies ran while one was open for 0% of the time, Pallas kernels for 0%

commit v1 on v0

v1 whole, which is shorter than its diff:
```python
import math

import jax
import jax.numpy as jnp
from jax import lax
from jax.experimental import pallas as pl
from jax.experimental.pallas import tpu as pltpu
from jax.sharding import PartitionSpec as P

FAN1 = 15
FAN2 = 10
CHUNK = 256
COLUMNS_FIRST = (((0,), (0,)), ((), ()))


def counts_of(rows, start, height):
    width = rows[0].shape[1]
    slots = lax.broadcasted_iota(jnp.int32, (height, width), 0).astype(jnp.float32).astype(jnp.bfloat16)
    one = jnp.ones((), jnp.bfloat16)
    zero = jnp.zeros((), jnp.bfloat16)
    counts = None
    for row in rows:
        near = (row - start).astype(jnp.float32).astype(jnp.bfloat16)
        hit = jnp.where(near == slots, one, zero)
        counts = hit if counts is None else counts + hit
    return counts


def partial_kernel(features, own, neigh, weight, partial):
    fan = neigh.shape[0]
    sources = features.shape[1]
    chunk = min(CHUNK, sources)
    rows = [neigh[k] for k in range(fan)]

    def summed_over(start):
        counts = counts_of(rows, start, chunk)
        return jnp.dot(features[:, pl.ds(start, chunk)], counts, preferred_element_type=jnp.float32)

    if sources // chunk <= 8:
        total = summed_over(0)
        for step in range(1, sources // chunk):
            total = total + summed_over(step * chunk)
    else:
        total = lax.fori_loop(
            0,
            sources // chunk,
            lambda step, so_far: so_far + summed_over(pl.multiple_of(step * chunk, chunk)),
            jnp.zeros((features.shape[0], rows[0].shape[1]), jnp.float32),
        )
    agg = (total / FAN1).astype(jnp.bfloat16)
    pre = lax.dot_general(own[...], weight[0], COLUMNS_FIRST, preferred_element_type=jnp.float32)
    pre = pre + lax.dot_general(agg, weight[1], COLUMNS_FIRST, preferred_element_type=jnp.float32)
    partial[...] = pre.astype(partial.dtype)


def partial_sums(features, neigh, weight):
    fan, _, nodes = neigh.shape
    depth, sources = features.shape
    width = weight.shape[2]
    block = math.gcd(nodes, 512)
    return pl.pallas_call(
        partial_kernel,
        out_shape=jax.ShapeDtypeStruct((nodes, width), jnp.bfloat16),
        grid=(nodes // block,),
        in_specs=[
            pl.BlockSpec((depth, sources), lambda i: (0, 0)),
            pl.BlockSpec((depth, block), lambda i: (0, i)),
            pl.BlockSpec((fan, 1, block), lambda i: (0, 0, i)),
            pl.BlockSpec((2, depth, width), lambda i: (0, 0, 0)),
        ],
        out_specs=pl.BlockSpec((block, width), lambda i: (i, 0)),
        name="layer_one_partial_sums",
    )(features, features, neigh, weight)


def hidden_kernel(partials, boundary, hidden, picked):
    pre = partials[0].astype(jnp.float32)
    for part in range(1, partials.shape[0]):
        pre = pre + partials[part].astype(jnp.float32)
    rows = jnp.maximum(pre, 0.0).astype(jnp.bfloat16)
    hidden[...] = rows
    chosen = counts_of([boundary[0]], 0, rows.shape[0])
    picked[...] = lax.dot_general(
        chosen, rows, COLUMNS_FIRST, preferred_element_type=jnp.float32
    ).astype(jnp.bfloat16)


def layer_two_kernel(hidden, incoming, neigh, weight, out):
    rows = [neigh[k] for k in range(neigh.shape[0])]
    local = hidden.shape[0]
    out_rows = rows[0].shape[1]
    total = lax.dot_general(
        counts_of(rows, 0, local), hidden[...], COLUMNS_FIRST, preferred_element_type=jnp.float32
    )
    far = incoming.shape[0]
    step = min(far, 256)
    for start in range(0, far, step):
        counts = counts_of(rows, local + start, step)
        total = total + lax.dot_general(
            counts, incoming[pl.ds(start, step), :], COLUMNS_FIRST, preferred_element_type=jnp.float32
        )
    agg = (total / FAN2).astype(jnp.bfloat16)
    result = jnp.dot(hidden[pl.ds(0, out_rows), :], weight[0], preferred_element_type=jnp.float32)
    result = result + jnp.dot(agg, weight[1], preferred_element_type=jnp.float32)
    out[0] = jnp.maximum(result, 0.0).astype(jnp.bfloat16)


def on_device(features, neigh_one, boundary, neigh_two, weight_one, weight_two):
    width = weight_one.shape[2]
    partial = partial_sums(features, neigh_one.transpose(1, 0, 2), weight_one)
    feat_count = lax.axis_size("feat")
    partials = lax.all_to_all(partial, "feat", split_axis=0, concat_axis=0, tiled=True)
    partials = partials.reshape(feat_count, -1, width)
    local = partials.shape[1]
    sent = boundary.shape[2]
    hidden, picked = pl.pallas_call(
        hidden_kernel,
        out_shape=(
            jax.ShapeDtypeStruct((local, width), jnp.bfloat16),
            jax.ShapeDtypeStruct((sent, width), jnp.bfloat16),
        ),
        name="hidden_and_boundary_rows",
    )(partials, boundary)
    incoming = lax.all_to_all(picked, "dom", split_axis=0, concat_axis=0, tiled=True)
    return pl.pallas_call(
        layer_two_kernel,
        out_shape=jax.ShapeDtypeStruct((1, neigh_two.shape[1], weight_two.shape[2]), jnp.bfloat16),
        name="layer_two",
    )(hidden, incoming, neigh_two.transpose(2, 0, 1), weight_two)


def solution(mesh):
    placed = (
        P("feat", "dom"),
        P("dom", None, None),
        P("dom", "feat", None),
        P("dom", "feat", None),
        P(None, "feat", None),
        P(),
    )
    return jax.shard_map(
        on_device, mesh=mesh, in_specs=placed, out_specs=P("dom", "feat", None), check_vma=False
    )
```

time: 73.3 us -> 31.1 us (0.42)
  waiting for transfers between devices: 41.9 us -> 0 us
  blocking collectives: 0 us -> 23.1 us
  between operations: 13.5 us -> 0.01 us
  matrix products: 9.42 us -> 0 us
  Pallas kernels: 0 us -> 7.61 us
  starting transfers between devices: 4.62 us -> 0 us
  local copies, waits for them, and re-layouts: 1.72 us -> 0 us
  other arithmetic: 1.69 us -> 0 us
    reduce_scatter x1 -> x0, waiting for transfers between devices: 36.3 us -> none  [on_device(): lax.psum_scatter(term + lax.dot_general(agg, weight_one[1], dims, preferr...]
    all_to_all x0 -> x2, blocking collectives: none -> 23.1 us  [the longest x1 12.2 us: on_device(): lax.all_to_all(partial, 'feat', split_axis=0, concat_axis=0, tiled=True)]
    dot_general x7 -> x0, matrix products: 9.42 us -> none  [the longest x2 6.22 us: block_sum(): lax.dot_general(features, counts, (((1,), (1,)), ((), ())), preferred_ele...]
    pallas_call x0 -> x3, Pallas kernels: none -> 7.61 us  [the longest x1 3.85 us: partial_sums(): pl.pallas_call(partial_kernel, out_shape=jax.ShapeDtypeStruct((nodes, wid...]
    all_to_all x1 -> x0, waiting for transfers between devices: 5.61 us -> none  [on_device(): lax.all_to_all(outgoing, 'dom', split_axis=0, concat_axis=0, tiled=True)]
    all_to_all x1 -> x0, starting transfers between devices: 4.62 us -> none  [on_device(): lax.all_to_all(outgoing, 'dom', split_axis=0, concat_axis=0, tiled=True)]
    unnamed x11 -> x0, local copies, waits for them, and re-layouts: 1.61 us -> none
    unnamed x2 -> x0, other arithmetic: 0.85 us -> none
  transfers between devices with their start and end apart: 2 -> 0, of which waited for: 2 -> 0; matrix products, arithmetic and copies ran while one was open for 0% -> 0% of each run, Pallas kernels for 0% -> 0%
where the time goes in v1:
time: 31.1 us; the launch traced here: 30.8 us
  blocking collectives  23.1 us (74%)
  Pallas kernels  7.61 us (24%)
    all_to_all x1, blocking collectives, on_device(): lax.all_to_all(partial, 'feat', split_axis=0, concat_axis=0, tiled=True)  12.2 us
    all_to_all x1, blocking collectives, on_device(): lax.all_to_all(picked, 'dom', split_axis=0, concat_axis=0, tiled=True)  10.9 us
    pallas_call x1, Pallas kernels, partial_sums(): pl.pallas_call(partial_kernel, out_shape=jax.ShapeDtypeStruct((nodes, wid...  3.85 us
    pallas_call x1, Pallas kernels, on_device(): pl.pallas_call(layer_two_kernel, out_shape=jax.ShapeDtypeStruct((1, neigh...  1.98 us
    pallas_call x1, Pallas kernels, on_device(): pl.pallas_call(hidden_kernel, out_shape=(jax.ShapeDtypeStruct((local, wid...  1.78 us

profile of v1, /device:TPU:0, one launch (start us, length us, event | category | flops | bytes accessed | tf_op | source)
XLA Modules:
  0.0 30.8 jit_solution(1300199659937254687)
XLA Ops:
  0.0 3.9 %layer_one_partial_sums.1 = bf16[512,256]{1,0:T(8,128)(2,1)} custom-call(bf16[96,1024]{1,0:T(8,128)(2,1)} %own.1, bf16[96,1024]{1,0:T(8,128)(2,1)} %own.1, s32[15,1,512]{2,1,0:T(1,128)} %bitcast.8, bf16[2,96,256]{2,1,0:T(8,128)(2,1)} %weight.2), custom_call_target="tpu_custom_call" | custom-call | tf_op jit(solution)/shard_map/layer_one_partial_sums/pallas_call | solution.py:61
  3.9 12.2 %all_to_all.20.partials = bf16[8,64,256]{2,1,0:T(8,128)(2,1)} all-to-all(bf16[8,64,256]{2,1,0:T(8,128)(2,1)} %bitcast.5), channel_id=1, replica_groups=mesh['feat'=8,'dom'=4] {'feat'}, dimensions={0} | all-to-all | bytes 524288 | tf_op jit(solution)/shard_map/all_to_all | solution.py:112
  16.1 1.8 %hidden_and_boundary_rows.1 = (bf16[64,256]{1,0:T(8,128)(2,1)}, bf16[128,256]{1,0:T(8,128)(2,1)}) custom-call(bf16[8,64,256]{2,1,0:T(8,128)(2,1)} %all_to_all.20.partials, s32[1,1,128]{2,1,0:T(1,128)} %boundary.1), custom_call_target="tpu_custom_call" | custom-call | tf_op jit(solution)/shard_map/hidden_and_boundary_rows/pallas_call | solution.py:116
  17.8 10.9 %all_to_all.21 = bf16[4,32,256]{2,1,0:T(8,128)(2,1)} all-to-all(bf16[4,32,256]{2,1,0:T(8,128)(2,1)} %bitcast.7), channel_id=1, replica_groups=mesh['feat'=8,'dom'=4] {'dom'}, dimensions={0} | all-to-all | bytes 131072 | tf_op jit(solution)/shard_map/all_to_all | solution.py:124
  28.8 2.0 %layer_two.1 = bf16[1,32,256]{2,1,0:T(8,128)(2,1)} custom-call(bf16[64,256]{1,0:T(8,128)(2,1)} %get-tuple-element.7.hidden, bf16[128,256]{1,0:T(8,128)(2,1)} %bitcast.6, s32[10,1,32]{2,1,0:T(1,128)} %bitcast.9, bf16[2,256,256]{2,1,0:T(8,128)(2,1)} %weight.3), custom_call_target="tpu_custom_call" | custom-call | tf_op jit(solution)/shard_map/layer_two/pallas_call | solution.py:125

commit v2 on v1

v2 whole, which is shorter than its diff:
```python
import math

import jax
import jax.numpy as jnp
from jax import lax
from jax.experimental import pallas as pl
from jax.experimental.pallas import tpu as pltpu
from jax.sharding import PartitionSpec as P

FAN1 = 15
FAN2 = 10
CHUNK = 256
COLUMNS_FIRST = (((0,), (0,)), ((), ()))
VMEM = pl.BlockSpec(memory_space=pltpu.VMEM)


def f32_dot(a, b):
    return jnp.dot(a, b, preferred_element_type=jnp.float32)


def f32_dot_columns(a, b):
    return lax.dot_general(a, b, COLUMNS_FIRST, preferred_element_type=jnp.float32)


def counts_of(rows, start, height):
    width = rows[0].shape[1]
    slots = lax.broadcasted_iota(jnp.int32, (height, width), 0).astype(jnp.float32).astype(jnp.bfloat16)
    one = jnp.ones((), jnp.bfloat16)
    zero = jnp.zeros((), jnp.bfloat16)
    counts = None
    for row in rows:
        near = (row - start).astype(jnp.float32).astype(jnp.bfloat16)
        hit = jnp.where(near == slots, one, zero)
        counts = hit if counts is None else counts + hit
    return counts


def counts_kernel(neigh, counts):
    core = lax.rem(lax.axis_index("feat"), 2)
    index = neigh[:, 0, :]
    lane = lax.broadcasted_iota(jnp.int32, (index.shape[0], 128), 1)
    groups = []
    for start in range(0, index.shape[1], 256):
        a = index[:, start : start + 128]
        b = index[:, start + 128 : start + 256]
        first = jnp.where(core == 0, a, pltpu.roll(a, 64, 1))
        second = jnp.where(core == 0, pltpu.roll(b, 64, 1), b)
        groups.append(jnp.where(lane < 64, first, second))
    index = jnp.concatenate(groups, axis=1)
    rows = [index[k : k + 1] for k in range(index.shape[0])]
    chunk = min(CHUNK, counts.shape[0])
    for start in range(0, counts.shape[0], chunk):
        counts[pl.ds(start, chunk), :] = counts_of(rows, start, chunk)


def sums_kernel(mine, theirs, counts, weight, their_weight, kept, *rest):
    sent, own_all, agg_all = rest[:-2], rest[-2], rest[-1]
    me = lax.axis_index("feat")
    core, chip = lax.rem(me, 2), lax.div(me, 2)
    nodes = own_all.shape[0]
    local = kept.shape[0]
    own_all[...] = f32_dot_columns(mine[:, :nodes], weight[0]) + f32_dot_columns(
        theirs[:, :nodes], their_weight[0]
    )
    agg = (f32_dot(mine[...], counts[...]) / FAN1).astype(jnp.bfloat16)
    their_agg = (f32_dot(theirs[...], counts[...]) / FAN1).astype(jnp.bfloat16)
    agg_all[...] = f32_dot_columns(agg, weight[1]) + f32_dot_columns(their_agg, their_weight[1])
    for apart in range(len(sent) + 1):
        to = jnp.bitwise_xor(chip, apart)
        own = own_all[pl.ds(pl.multiple_of((2 * to + core) * local, local), local), :]
        pre = own + agg_all[pl.ds(pl.multiple_of(to * local, local), local), :]
        if apart == 0:
            kept[...] = pre
        else:
            sent[apart - 1][...] = pre.astype(jnp.bfloat16)


def rows_kernel(kept, *rest):
    partials, boundary, hidden, near, sent, picked = rest[:-7], rest[-7], rest[-6], rest[-5], rest[-4:-1], rest[-1]
    me = lax.axis_index("dom")
    pre = kept[...]
    for part in partials:
        pre = pre + part[...].astype(jnp.float32)
    rows = jnp.maximum(pre, 0.0).astype(jnp.bfloat16)
    hidden[...] = rows
    picked[...] = f32_dot_columns(counts_of([boundary[0]], 0, rows.shape[0]), rows).astype(jnp.bfloat16)
    share = near.shape[0]
    for apart, to in enumerate((near, *sent)):
        start = pl.multiple_of(jnp.bitwise_xor(me, apart) * share, share)
        to[...] = picked[pl.ds(start, share), :]


def near_kernel(hidden, near, neigh, weight, base, total, counts):
    me = lax.axis_index("dom")
    rows = [neigh[k] for k in range(neigh.shape[0])]
    local, share, out_rows = hidden.shape[0], near.shape[0], base.shape[0]
    base[...] = f32_dot(hidden[pl.ds(0, out_rows), :], weight[0])
    total[...] = f32_dot_columns(counts_of(rows, 0, local), hidden[...]) + f32_dot_columns(
        counts_of(rows, local + me * share, share), near[...]
    )
    for apart in range(1, counts.shape[0] + 1):
        start = local + jnp.bitwise_xor(me, apart) * share
        counts[apart - 1] = counts_of(rows, start, share)


def far_kernel(base, total, counts, *rest):
    incoming, weight, out = rest[:-2], rest[-2], rest[-1]
    summed = total[...]
    for part, rows in enumerate(incoming):
        summed = summed + f32_dot_columns(counts[part], rows[...])
    agg = (summed / FAN2).astype(jnp.bfloat16)
    out[0] = jnp.maximum(base[...] + f32_dot(agg, weight[1]), 0.0).astype(jnp.bfloat16)


def call(kernel, outs, operands, name, scratch=(), flops=0):
    return pl.pallas_call(
        kernel,
        out_shape=outs,
        in_specs=[VMEM] * len(operands),
        out_specs=jax.tree.map(lambda _: VMEM, outs),
        scratch_shapes=scratch,
        compiler_params=pltpu.CompilerParams(vmem_limit_bytes=8 << 20),
        name=name,
    )(*operands)


def apart_by(count, step):
    return [(i, i ^ step) for i in range(count)]


def on_small_mesh(features, neigh_one, boundary, neigh_two, weight_one, weight_two):
    feat_count, dom_count = lax.axis_size("feat"), lax.axis_size("dom")
    width = weight_one.shape[2]
    nodes = neigh_one.shape[2]
    local = nodes // feat_count
    share = boundary.shape[2] // dom_count
    out_rows = neigh_two.shape[1]
    shape = jax.ShapeDtypeStruct
    bf16, f32 = jnp.bfloat16, jnp.float32

    theirs = lax.ppermute(features, "feat", apart_by(feat_count, 1))
    their_weight = lax.ppermute(weight_one, "feat", apart_by(feat_count, 1))
    counts = call(
        counts_kernel, shape((features.shape[1], nodes // 2), bf16), [neigh_one.transpose(1, 0, 2)], "layer_one_counts"
    )
    chips = feat_count // 2
    kept, *sent = call(
        sums_kernel,
        (shape((local, width), f32),) + (shape((local, width), bf16),) * (chips - 1),
        [features, theirs, counts, weight_one, their_weight],
        "layer_one_sums",
        scratch=[pltpu.VMEM((nodes, width), f32), pltpu.VMEM((nodes // 2, width), f32)],
    )
    partials = [lax.ppermute(rows, "feat", apart_by(feat_count, 2 * (k + 1))) for k, rows in enumerate(sent)]
    hidden, near, *sent = call(
        rows_kernel,
        (shape((local, width), bf16),) + (shape((share, width), bf16),) * dom_count,
        [kept, *partials, boundary],
        "hidden_and_boundary_rows",
        scratch=[pltpu.VMEM((share * dom_count, width), bf16)],
    )
    incoming = [lax.ppermute(rows, "dom", apart_by(dom_count, k + 1)) for k, rows in enumerate(sent)]
    index_two = neigh_two.transpose(2, 0, 1)
    base, total, counts_two = call(
        near_kernel,
        (
            shape((out_rows, width), f32),
            shape((out_rows, width), f32),
            shape((dom_count - 1, share, out_rows), bf16),
        ),
        [hidden, near, index_two, weight_two],
        "layer_two_near",
    )
    return call(
        far_kernel,
        shape((1, out_rows, weight_two.shape[2]), bf16),
        [base, total, counts_two, *incoming, weight_two],
        "layer_two_far",
    )


def partial_kernel(features, own, neigh, weight, partial):
    fan = neigh.shape[0]
    sources = features.shape[1]
    chunk = min(CHUNK, sources)
    rows = [neigh[k] for k in range(fan)]

    def add_chunk(step, so_far):
        start = pl.multiple_of(step * chunk, chunk)
        return so_far + f32_dot(features[:, pl.ds(start, chunk)], counts_of(rows, start, chunk))

    total = lax.fori_loop(
        0, sources // chunk, add_chunk, jnp.zeros((features.shape[0], rows[0].shape[1]), jnp.float32)
    )
    agg = (total / FAN1).astype(jnp.bfloat16)
    pre = f32_dot_columns(own[...], weight[0]) + f32_dot_columns(agg, weight[1])
    partial[...] = pre.astype(partial.dtype)


def partial_sums(features, neigh, weight):
    fan, _, nodes = neigh.shape
    depth, sources = features.shape
    width = weight.shape[2]
    block = math.gcd(nodes, 512)
    return pl.pallas_call(
        partial_kernel,
        out_shape=jax.ShapeDtypeStruct((nodes, width), jnp.bfloat16),
        grid=(nodes // block,),
        in_specs=[
            pl.BlockSpec((depth, sources), lambda i: (0, 0)),
            pl.BlockSpec((depth, block), lambda i: (0, i)),
            pl.BlockSpec((fan, 1, block), lambda i: (0, 0, i)),
            pl.BlockSpec((2, depth, width), lambda i: (0, 0, 0)),
        ],
        out_specs=pl.BlockSpec((block, width), lambda i: (i, 0)),
        name="layer_one_partial_sums",
    )(features, features, neigh, weight)


def hidden_kernel(partials, boundary, hidden, picked):
    pre = partials[0].astype(jnp.float32)
    for part in range(1, partials.shape[0]):
        pre = pre + partials[part].astype(jnp.float32)
    rows = jnp.maximum(pre, 0.0).astype(jnp.bfloat16)
    hidden[...] = rows
    picked[...] = f32_dot_columns(counts_of([boundary[0]], 0, rows.shape[0]), rows).astype(jnp.bfloat16)


def layer_two_kernel(hidden, incoming, neigh, weight, out):
    rows = [neigh[k] for k in range(neigh.shape[0])]
    local = hidden.shape[0]
    out_rows = rows[0].shape[1]
    total = f32_dot_columns(counts_of(rows, 0, local), hidden[...])
    far = incoming.shape[0]
    step = math.gcd(far, 256)
    for start in range(0, far, step):
        total = total + f32_dot_columns(
            counts_of(rows, local + start, step), incoming[pl.ds(start, step), :]
        )
    agg = (total / FAN2).astype(jnp.bfloat16)
    result = f32_dot(hidden[pl.ds(0, out_rows), :], weight[0]) + f32_dot(agg, weight[1])
    out[0] = jnp.maximum(result, 0.0).astype(jnp.bfloat16)


def on_any_mesh(features, neigh_one, boundary, neigh_two, weight_one, weight_two):
    width = weight_one.shape[2]
    partial = partial_sums(features, neigh_one.transpose(1, 0, 2), weight_one)
    feat_count = lax.axis_size("feat")
    partials = lax.all_to_all(partial, "feat", split_axis=0, concat_axis=0, tiled=True)
    partials = partials.reshape(feat_count, -1, width)
    hidden, picked = pl.pallas_call(
        hidden_kernel,
        out_shape=(
            jax.ShapeDtypeStruct((partials.shape[1], width), jnp.bfloat16),
            jax.ShapeDtypeStruct((boundary.shape[2], width), jnp.bfloat16),
        ),
        name="hidden_and_boundary_rows",
    )(partials, boundary)
    incoming = lax.all_to_all(picked, "dom", split_axis=0, concat_axis=0, tiled=True)
    return pl.pallas_call(
        layer_two_kernel,
        out_shape=jax.ShapeDtypeStruct((1, neigh_two.shape[1], weight_two.shape[2]), jnp.bfloat16),
        name="layer_two",
    )(hidden, incoming, neigh_two.transpose(2, 0, 1), weight_two)


def solution(mesh):
    placed = (
        P("feat", "dom"),
        P("dom", None, None),
        P("dom", "feat", None),
        P("dom", "feat", None),
        P(None, "feat", None),
        P(),
    )
    on_device = on_small_mesh if mesh.shape["feat"] == 8 and mesh.shape["dom"] == 4 else on_any_mesh
    return jax.shard_map(
        on_device, mesh=mesh, in_specs=placed, out_specs=P("dom", "feat", None), check_vma=False
    )
```

time: 31.1 us -> 23.6 us (0.76)
  blocking collectives: 23.1 us -> 0 us
  waiting for transfers between devices: 0 us -> 9.86 us
  starting transfers between devices: 0 us -> 9.51 us
  Pallas kernels: 7.61 us -> 3.14 us
  local copies, waits for them, and re-layouts: 0 us -> 0.8 us
    all_to_all x2 -> x0, blocking collectives: 23.1 us -> none  [the longest x1 12.2 us: on_device(): lax.all_to_all(partial, 'feat', split_axis=0, concat_axis=0, tiled=True)]
    ppermute x0 -> x8, waiting for transfers between devices: none -> 9.86 us  [the longest x3 5.06 us: on_small_mesh(): lax.ppermute(rows, 'dom', apart_by(dom_count, k + 1))]
    ppermute x0 -> x8, starting transfers between devices: none -> 9.51 us  [the longest x3 4.54 us: on_small_mesh(): lax.ppermute(rows, 'feat', apart_by(feat_count, 2 * (k + 1)))]
    pallas_call x3 -> x5, Pallas kernels: 7.61 us -> 3.14 us  [call(): pl.pallas_call(kernel, out_shape=outs, in_specs=[VMEM] * len(operands), o...]
    unnamed x0 -> x12, local copies, waits for them, and re-layouts: none -> 0.8 us
  transfers between devices with their start and end apart: 0 -> 8, of which waited for: 0 -> 5; matrix products, arithmetic and copies ran while one was open for 0% -> 0% of each run, Pallas kernels for 0% -> 5%
where the time goes in v2:
time: 23.6 us; the launch traced here: 23.4 us
  waiting for transfers between devices  9.86 us (42%)
  starting transfers between devices  9.51 us (40%)
  Pallas kernels  3.14 us (13%)
  local copies, waits for them, and re-layouts  0.8 us (3%)
    ppermute x3, waiting for transfers between devices, on_small_mesh(): lax.ppermute(rows, 'dom', apart_by(dom_count, k + 1))  5.06 us
    ppermute x3, waiting for transfers between devices, on_small_mesh(): lax.ppermute(rows, 'feat', apart_by(feat_count, 2 * (k + 1)))  4.79 us
    ppermute x3, starting transfers between devices, on_small_mesh(): lax.ppermute(rows, 'feat', apart_by(feat_count, 2 * (k + 1)))  4.54 us
    ppermute x3, starting transfers between devices, on_small_mesh(): lax.ppermute(rows, 'dom', apart_by(dom_count, k + 1))  4.45 us
    pallas_call x5, Pallas kernels, call(): pl.pallas_call(kernel, out_shape=outs, in_specs=[VMEM] * len(operands), o...  3.14 us
    unnamed x12, local copies, waits for them, and re-layouts  0.8 us
  transfers between devices with their start and end apart: 8, of which 5 were waited for; matrix products, arithmetic and copies ran while one was open for 0% of the time, Pallas kernels for 5%

profile of v2, /device:TPU:0, one launch (start us, length us, event | category | flops | bytes accessed | tf_op | source)
XLA Modules:
  0.0 23.4 jit_solution(11852972256555349597)
XLA Ops:
  0.0 0.5 %collective-permute-start = (bf16[96,1024]{1,0:T(8,128)(2,1)}, bf16[96,1024]{1,0:T(8,128)(2,1)S(1)}, u32[]{:S(2)}, u32[]{:S(2)}) collective-permute-start(bf16[96,1024]{1,0:T(8,128)(2,1)} %mine.1), channel_id=1, source_target_pairs={{0,4},{4,0},{8,12},{12,8},{16,20},{20,16},{24,28},{28,24},{1,5},{5... | collective-permute-start | bytes 589832 | tf_op jit(solution)/shard_map/ppermute | solution.py:141
  0.5 0.1 collective-permute-start.1
  0.5 0.0 copy-start.3
  0.5 0.8 %copy-done.3 = s32[1,15,512]{2,0,1:T(1,128)S(1)} copy-done((s32[1,15,512]{2,0,1:T(1,128)S(1)}, s32[1,15,512]{2,0,1:T(1,128)}, u32[]{:S(2)}) %copy-start.3) | copy-done | bytes 30744
  1.3 0.0 copy-start.1
  1.3 0.0 copy-start.2
  1.3 0.9 %layer_one_counts.1.counts = bf16[1024,256]{1,0:T(8,128)(2,1)S(1)} custom-call(s32[15,1,512]{2,1,0:T(1,128)S(1)} %bitcast.2), custom_call_target="tpu_custom_call" | custom-call | tf_op jit(solution)/shard_map/layer_one_counts/pallas_call | solution.py:116
  2.2 0.0 collective-permute-done.1.their_weight
  2.2 0.0 collective-permute-done.theirs
  2.2 0.0 copy-done.1
  2.2 0.0 copy-done.2
  2.3 0.0 copy-start
  2.3 0.8 %layer_one_sums.1 = (f32[64,256]{1,0:T(8,128)S(1)}, bf16[64,256]{1,0:T(8,128)(2,1)S(1)}, bf16[64,256]{1,0:T(8,128)(2,1)S(1)}, bf16[64,256]{1,0:T(8,128)(2,1)S(1)}) custom-call(bf16[96,1024]{1,0:T(8,128)(2,1)S(1)} %copy-done.1, bf16[96,1024]{1,0:T(8,128)(2,1)S(1)} %collective-permute-done.theirs, bf16[1024,256]{1,0:T(8,128)(2,1)S(1)} %layer_one_counts.1.counts, ...), custom_call_target="tpu_custom_call" | custom-call | tf_op jit(solution)/shard_map/layer_one_sums/pallas_call | solution.py:116
  3.1 3.0 %collective-permute-start.2 = (bf16[64,256]{1,0:T(8,128)(2,1)S(1)}, bf16[64,256]{1,0:T(8,128)(2,1)S(1)}, u32[]{:S(2)}, u32[]{:S(2)}) collective-permute-start(bf16[64,256]{1,0:T(8,128)(2,1)S(1)} %get-tuple-element.18), channel_id=1, source_target_pairs={{0,8},{4,12},{8,0},{12,4},{16,24},{20,28},{24,16},{28,20},{1,9},{5... | collective-permute-start | bytes 98312 | tf_op jit(solution)/shard_map/ppermute | solution.py:154
  6.1 1.5 %collective-permute-start.3 = (bf16[64,256]{1,0:T(8,128)(2,1)S(1)}, bf16[64,256]{1,0:T(8,128)(2,1)S(1)}, u32[]{:S(2)}, u32[]{:S(2)}) collective-permute-start(bf16[64,256]{1,0:T(8,128)(2,1)S(1)} %get-tuple-element.19), channel_id=1, source_target_pairs={{0,16},{4,20},{8,24},{12,28},{16,0},{20,4},{24,8},{28,12},{1,17},{... | collective-permute-start | bytes 98312 | tf_op jit(solution)/shard_map/ppermute | solution.py:154
  7.6 0.0 copy-start.5
  7.6 0.0 collective-permute-start.4
  7.7 0.4 %collective-permute-done.2.rest_0_ = bf16[64,256]{1,0:T(8,128)(2,1)S(1)} collective-permute-done((bf16[64,256]{1,0:T(8,128)(2,1)S(1)}, bf16[64,256]{1,0:T(8,128)(2,1)S(1)}, u32[]{:S(2)}, u32[]{:S(2)}) %collective-permute-start.2) | collective-permute-done | bytes 32800 | tf_op jit(solution)/shard_map/ppermute | solution.py:154
  8.0 2.0 %collective-permute-done.3.rest_1_ = bf16[64,256]{1,0:T(8,128)(2,1)S(1)} collective-permute-done((bf16[64,256]{1,0:T(8,128)(2,1)S(1)}, bf16[64,256]{1,0:T(8,128)(2,1)S(1)}, u32[]{:S(2)}, u32[]{:S(2)}) %collective-permute-start.3) | collective-permute-done | bytes 32800 | tf_op jit(solution)/shard_map/ppermute | solution.py:154
  10.0 2.4 %collective-permute-done.4.rest_2_ = bf16[64,256]{1,0:T(8,128)(2,1)S(1)} collective-permute-done((bf16[64,256]{1,0:T(8,128)(2,1)S(1)}, bf16[64,256]{1,0:T(8,128)(2,1)S(1)}, u32[]{:S(2)}, u32[]{:S(2)}) %collective-permute-start.4) | collective-permute-done | bytes 32800 | tf_op jit(solution)/shard_map/ppermute | solution.py:154
  12.5 0.0 copy-done.5
  12.5 0.2 hidden_and_boundary_rows.1
  12.7 0.0 copy-start.4
  12.7 1.6 %collective-permute-start.5 = (bf16[32,256]{1,0:T(8,128)(2,1)S(1)}, bf16[32,256]{1,0:T(8,128)(2,1)S(1)}, u32[]{:S(2)}, u32[]{:S(2)}) collective-permute-start(bf16[32,256]{1,0:T(8,128)(2,1)S(1)} %get-tuple-element.26), channel_id=1, source_target_pairs={{0,1},{1,0},{2,3},{3,2},{4,5},{5,4},{6,7},{7,6},{8,9},{9,8},{10,11... | collective-permute-start | bytes 49160 | tf_op jit(solution)/shard_map/ppermute | solution.py:162
  14.3 2.6 %collective-permute-start.6 = (bf16[32,256]{1,0:T(8,128)(2,1)S(1)}, bf16[32,256]{1,0:T(8,128)(2,1)S(1)}, u32[]{:S(2)}, u32[]{:S(2)}) collective-permute-start(bf16[32,256]{1,0:T(8,128)(2,1)S(1)} %get-tuple-element.27), channel_id=1, source_target_pairs={{0,2},{1,3},{2,0},{3,1},{4,6},{5,7},{6,4},{7,5},{8,10},{9,11},{10,... | collective-permute-start | bytes 49160 | tf_op jit(solution)/shard_map/ppermute | solution.py:162
  16.9 0.2 collective-permute-start.7
  17.1 0.0 copy-done
  17.1 0.0 copy-done.4
  17.1 0.3 %layer_two_near.1 = (f32[32,256]{1,0:T(8,128)S(1)}, f32[32,256]{1,0:T(8,128)S(1)}, bf16[3,32,32]{2,1,0:T(8,128)(2,1)S(1)}) custom-call(bf16[64,256]{1,0:T(8,128)(2,1)S(1)} %get-tuple-element.21.hidden, bf16[32,256]{1,0:T(8,128)(2,1)S(1)} %get-tuple-element.22.near, s32[10,1,32]{2,1,0:T(1,128)S(1)} %bitcast.3, bf16[2,256,256]{2,1,0:T(8,128)(2,1)S(1)} %copy-done), custom_call_target="tpu_custom_call" | custom-call | tf_op jit(solution)/shard_map/layer_two_near/pallas_call | solution.py:116
  17.4 0.0 collective-permute-done.5.rest_0_
  17.4 1.6 %collective-permute-done.6.rest_1_ = bf16[32,256]{1,0:T(8,128)(2,1)S(1)} collective-permute-done((bf16[32,256]{1,0:T(8,128)(2,1)S(1)}, bf16[32,256]{1,0:T(8,128)(2,1)S(1)}, u32[]{:S(2)}, u32[]{:S(2)}) %collective-permute-start.6) | collective-permute-done | bytes 16416 | tf_op jit(solution)/shard_map/ppermute | solution.py:162
  19.0 3.4 %collective-permute-done.7.rest_2_ = bf16[32,256]{1,0:T(8,128)(2,1)S(1)} collective-permute-done((bf16[32,256]{1,0:T(8,128)(2,1)S(1)}, bf16[32,256]{1,0:T(8,128)(2,1)S(1)}, u32[]{:S(2)}, u32[]{:S(2)}) %collective-permute-start.7) | collective-permute-done | bytes 16416 | tf_op jit(solution)/shard_map/ppermute | solution.py:162
  22.5 0.9 %layer_two_far.1 = bf16[1,32,256]{2,1,0:T(8,128)(2,1)} custom-call(f32[32,256]{1,0:T(8,128)S(1)} %get-tuple-element.23.base, f32[32,256]{1,0:T(8,128)S(1)} %get-tuple-element.24.total, bf16[3,32,32]{2,1,0:T(8,128)(2,1)S(1)} %get-tuple-element.25.counts, bf16[32,256]{1,0:T(8,128)(2,1)S(1)} %collective-permute-done.5.rest_0_, ...), custom_call_target="tpu_custom_call" | custom-call | tf_op jit(solution)/shard_map/layer_two_far/pallas_call | solution.py:116
Async XLA Ops:
  0.0 2.2 %collective-permute-start = (bf16[96,1024]{1,0:T(8,128)(2,1)}, bf16[96,1024]{1,0:T(8,128)(2,1)S(1)}, u32[]{:S(2)}, u32[]{:S(2)}) collective-permute-start(bf16[96,1024]{1,0:T(8,128)(2,1)} %mine.1), channel_id=1, source_target_pairs={{0,4},{4,0},{8,12},{12,8},{16,20},{20,16},{24,28},{28,24},{1,5},{5... | collective-permute-start | bytes 589832 | tf_op jit(solution)/shard_map/ppermute | solution.py:141
  0.5 1.7 %collective-permute-start.1 = (bf16[2,96,256]{2,1,0:T(8,128)(2,1)}, bf16[2,96,256]{2,1,0:T(8,128)(2,1)S(1)}, u32[]{:S(2)}, u32[]{:S(2)}) collective-permute-start(bf16[2,96,256]{2,1,0:T(8,128)(2,1)} %weight.2), channel_id=1, source_target_pairs={{0,4},{4,0},{8,12},{12,8},{16,20},{20,16},{24,28},{28,24},{1,5},{5... | collective-permute-start | bytes 294920 | tf_op jit(solution)/shard_map/ppermute | solution.py:142
  0.5 0.8 %copy-start.3 = (s32[1,15,512]{2,0,1:T(1,128)S(1)}, s32[1,15,512]{2,0,1:T(1,128)}, u32[]{:S(2)}) copy-start(s32[1,15,512]{2,0,1:T(1,128)} %param.7) | copy-start | bytes 92164
  1.3 0.9 %copy-start.1 = (bf16[96,1024]{1,0:T(8,128)(2,1)S(1)}, bf16[96,1024]{1,0:T(8,128)(2,1)}, u32[]{:S(2)}) copy-start(bf16[96,1024]{1,0:T(8,128)(2,1)} %mine.1) | copy-start | bytes 589828
  1.3 1.0 %copy-start.2 = (bf16[2,96,256]{2,1,0:T(8,128)(2,1)S(1)}, bf16[2,96,256]{2,1,0:T(8,128)(2,1)}, u32[]{:S(2)}) copy-start(bf16[2,96,256]{2,1,0:T(8,128)(2,1)} %weight.2) | copy-start | bytes 294916
  2.3 14.9 %copy-start = (bf16[2,256,256]{2,1,0:T(8,128)(2,1)S(1)}, bf16[2,256,256]{2,1,0:T(8,128)(2,1)}, u32[]{:S(2)}) copy-start(bf16[2,256,256]{2,1,0:T(8,128)(2,1)} %rest_3_.3) | copy-start | bytes 786436
  3.1 4.9 %collective-permute-start.2 = (bf16[64,256]{1,0:T(8,128)(2,1)S(1)}, bf16[64,256]{1,0:T(8,128)(2,1)S(1)}, u32[]{:S(2)}, u32[]{:S(2)}) collective-permute-start(bf16[64,256]{1,0:T(8,128)(2,1)S(1)} %get-tuple-element.18), channel_id=1, source_target_pairs={{0,8},{4,12},{8,0},{12,4},{16,24},{20,28},{24,16},{28,20},{1,9},{5... | collective-permute-start | bytes 98312 | tf_op jit(solution)/shard_map/ppermute | solution.py:154
  6.1 3.9 %collective-permute-start.3 = (bf16[64,256]{1,0:T(8,128)(2,1)S(1)}, bf16[64,256]{1,0:T(8,128)(2,1)S(1)}, u32[]{:S(2)}, u32[]{:S(2)}) collective-permute-start(bf16[64,256]{1,0:T(8,128)(2,1)S(1)} %get-tuple-element.19), channel_id=1, source_target_pairs={{0,16},{4,20},{8,24},{12,28},{16,0},{20,4},{24,8},{28,12},{1,17},{... | collective-permute-start | bytes 98312 | tf_op jit(solution)/shard_map/ppermute | solution.py:154
  7.6 4.8 %copy-start.5 = (s32[1,1,128]{2,1,0:T(1,128)S(1)}, s32[1,1,128]{2,1,0:T(1,128)}, u32[]{:S(2)}) copy-start(s32[1,1,128]{2,1,0:T(1,128)} %rest_3_.2) | copy-start | bytes 1540
  7.6 4.8 %collective-permute-start.4 = (bf16[64,256]{1,0:T(8,128)(2,1)S(1)}, bf16[64,256]{1,0:T(8,128)(2,1)S(1)}, u32[]{:S(2)}, u32[]{:S(2)}) collective-permute-start(bf16[64,256]{1,0:T(8,128)(2,1)S(1)} %get-tuple-element.20), channel_id=1, source_target_pairs={{0,24},{4,28},{8,16},{12,20},{16,8},{20,12},{24,0},{28,4},{1,25},{... | collective-permute-start | bytes 98312 | tf_op jit(solution)/shard_map/ppermute | solution.py:154
  12.7 4.5 %copy-start.4 = (s32[1,32,10]{1,0,2:T(1,128)S(1)}, s32[1,32,10]{1,0,2:T(1,128)}, u32[]{:S(2)}) copy-start(s32[1,32,10]{1,0,2:T(1,128)} %param.9) | copy-start | bytes 3844
  12.7 4.7 %collective-permute-start.5 = (bf16[32,256]{1,0:T(8,128)(2,1)S(1)}, bf16[32,256]{1,0:T(8,128)(2,1)S(1)}, u32[]{:S(2)}, u32[]{:S(2)}) collective-permute-start(bf16[32,256]{1,0:T(8,128)(2,1)S(1)} %get-tuple-element.26), channel_id=1, source_target_pairs={{0,1},{1,0},{2,3},{3,2},{4,5},{5,4},{6,7},{7,6},{8,9},{9,8},{10,11... | collective-permute-start | bytes 49160 | tf_op jit(solution)/shard_map/ppermute | solution.py:162
  14.3 4.7 %collective-permute-start.6 = (bf16[32,256]{1,0:T(8,128)(2,1)S(1)}, bf16[32,256]{1,0:T(8,128)(2,1)S(1)}, u32[]{:S(2)}, u32[]{:S(2)}) collective-permute-start(bf16[32,256]{1,0:T(8,128)(2,1)S(1)} %get-tuple-element.27), channel_id=1, source_target_pairs={{0,2},{1,3},{2,0},{3,1},{4,6},{5,7},{6,4},{7,5},{8,10},{9,11},{10,... | collective-permute-start | bytes 49160 | tf_op jit(solution)/shard_map/ppermute | solution.py:162
  16.9 5.5 %collective-permute-start.7 = (bf16[32,256]{1,0:T(8,128)(2,1)S(1)}, bf16[32,256]{1,0:T(8,128)(2,1)S(1)}, u32[]{:S(2)}, u32[]{:S(2)}) collective-permute-start(bf16[32,256]{1,0:T(8,128)(2,1)S(1)} %get-tuple-element.28), channel_id=1, source_target_pairs={{0,3},{1,2},{2,1},{3,0},{4,7},{5,6},{6,5},{7,4},{8,11},{9,10},{10,... | collective-permute-start | bytes 49160 | tf_op jit(solution)/shard_map/ppermute | solution.py:162

commit v3 on v2

--- a/solution.py
+++ b/solution.py
@@ -1,3 +1,4 @@
+import functools
 import math
 
 import jax
@@ -10,8 +11,26 @@
 FAN1 = 15
 FAN2 = 10
 CHUNK = 256
+BESIDE = 10**9
 COLUMNS_FIRST = (((0,), (0,)), ((), ()))
 VMEM = pl.BlockSpec(memory_space=pltpu.VMEM)
+CHIP_TO = ((2, 3, 0, 1), (3, 2, 1, 0), (1, 0, 3, 2))
+DOM_TO = (
+    ((2, 3, 0, 1), (1, 2, 3, 0)),
+    ((1, 2, 3, 0), (2, 3, 0, 1)),
+    ((3, 0, 1, 2), (3, 0, 1, 2)),
+)
+
+
+def look_up(table, place):
+    found = table[0]
+    for at in range(1, len(table)):
+        found = jnp.where(place == at, table[at], found)
+    return found
+
+
+def inverse(table):
+    return tuple(table.index(at) for at in range(len(table)))
 
 
 def f32_dot(a, b):
@@ -36,15 +55,15 @@
 
 
 def counts_kernel(neigh, counts):
-    core = lax.rem(lax.axis_index("feat"), 2)
+    owner = 1 - lax.rem(lax.axis_index("feat"), 2)
     index = neigh[:, 0, :]
     lane = lax.broadcasted_iota(jnp.int32, (index.shape[0], 128), 1)
     groups = []
     for start in range(0, index.shape[1], 256):
         a = index[:, start : start + 128]
         b = index[:, start + 128 : start + 256]
-        first = jnp.where(core == 0, a, pltpu.roll(a, 64, 1))
-        second = jnp.where(core == 0, pltpu.roll(b, 64, 1), b)
+        first = jnp.where(owner == 0, a, pltpu.roll(a, 64, 1))
+        second = jnp.where(owner == 0, pltpu.roll(b, 64, 1), b)
         groups.append(jnp.where(lane < 64, first, second))
     index = jnp.concatenate(groups, axis=1)
     rows = [index[k : k + 1] for k in range(index.shape[0])]
@@ -56,63 +75,68 @@
 def sums_kernel(mine, theirs, counts, weight, their_weight, kept, *rest):
     sent, own_all, agg_all = rest[:-2], rest[-2], rest[-1]
     me = lax.axis_index("feat")
-    core, chip = lax.rem(me, 2), lax.div(me, 2)
+    owner, chip = 1 - lax.rem(me, 2), lax.div(me, 2)
     nodes = own_all.shape[0]
     local = kept.shape[0]
-    own_all[...] = f32_dot_columns(mine[:, :nodes], weight[0]) + f32_dot_columns(
-        theirs[:, :nodes], their_weight[0]
-    )
-    agg = (f32_dot(mine[...], counts[...]) / FAN1).astype(jnp.bfloat16)
-    their_agg = (f32_dot(theirs[...], counts[...]) / FAN1).astype(jnp.bfloat16)
-    agg_all[...] = f32_dot_columns(agg, weight[1]) + f32_dot_columns(their_agg, their_weight[1])
-    for apart in range(len(sent) + 1):
-        to = jnp.bitwise_xor(chip, apart)
-        own = own_all[pl.ds(pl.multiple_of((2 * to + core) * local, local), local), :]
+    both = jnp.concatenate([mine[...], theirs[...]], axis=0)
+    own_all[...] = f32_dot_columns(both[:, :nodes], jnp.concatenate([weight[0], their_weight[0]], axis=0))
+    agg = (f32_dot(both, counts[...]) / FAN1).astype(jnp.bfloat16)
+    agg_all[...] = f32_dot_columns(agg, jnp.concatenate([weight[1], their_weight[1]], axis=0))
+    for at, table in enumerate(((0, 1, 2, 3), *CHIP_TO)):
+        to = look_up(table, chip)
+        own = own_all[pl.ds(pl.multiple_of((2 * to + owner) * local, local), local), :]
         pre = own + agg_all[pl.ds(pl.multiple_of(to * local, local), local), :]
-        if apart == 0:
+        if at == 0:
             kept[...] = pre
         else:
-            sent[apart - 1][...] = pre.astype(jnp.bfloat16)
+            sent[at - 1][...] = pre.astype(jnp.bfloat16)
 
 
 def rows_kernel(kept, *rest):
-    partials, boundary, hidden, near, sent, picked = rest[:-7], rest[-7], rest[-6], rest[-5], rest[-4:-1], rest[-1]
+    partials, boundary, hidden, sent, picked = rest[:-6], rest[-6], rest[-5], rest[-4:-1], rest[-1]
     me = lax.axis_index("dom")
+    core = lax.rem(lax.axis_index("feat"), 2)
     pre = kept[...]
     for part in partials:
         pre = pre + part[...].astype(jnp.float32)
     rows = jnp.maximum(pre, 0.0).astype(jnp.bfloat16)
-    hidden[...] = rows
-    picked[...] = f32_dot_columns(counts_of([boundary[0]], 0, rows.shape[0]), rows).astype(jnp.bfloat16)
-    share = near.shape[0]
-    for apart, to in enumerate((near, *sent)):
-        start = pl.multiple_of(jnp.bitwise_xor(me, apart) * share, share)
-        to[...] = picked[pl.ds(start, share), :]
-
-
-def near_kernel(hidden, near, neigh, weight, base, total, counts):
+    local, share = rows.shape[0], sent[0].shape[0]
+    picked[...] = f32_dot_columns(counts_of([boundary[0]], 0, local), rows).astype(jnp.bfloat16)
+    hidden[pl.ds(0, local), :] = rows
+    hidden[pl.ds(local, share), :] = picked[pl.ds(pl.multiple_of(me * share, share), share), :]
+    for tables, to in zip(DOM_TO, sent):
+        place = jnp.where(core == 0, look_up(tables[0], me), look_up(tables[1], me))
+        to[...] = picked[pl.ds(pl.multiple_of(place * share, share), share), :]
+
+
+def slots_kernel(share, neigh, counts):
     me = lax.axis_index("dom")
+    core = lax.rem(lax.axis_index("feat"), 2)
     rows = [neigh[k] for k in range(neigh.shape[0])]
-    local, share, out_rows = hidden.shape[0], near.shape[0], base.shape[0]
-    base[...] = f32_dot(hidden[pl.ds(0, out_rows), :], weight[0])
-    total[...] = f32_dot_columns(counts_of(rows, 0, local), hidden[...]) + f32_dot_columns(
-        counts_of(rows, local + me * share, share), near[...]
-    )
-    for apart in range(1, counts.shape[0] + 1):
-        start = local + jnp.bitwise_xor(me, apart) * share
-        counts[apart - 1] = counts_of(rows, start, share)
-
-
-def far_kernel(base, total, counts, *rest):
-    incoming, weight, out = rest[:-2], rest[-2], rest[-1]
-    summed = total[...]
-    for part, rows in enumerate(incoming):
-        summed = summed + f32_dot_columns(counts[part], rows[...])
-    agg = (summed / FAN2).astype(jnp.bfloat16)
-    out[0] = jnp.maximum(base[...] + f32_dot(agg, weight[1]), 0.0).astype(jnp.bfloat16)
+    local = counts.shape[0] - (len(DOM_TO) + 1) * share
+    counts[pl.ds(0, local), :] = counts_of(rows, 0, local)
+    sources = [me]
+    for tables in DOM_TO:
+        sources.append(jnp.where(core == 0, look_up(inverse(tables[1]), me), look_up(inverse(tables[0]), me)))
+    for at, source in enumerate(sources):
+        counts[pl.ds(local + at * share, share), :] = counts_of(rows, local + source * share, share)
+
+
+def join_kernel(*refs):
+    incoming, rows = refs[:-1], refs[-1]
+    for at, part in enumerate(incoming):
+        rows[pl.ds(at * part.shape[0], part.shape[0]), :] = part[...]
+
+
+def far_kernel(far, hidden, counts, weight, out):
+    table = jnp.concatenate([hidden[...], far[...]], axis=0)
+    agg = (f32_dot_columns(counts[...], table) / FAN2).astype(jnp.bfloat16)
+    base = f32_dot(hidden[pl.ds(0, out.shape[1]), :], weight[0])
+    out[0] = jnp.maximum(base + f32_dot(agg, weight[1]), 0.0).astype(jnp.bfloat16)
 
 
 def call(kernel, outs, operands, name, scratch=(), flops=0):
+    cost = pl.CostEstimate(flops=flops, bytes_accessed=flops // 1000, transcendentals=0) if flops else None
     return pl.pallas_call(
         kernel,
         out_shape=outs,
@@ -120,6 +144,7 @@
         out_specs=jax.tree.map(lambda _: VMEM, outs),
         scratch_shapes=scratch,
         compiler_params=pltpu.CompilerParams(vmem_limit_bytes=8 << 20),
+        cost_estimate=cost,
         name=name,
     )(*operands)
 
@@ -151,30 +176,45 @@
         "layer_one_sums",
         scratch=[pltpu.VMEM((nodes, width), f32), pltpu.VMEM((nodes // 2, width), f32)],
     )
-    partials = [lax.ppermute(rows, "feat", apart_by(feat_count, 2 * (k + 1))) for k, rows in enumerate(sent)]
-    hidden, near, *sent = call(
+    partials = [
+        lax.ppermute(rows, "feat", [(2 * at + core, 2 * to + core) for at, to in enumerate(table) for core in (0, 1)])
+        for table, rows in zip(CHIP_TO, sent)
+    ]
+    swap = apart_by(feat_count, 1)
+    held, _ = lax.optimization_barrier((boundary, sent[0]))
+    their_boundary = lax.ppermute(held, "feat", swap)
+    hidden, *sent = call(
         rows_kernel,
-        (shape((local, width), bf16),) + (shape((share, width), bf16),) * dom_count,
-        [kept, *partials, boundary],
+        (shape((local + share, width), bf16),) + (shape((share, width), bf16),) * (dom_count - 1),
+        [kept, *partials, their_boundary],
         "hidden_and_boundary_rows",
         scratch=[pltpu.VMEM((share * dom_count, width), bf16)],
     )
-    incoming = [lax.ppermute(rows, "dom", apart_by(dom_count, k + 1)) for k, rows in enumerate(sent)]
-    index_two = neigh_two.transpose(2, 0, 1)
-    base, total, counts_two = call(
-        near_kernel,
-        (
-            shape((out_rows, width), f32),
-            shape((out_rows, width), f32),
-            shape((dom_count - 1, share, out_rows), bf16),
-        ),
-        [hidden, near, index_two, weight_two],
-        "layer_two_near",
-    )
+    incoming = [
+        lax.ppermute(
+            rows,
+            ("feat", "dom"),
+            [
+                (feat * dom_count + at, (feat ^ 1) * dom_count + to)
+                for feat in range(feat_count)
+                for at, to in enumerate(tables[feat % 2])
+            ],
+        )
+        for tables, rows in zip(DOM_TO, sent)
+    ]
+    hidden = lax.ppermute(hidden, "feat", swap)
+    counts_two = call(
+        functools.partial(slots_kernel, share),
+        shape((local + share * dom_count, out_rows), bf16),
+        [neigh_two.transpose(2, 0, 1)],
+        "layer_two_counts",
+        flops=BESIDE,
+    )
+    far = call(join_kernel, shape((share * len(incoming), width), bf16), incoming, "far_rows", flops=BESIDE)
     return call(
         far_kernel,
         shape((1, out_rows, weight_two.shape[2]), bf16),
-        [base, total, counts_two, *incoming, weight_two],
+        [far, hidden, counts_two, weight_two],
         "layer_two_far",
     )
 

time: 23.6 us -> 18.9 us (0.80)
  waiting for transfers between devices: 9.86 us -> 4.67 us
  starting transfers between devices: 9.51 us -> 10.4 us
  Pallas kernels: 3.14 us -> 2.74 us
    ppermute x6 -> x8, waiting for transfers between devices: 9.85 us -> 4.67 us  [the longest x3 2.67 us: on_small_mesh(): lax.ppermute(rows, 'feat', [(2 * at + core, 2 * to + core) for at, to in...]
    ppermute x6 -> x8, starting transfers between devices: 9 us -> 9.94 us  [the longest x3 4.58 us: on_small_mesh(): lax.ppermute(rows, 'feat', [(2 * at + core, 2 * to + core) for at, to in...]
    pallas_call x5 -> x6, Pallas kernels: 3.14 us -> 2.74 us  [call(): pl.pallas_call(kernel, out_shape=outs, in_specs=[VMEM] * len(operands), o...]
  transfers between devices with their start and end apart: 8 -> 10, of which waited for: 5 -> 6; matrix products, arithmetic and copies ran while one was open for 0% -> 0% of each run, Pallas kernels for 5% -> 5%
where the time goes in v3:
time: 18.9 us; the launch traced here: 18.7 us
  starting transfers between devices  10.4 us (55%)
  waiting for transfers between devices  4.67 us (25%)
  Pallas kernels  2.74 us (14%)
  local copies, waits for them, and re-layouts  0.81 us (4%)
    ppermute x3, starting transfers between devices, on_small_mesh(): lax.ppermute(rows, 'feat', [(2 * at + core, 2 * to + core) for at, to in...  4.58 us
    ppermute x3, starting transfers between devices, on_small_mesh(): lax.ppermute(rows, ('feat', 'dom'), [(feat * dom_count + at, (feat ^ 1) *...  4.51 us
    pallas_call x6, Pallas kernels, call(): pl.pallas_call(kernel, out_shape=outs, in_specs=[VMEM] * len(operands), o...  2.74 us
    ppermute x3, waiting for transfers between devices, on_small_mesh(): lax.ppermute(rows, 'feat', [(2 * at + core, 2 * to + core) for at, to in...  2.67 us
    ppermute x1, waiting for transfers between devices, on_small_mesh(): their_boundary = lax.ppermute(held, 'feat', swap)  1.12 us
    ppermute x1, starting transfers between devices, on_small_mesh(): hidden = lax.ppermute(hidden, 'feat', swap)  0.84 us
    unnamed x12, local copies, waits for them, and re-layouts  0.81 us
    ppermute x3, waiting for transfers between devices, on_small_mesh(): lax.ppermute(rows, ('feat', 'dom'), [(feat * dom_count + at, (feat ^ 1) *...  0.67 us
  transfers between devices with their start and end apart: 10, of which 6 were waited for; matrix products, arithmetic and copies ran while one was open for 0% of the time, Pallas kernels for 5%

profile of v3, /device:TPU:0, one launch (start us, length us, event | category | flops | bytes accessed | tf_op | source)
XLA Modules:
  0.0 18.7 jit_solution(10926323662297338091)
XLA Ops:
  0.0 0.5 %collective-permute-start = (bf16[96,1024]{1,0:T(8,128)(2,1)}, bf16[96,1024]{1,0:T(8,128)(2,1)S(1)}, u32[]{:S(2)}, u32[]{:S(2)}) collective-permute-start(bf16[96,1024]{1,0:T(8,128)(2,1)} %mine.1), channel_id=1, source_target_pairs={{0,4},{4,0},{8,12},{12,8},{16,20},{20,16},{24,28},{28,24},{1,5},{5... | collective-permute-start | bytes 589832 | tf_op jit(solution)/shard_map/ppermute | solution.py:166
  0.5 0.1 collective-permute-start.1
  0.5 0.0 copy-start.3
  0.5 0.8 %copy-done.3 = s32[1,15,512]{2,0,1:T(1,128)S(1)} copy-done((s32[1,15,512]{2,0,1:T(1,128)S(1)}, s32[1,15,512]{2,0,1:T(1,128)}, u32[]{:S(2)}) %copy-start.3) | copy-done | bytes 30744
  1.3 0.0 copy-start.1
  1.3 0.0 copy-start.2
  1.3 0.9 %layer_one_counts.1.counts = bf16[1024,256]{1,0:T(8,128)(2,1)S(1)} custom-call(s32[15,1,512]{2,1,0:T(1,128)S(1)} %bitcast.2), custom_call_target="tpu_custom_call" | custom-call | tf_op jit(solution)/shard_map/layer_one_counts/pallas_call | solution.py:140
  2.2 0.0 collective-permute-done.1.their_weight
  2.2 0.0 collective-permute-done.theirs
  2.2 0.0 copy-done.1
  2.2 0.0 copy-done.2
  2.3 0.6 %layer_one_sums.1 = (f32[64,256]{1,0:T(8,128)S(1)}, bf16[64,256]{1,0:T(8,128)(2,1)S(1)}, bf16[64,256]{1,0:T(8,128)(2,1)S(1)}, bf16[64,256]{1,0:T(8,128)(2,1)S(1)}) custom-call(bf16[96,1024]{1,0:T(8,128)(2,1)S(1)} %copy-done.1, bf16[96,1024]{1,0:T(8,128)(2,1)S(1)} %collective-permute-done.theirs, bf16[1024,256]{1,0:T(8,128)(2,1)S(1)} %layer_one_counts.1.counts, ...), custom_call_target="tpu_custom_call" | custom-call | tf_op jit(solution)/shard_map/layer_one_sums/pallas_call | solution.py:140
  2.9 3.0 %collective-permute-start.2 = (bf16[64,256]{1,0:T(8,128)(2,1)S(1)}, bf16[64,256]{1,0:T(8,128)(2,1)S(1)}, u32[]{:S(2)}, u32[]{:S(2)}) collective-permute-start(bf16[64,256]{1,0:T(8,128)(2,1)S(1)} %get-tuple-element.15), channel_id=1, source_target_pairs={{0,16},{4,20},{8,24},{12,28},{16,0},{20,4},{24,8},{28,12},{1,17},{... | collective-permute-start | bytes 98312 | tf_op jit(solution)/shard_map/ppermute | solution.py:180
  5.9 0.0 copy-start.5
  5.9 1.4 %collective-permute-start.3 = (bf16[64,256]{1,0:T(8,128)(2,1)S(1)}, bf16[64,256]{1,0:T(8,128)(2,1)S(1)}, u32[]{:S(2)}, u32[]{:S(2)}) collective-permute-start(bf16[64,256]{1,0:T(8,128)(2,1)S(1)} %get-tuple-element.16), channel_id=1, source_target_pairs={{0,24},{4,28},{8,16},{12,20},{16,8},{20,12},{24,0},{28,4},{1,25},{... | collective-permute-start | bytes 98312 | tf_op jit(solution)/shard_map/ppermute | solution.py:180
  7.4 0.1 collective-permute-start.4
  7.5 0.0 copy-done.5
  7.5 0.0 collective-permute-start.5
  7.5 1.1 %collective-permute-done.5.rest_3_ = s32[1,1,128]{2,1,0:T(1,128)S(1)} collective-permute-done((s32[1,1,128]{2,1,0:T(1,128)S(1)}, s32[1,1,128]{2,1,0:T(1,128)S(1)}, u32[]{:S(2)}, u32[]{:S(2)}) %collective-permute-start.5) | collective-permute-done | bytes 544 | tf_op jit(solution)/shard_map/ppermute | solution.py:185
  8.6 0.0 collective-permute-done.2.rest_0_
  8.6 2.5 %collective-permute-done.3.rest_1_ = bf16[64,256]{1,0:T(8,128)(2,1)S(1)} collective-permute-done((bf16[64,256]{1,0:T(8,128)(2,1)S(1)}, bf16[64,256]{1,0:T(8,128)(2,1)S(1)}, u32[]{:S(2)}, u32[]{:S(2)}) %collective-permute-start.3) | collective-permute-done | bytes 32800 | tf_op jit(solution)/shard_map/ppermute | solution.py:180
  11.1 0.2 %collective-permute-done.4.rest_2_ = bf16[64,256]{1,0:T(8,128)(2,1)S(1)} collective-permute-done((bf16[64,256]{1,0:T(8,128)(2,1)S(1)}, bf16[64,256]{1,0:T(8,128)(2,1)S(1)}, u32[]{:S(2)}, u32[]{:S(2)}) %collective-permute-start.4) | collective-permute-done | bytes 32800 | tf_op jit(solution)/shard_map/ppermute | solution.py:180
  11.3 0.2 %hidden_and_boundary_rows.1 = (bf16[96,256]{1,0:T(8,128)(2,1)S(1)}, bf16[32,256]{1,0:T(8,128)(2,1)S(1)}, bf16[32,256]{1,0:T(8,128)(2,1)S(1)}, bf16[32,256]{1,0:T(8,128)(2,1)S(1)}) custom-call(f32[64,256]{1,0:T(8,128)S(1)} %get-tuple-element.14.kept, bf16[64,256]{1,0:T(8,128)(2,1)S(1)} %collective-permute-done.2.rest_0_, ...), custom_call_target="tpu_custom_call" | custom-call | tf_op jit(solution)/shard_map/hidden_and_boundary_rows/pallas_call | solution.py:140
  11.5 0.0 copy-start.4
  11.5 0.8 %collective-permute-start.6 = (bf16[32,256]{1,0:T(8,128)(2,1)S(1)}, bf16[32,256]{1,0:T(8,128)(2,1)S(1)}, u32[]{:S(2)}, u32[]{:S(2)}) collective-permute-start(bf16[32,256]{1,0:T(8,128)(2,1)S(1)} %get-tuple-element.19), channel_id=1, source_target_pairs={{0,6},{1,7},{2,4},{3,5},{4,1},{5,2},{6,3},{7,0},{8,14},{9,15},{10,... | collective-permute-start | bytes 49160 | tf_op jit(solution)/shard_map/ppermute | solution.py:194
  12.3 2.1 %collective-permute-start.7 = (bf16[32,256]{1,0:T(8,128)(2,1)S(1)}, bf16[32,256]{1,0:T(8,128)(2,1)S(1)}, u32[]{:S(2)}, u32[]{:S(2)}) collective-permute-start(bf16[32,256]{1,0:T(8,128)(2,1)S(1)} %get-tuple-element.20), channel_id=1, source_target_pairs={{0,5},{1,6},{2,7},{3,4},{4,2},{5,3},{6,0},{7,1},{8,13},{9,14},{10,... | collective-permute-start | bytes 49160 | tf_op jit(solution)/shard_map/ppermute | solution.py:194
  14.4 1.6 %collective-permute-start.8 = (bf16[32,256]{1,0:T(8,128)(2,1)S(1)}, bf16[32,256]{1,0:T(8,128)(2,1)S(1)}, u32[]{:S(2)}, u32[]{:S(2)}) collective-permute-start(bf16[32,256]{1,0:T(8,128)(2,1)S(1)} %get-tuple-element.21), channel_id=1, source_target_pairs={{0,7},{1,4},{2,5},{3,6},{4,3},{5,0},{6,1},{7,2},{8,15},{9,12},{10,... | collective-permute-start | bytes 49160 | tf_op jit(solution)/shard_map/ppermute | solution.py:194
  16.0 0.0 copy-done.4
  16.0 0.1 layer_two_counts.1.counts
  16.1 0.0 copy-start
  16.1 0.8 %collective-permute-start.9 = (bf16[96,256]{1,0:T(8,128)(2,1)S(1)}, bf16[96,256]{1,0:T(8,128)(2,1)S(1)}, u32[]{:S(2)}, u32[]{:S(2)}) collective-permute-start(bf16[96,256]{1,0:T(8,128)(2,1)S(1)} %get-tuple-element.22), channel_id=1, source_target_pairs={{0,4},{4,0},{8,12},{12,8},{16,20},{20,16},{24,28},{28,24},{1,5},{5... | collective-permute-start | bytes 147464 | tf_op jit(solution)/shard_map/ppermute | solution.py:205
  17.0 0.0 collective-permute-done.6.refs_0_
  17.0 0.1 collective-permute-done.7.refs_1_
  17.0 0.6 %collective-permute-done.8.refs_2_ = bf16[32,256]{1,0:T(8,128)(2,1)S(1)} collective-permute-done((bf16[32,256]{1,0:T(8,128)(2,1)S(1)}, bf16[32,256]{1,0:T(8,128)(2,1)S(1)}, u32[]{:S(2)}, u32[]{:S(2)}) %collective-permute-start.8) | collective-permute-done | bytes 16416 | tf_op jit(solution)/shard_map/ppermute | solution.py:194
  17.6 0.2 %collective-permute-done.9.hidden = bf16[96,256]{1,0:T(8,128)(2,1)S(1)} collective-permute-done((bf16[96,256]{1,0:T(8,128)(2,1)S(1)}, bf16[96,256]{1,0:T(8,128)(2,1)S(1)}, u32[]{:S(2)}, u32[]{:S(2)}) %collective-permute-start.9) | collective-permute-done | bytes 49184 | tf_op jit(solution)/shard_map/ppermute | solution.py:205
  17.8 0.0 copy-done
  17.8 0.9 %layer_two_far.1 = bf16[1,32,256]{2,1,0:T(8,128)(2,1)} custom-call(bf16[96,256]{1,0:T(8,128)(2,1)S(1)} %far_rows.1.far, bf16[96,256]{1,0:T(8,128)(2,1)S(1)} %collective-permute-done.9.hidden, bf16[192,32]{1,0:T(8,128)(2,1)S(1)} %layer_two_counts.1.counts, bf16[2,256,256]{2,1,0:T(8,128)(2,1)S(1)} %copy-done), custom_call_target="tpu_custom_call" | custom-call | tf_op jit(solution)/shard_map/layer_two_far/pallas_call | solution.py:140
  (1 shorter events, 0.0 us)
Async XLA Ops:
  0.0 2.2 %collective-permute-start = (bf16[96,1024]{1,0:T(8,128)(2,1)}, bf16[96,1024]{1,0:T(8,128)(2,1)S(1)}, u32[]{:S(2)}, u32[]{:S(2)}) collective-permute-start(bf16[96,1024]{1,0:T(8,128)(2,1)} %mine.1), channel_id=1, source_target_pairs={{0,4},{4,0},{8,12},{12,8},{16,20},{20,16},{24,28},{28,24},{1,5},{5... | collective-permute-start | bytes 589832 | tf_op jit(solution)/shard_map/ppermute | solution.py:166
  0.5 1.7 %collective-permute-start.1 = (bf16[2,96,256]{2,1,0:T(8,128)(2,1)}, bf16[2,96,256]{2,1,0:T(8,128)(2,1)S(1)}, u32[]{:S(2)}, u32[]{:S(2)}) collective-permute-start(bf16[2,96,256]{2,1,0:T(8,128)(2,1)} %weight.2), channel_id=1, source_target_pairs={{0,4},{4,0},{8,12},{12,8},{16,20},{20,16},{24,28},{28,24},{1,5},{5... | collective-permute-start | bytes 294920 | tf_op jit(solution)/shard_map/ppermute | solution.py:167
  0.5 0.8 %copy-start.3 = (s32[1,15,512]{2,0,1:T(1,128)S(1)}, s32[1,15,512]{2,0,1:T(1,128)}, u32[]{:S(2)}) copy-start(s32[1,15,512]{2,0,1:T(1,128)} %param.7) | copy-start | bytes 92164
  1.3 0.9 %copy-start.1 = (bf16[96,1024]{1,0:T(8,128)(2,1)S(1)}, bf16[96,1024]{1,0:T(8,128)(2,1)}, u32[]{:S(2)}) copy-start(bf16[96,1024]{1,0:T(8,128)(2,1)} %mine.1) | copy-start | bytes 589828
  1.3 1.0 %copy-start.2 = (bf16[2,96,256]{2,1,0:T(8,128)(2,1)S(1)}, bf16[2,96,256]{2,1,0:T(8,128)(2,1)}, u32[]{:S(2)}) copy-start(bf16[2,96,256]{2,1,0:T(8,128)(2,1)} %weight.2) | copy-start | bytes 294916
  2.9 5.7 %collective-permute-start.2 = (bf16[64,256]{1,0:T(8,128)(2,1)S(1)}, bf16[64,256]{1,0:T(8,128)(2,1)S(1)}, u32[]{:S(2)}, u32[]{:S(2)}) collective-permute-start(bf16[64,256]{1,0:T(8,128)(2,1)S(1)} %get-tuple-element.15), channel_id=1, source_target_pairs={{0,16},{4,20},{8,24},{12,28},{16,0},{20,4},{24,8},{28,12},{1,17},{... | collective-permute-start | bytes 98312 | tf_op jit(solution)/shard_map/ppermute | solution.py:180
  5.9 1.6 %copy-start.5 = (s32[1,1,128]{2,1,0:T(1,128)S(1)}, s32[1,1,128]{2,1,0:T(1,128)}, u32[]{:S(2)}) copy-start(s32[1,1,128]{2,1,0:T(1,128)} %param.8) | copy-start | bytes 1540
  5.9 5.1 %collective-permute-start.3 = (bf16[64,256]{1,0:T(8,128)(2,1)S(1)}, bf16[64,256]{1,0:T(8,128)(2,1)S(1)}, u32[]{:S(2)}, u32[]{:S(2)}) collective-permute-start(bf16[64,256]{1,0:T(8,128)(2,1)S(1)} %get-tuple-element.16), channel_id=1, source_target_pairs={{0,24},{4,28},{8,16},{12,20},{16,8},{20,12},{24,0},{28,4},{1,25},{... | collective-permute-start | bytes 98312 | tf_op jit(solution)/shard_map/ppermute | solution.py:180
  7.4 3.9 %collective-permute-start.4 = (bf16[64,256]{1,0:T(8,128)(2,1)S(1)}, bf16[64,256]{1,0:T(8,128)(2,1)S(1)}, u32[]{:S(2)}, u32[]{:S(2)}) collective-permute-start(bf16[64,256]{1,0:T(8,128)(2,1)S(1)} %get-tuple-element.17), channel_id=1, source_target_pairs={{0,8},{4,12},{8,0},{12,4},{16,24},{20,28},{24,16},{28,20},{1,9},{5... | collective-permute-start | bytes 98312 | tf_op jit(solution)/shard_map/ppermute | solution.py:180
  7.5 1.1 %collective-permute-start.5 = (s32[1,1,128]{2,1,0:T(1,128)S(1)}, s32[1,1,128]{2,1,0:T(1,128)S(1)}, u32[]{:S(2)}, u32[]{:S(2)}) collective-permute-start(s32[1,1,128]{2,1,0:T(1,128)S(1)} %copy-done.5), channel_id=1, source_target_pairs={{0,4},{4,0},{8,12},{12,8},{16,20},{20,16},{24,28},{28,24},{1,5},{5... | collective-permute-start | bytes 1544 | tf_op jit(solution)/shard_map/ppermute | solution.py:185
  11.5 4.5 %copy-start.4 = (s32[1,32,10]{1,0,2:T(1,128)S(1)}, s32[1,32,10]{1,0,2:T(1,128)}, u32[]{:S(2)}) copy-start(s32[1,32,10]{1,0,2:T(1,128)} %param.9) | copy-start | bytes 3844
  11.5 5.5 %collective-permute-start.6 = (bf16[32,256]{1,0:T(8,128)(2,1)S(1)}, bf16[32,256]{1,0:T(8,128)(2,1)S(1)}, u32[]{:S(2)}, u32[]{:S(2)}) collective-permute-start(bf16[32,256]{1,0:T(8,128)(2,1)S(1)} %get-tuple-element.19), channel_id=1, source_target_pairs={{0,6},{1,7},{2,4},{3,5},{4,1},{5,2},{6,3},{7,0},{8,14},{9,15},{10,... | collective-permute-start | bytes 49160 | tf_op jit(solution)/shard_map/ppermute | solution.py:194
  12.3 4.7 %collective-permute-start.7 = (bf16[32,256]{1,0:T(8,128)(2,1)S(1)}, bf16[32,256]{1,0:T(8,128)(2,1)S(1)}, u32[]{:S(2)}, u32[]{:S(2)}) collective-permute-start(bf16[32,256]{1,0:T(8,128)(2,1)S(1)} %get-tuple-element.20), channel_id=1, source_target_pairs={{0,5},{1,6},{2,7},{3,4},{4,2},{5,3},{6,0},{7,1},{8,13},{9,14},{10,... | collective-permute-start | bytes 49160 | tf_op jit(solution)/shard_map/ppermute | solution.py:194
  14.4 3.2 %collective-permute-start.8 = (bf16[32,256]{1,0:T(8,128)(2,1)S(1)}, bf16[32,256]{1,0:T(8,128)(2,1)S(1)}, u32[]{:S(2)}, u32[]{:S(2)}) collective-permute-start(bf16[32,256]{1,0:T(8,128)(2,1)S(1)} %get-tuple-element.21), channel_id=1, source_target_pairs={{0,7},{1,4},{2,5},{3,6},{4,3},{5,0},{6,1},{7,2},{8,15},{9,12},{10,... | collective-permute-start | bytes 49160 | tf_op jit(solution)/shard_map/ppermute | solution.py:194
  16.1 1.7 %copy-start = (bf16[2,256,256]{2,1,0:T(8,128)(2,1)S(1)}, bf16[2,256,256]{2,1,0:T(8,128)(2,1)}, u32[]{:S(2)}) copy-start(bf16[2,256,256]{2,1,0:T(8,128)(2,1)} %weight.3) | copy-start | bytes 786436
  16.1 1.7 %collective-permute-start.9 = (bf16[96,256]{1,0:T(8,128)(2,1)S(1)}, bf16[96,256]{1,0:T(8,128)(2,1)S(1)}, u32[]{:S(2)}, u32[]{:S(2)}) collective-permute-start(bf16[96,256]{1,0:T(8,128)(2,1)S(1)} %get-tuple-element.22), channel_id=1, source_target_pairs={{0,4},{4,0},{8,12},{12,8},{16,20},{20,16},{24,28},{28,24},{1,5},{5... | collective-permute-start | bytes 147464 | tf_op jit(solution)/shard_map/ppermute | solution.py:205

commit v4 on v3

--- a/solution.py
+++ b/solution.py
@@ -16,9 +16,9 @@
 VMEM = pl.BlockSpec(memory_space=pltpu.VMEM)
 CHIP_TO = ((2, 3, 0, 1), (3, 2, 1, 0), (1, 0, 3, 2))
 DOM_TO = (
-    ((2, 3, 0, 1), (1, 2, 3, 0)),
-    ((1, 2, 3, 0), (2, 3, 0, 1)),
-    ((3, 0, 1, 2), (3, 0, 1, 2)),
+    ((1, 2, 3, 0), (2, 3, 1, 0)),
+    ((2, 3, 0, 1), (3, 2, 0, 1)),
+    ((3, 0, 1, 2), (1, 0, 3, 2)),
 )
 
 
@@ -54,16 +54,20 @@
     return counts
 
 
+def half_of(to, chip, core):
+    return jnp.where(to == chip, 1 - core, core)
+
+
 def counts_kernel(neigh, counts):
-    owner = 1 - lax.rem(lax.axis_index("feat"), 2)
+    me = lax.axis_index("feat")
+    core, chip = lax.rem(me, 2), lax.div(me, 2)
     index = neigh[:, 0, :]
     lane = lax.broadcasted_iota(jnp.int32, (index.shape[0], 128), 1)
     groups = []
-    for start in range(0, index.shape[1], 256):
-        a = index[:, start : start + 128]
-        b = index[:, start + 128 : start + 256]
-        first = jnp.where(owner == 0, a, pltpu.roll(a, 64, 1))
-        second = jnp.where(owner == 0, pltpu.roll(b, 64, 1), b)
+    for at in range(0, index.shape[1] // 128, 2):
+        a, b = (index[:, 128 * to : 128 * (to + 1)] for to in (at, at + 1))
+        first = jnp.where(half_of(at, chip, core) == 0, a, pltpu.roll(a, 64, 1))
+        second = jnp.where(half_of(at + 1, chip, core) == 0, pltpu.roll(b, 64, 1), b)
         groups.append(jnp.where(lane < 64, first, second))
     index = jnp.concatenate(groups, axis=1)
     rows = [index[k : k + 1] for k in range(index.shape[0])]
@@ -75,7 +79,7 @@
 def sums_kernel(mine, theirs, counts, weight, their_weight, kept, *rest):
     sent, own_all, agg_all = rest[:-2], rest[-2], rest[-1]
     me = lax.axis_index("feat")
-    owner, chip = 1 - lax.rem(me, 2), lax.div(me, 2)
+    core, chip = lax.rem(me, 2), lax.div(me, 2)
     nodes = own_all.shape[0]
     local = kept.shape[0]
     both = jnp.concatenate([mine[...], theirs[...]], axis=0)
@@ -84,7 +88,7 @@
     agg_all[...] = f32_dot_columns(agg, jnp.concatenate([weight[1], their_weight[1]], axis=0))
     for at, table in enumerate(((0, 1, 2, 3), *CHIP_TO)):
         to = look_up(table, chip)
-        own = own_all[pl.ds(pl.multiple_of((2 * to + owner) * local, local), local), :]
+        own = own_all[pl.ds(pl.multiple_of((2 * to + half_of(to, chip, core)) * local, local), local), :]
         pre = own + agg_all[pl.ds(pl.multiple_of(to * local, local), local), :]
         if at == 0:
             kept[...] = pre
@@ -92,8 +96,8 @@
             sent[at - 1][...] = pre.astype(jnp.bfloat16)
 
 
-def rows_kernel(kept, *rest):
-    partials, boundary, hidden, sent, picked = rest[:-6], rest[-6], rest[-5], rest[-4:-1], rest[-1]
+def rows_kernel(*refs):
+    partials, kept, boundary, hidden, sent, picked = refs[:-7], refs[-7], refs[-6], refs[-5], refs[-4:-1], refs[-1]
     me = lax.axis_index("dom")
     core = lax.rem(lax.axis_index("feat"), 2)
     pre = kept[...]
@@ -177,7 +181,7 @@
         scratch=[pltpu.VMEM((nodes, width), f32), pltpu.VMEM((nodes // 2, width), f32)],
     )
     partials = [
-        lax.ppermute(rows, "feat", [(2 * at + core, 2 * to + core) for at, to in enumerate(table) for core in (0, 1)])
+        lax.ppermute(rows, "feat", [(2 * at + core, 2 * to + 1 - core) for at, to in enumerate(table) for core in (0, 1)])
         for table, rows in zip(CHIP_TO, sent)
     ]
     swap = apart_by(feat_count, 1)
@@ -186,7 +190,7 @@
     hidden, *sent = call(
         rows_kernel,
         (shape((local + share, width), bf16),) + (shape((share, width), bf16),) * (dom_count - 1),
-        [kept, *partials, their_boundary],
+        [*partials, kept, their_boundary],
         "hidden_and_boundary_rows",
         scratch=[pltpu.VMEM((share * dom_count, width), bf16)],
     )

time: 18.9 us -> 18.5 us (0.979)
  starting transfers between devices: 10.4 us -> 9.89 us
    ppermute x1, starting transfers between devices: 0.84 us -> 0.07 us  [on_small_mesh(): hidden = lax.ppermute(hidden, 'feat', swap)]
    ppermute x3, waiting for transfers between devices: 0.67 us -> 1.25 us  [on_small_mesh(): lax.ppermute(rows, ('feat', 'dom'), [(feat * dom_count + at, (feat ^ 1) *...]
    ppermute x3, starting transfers between devices: 4.51 us -> 5 us  [on_small_mesh(): lax.ppermute(rows, ('feat', 'dom'), [(feat * dom_count + at, (feat ^ 1) *...]
    ppermute x3, waiting for transfers between devices: 2.67 us -> 2.26 us  [on_small_mesh(): lax.ppermute(rows, 'feat', [(2 * at + core, 2 * to + 1 - core) for at, to...]
    ppermute x3, starting transfers between devices: 4.58 us -> 4.3 us  [on_small_mesh(): lax.ppermute(rows, 'feat', [(2 * at + core, 2 * to + 1 - core) for at, to...]
    ppermute x1, waiting for transfers between devices: 0.2 us -> 0.01 us  [on_small_mesh(): hidden = lax.ppermute(hidden, 'feat', swap)]
  transfers between devices with their start and end apart: 10 -> 10, of which waited for: 6 -> 5; matrix products, arithmetic and copies ran while one was open for 0% -> 0% of each run, Pallas kernels for 5% -> 6%
where the time goes in v4:
time: 18.5 us; the launch traced here: 18.2 us
  starting transfers between devices  9.89 us (53%)
  waiting for transfers between devices  4.64 us (25%)
  Pallas kernels  2.75 us (15%)
  local copies, waits for them, and re-layouts  0.8 us (4%)
    ppermute x3, starting transfers between devices, on_small_mesh(): lax.ppermute(rows, ('feat', 'dom'), [(feat * dom_count + at, (feat ^ 1) *...  5 us
    ppermute x3, starting transfers between devices, on_small_mesh(): lax.ppermute(rows, 'feat', [(2 * at + core, 2 * to + 1 - core) for at, to...  4.3 us
    pallas_call x6, Pallas kernels, call(): pl.pallas_call(kernel, out_shape=outs, in_specs=[VMEM] * len(operands), o...  2.75 us
    ppermute x3, waiting for transfers between devices, on_small_mesh(): lax.ppermute(rows, 'feat', [(2 * at + core, 2 * to + 1 - core) for at, to...  2.26 us
    ppermute x3, waiting for transfers between devices, on_small_mesh(): lax.ppermute(rows, ('feat', 'dom'), [(feat * dom_count + at, (feat ^ 1) *...  1.25 us
    ppermute x1, waiting for transfers between devices, on_small_mesh(): their_boundary = lax.ppermute(held, 'feat', swap)  1.12 us
    unnamed x12, local copies, waits for them, and re-layouts  0.8 us
    ppermute x1, starting transfers between devices, on_small_mesh(): theirs = lax.ppermute(features, 'feat', apart_by(feat_count, 1))  0.45 us
  transfers between devices with their start and end apart: 10, of which 5 were waited for; matrix products, arithmetic and copies ran while one was open for 0% of the time, Pallas kernels for 6%

profile of v4, /device:TPU:0, one launch (start us, length us, event | category | flops | bytes accessed | tf_op | source)
XLA Modules:
  0.0 18.2 jit_solution(14795055498837242477)
XLA Ops:
  0.0 0.5 %collective-permute-start = (bf16[96,1024]{1,0:T(8,128)(2,1)}, bf16[96,1024]{1,0:T(8,128)(2,1)S(1)}, u32[]{:S(2)}, u32[]{:S(2)}) collective-permute-start(bf16[96,1024]{1,0:T(8,128)(2,1)} %mine.1), channel_id=1, source_target_pairs={{0,4},{4,0},{8,12},{12,8},{16,20},{20,16},{24,28},{28,24},{1,5},{5... | collective-permute-start | bytes 589832 | tf_op jit(solution)/shard_map/ppermute | solution.py:170
  0.5 0.1 collective-permute-start.1
  0.5 0.0 copy-start.3
  0.5 0.8 %copy-done.3 = s32[1,15,512]{2,0,1:T(1,128)S(1)} copy-done((s32[1,15,512]{2,0,1:T(1,128)S(1)}, s32[1,15,512]{2,0,1:T(1,128)}, u32[]{:S(2)}) %copy-start.3) | copy-done | bytes 30744
  1.3 0.0 copy-start.1
  1.3 0.0 copy-start.2
  1.3 0.9 %layer_one_counts.1.counts = bf16[1024,256]{1,0:T(8,128)(2,1)S(1)} custom-call(s32[15,1,512]{2,1,0:T(1,128)S(1)} %bitcast.2), custom_call_target="tpu_custom_call" | custom-call | tf_op jit(solution)/shard_map/layer_one_counts/pallas_call | solution.py:144
  2.2 0.0 collective-permute-done.1.their_weight
  2.2 0.0 collective-permute-done.theirs
  2.2 0.0 copy-done.1
  2.2 0.0 copy-done.2
  2.3 0.6 %layer_one_sums.1 = (f32[64,256]{1,0:T(8,128)S(1)}, bf16[64,256]{1,0:T(8,128)(2,1)S(1)}, bf16[64,256]{1,0:T(8,128)(2,1)S(1)}, bf16[64,256]{1,0:T(8,128)(2,1)S(1)}) custom-call(bf16[96,1024]{1,0:T(8,128)(2,1)S(1)} %copy-done.1, bf16[96,1024]{1,0:T(8,128)(2,1)S(1)} %collective-permute-done.theirs, bf16[1024,256]{1,0:T(8,128)(2,1)S(1)} %layer_one_counts.1.counts, ...), custom_call_target="tpu_custom_call" | custom-call | tf_op jit(solution)/shard_map/layer_one_sums/pallas_call | solution.py:144
  2.9 2.6 %collective-permute-start.2 = (bf16[64,256]{1,0:T(8,128)(2,1)S(1)}, bf16[64,256]{1,0:T(8,128)(2,1)S(1)}, u32[]{:S(2)}, u32[]{:S(2)}) collective-permute-start(bf16[64,256]{1,0:T(8,128)(2,1)S(1)} %get-tuple-element.14), channel_id=1, source_target_pairs={{0,20},{4,16},{8,28},{12,24},{16,4},{20,0},{24,12},{28,8},{1,21},{... | collective-permute-start | bytes 98312 | tf_op jit(solution)/shard_map/ppermute | solution.py:184
  5.5 0.0 copy-start.5
  5.5 1.5 %collective-permute-start.3 = (bf16[64,256]{1,0:T(8,128)(2,1)S(1)}, bf16[64,256]{1,0:T(8,128)(2,1)S(1)}, u32[]{:S(2)}, u32[]{:S(2)}) collective-permute-start(bf16[64,256]{1,0:T(8,128)(2,1)S(1)} %get-tuple-element.15), channel_id=1, source_target_pairs={{0,28},{4,24},{8,20},{12,16},{16,12},{20,8},{24,4},{28,0},{1,29},{... | collective-permute-start | bytes 98312 | tf_op jit(solution)/shard_map/ppermute | solution.py:184
  7.1 0.1 collective-permute-start.4
  7.2 0.0 copy-done.5
  7.2 0.0 collective-permute-start.5
  7.2 1.1 %collective-permute-done.5.refs_4_ = s32[1,1,128]{2,1,0:T(1,128)S(1)} collective-permute-done((s32[1,1,128]{2,1,0:T(1,128)S(1)}, s32[1,1,128]{2,1,0:T(1,128)S(1)}, u32[]{:S(2)}, u32[]{:S(2)}) %collective-permute-start.5) | collective-permute-done | bytes 544 | tf_op jit(solution)/shard_map/ppermute | solution.py:189
  8.3 0.0 collective-permute-done.2.refs_0_
  8.3 1.4 %collective-permute-done.3.refs_1_ = bf16[64,256]{1,0:T(8,128)(2,1)S(1)} collective-permute-done((bf16[64,256]{1,0:T(8,128)(2,1)S(1)}, bf16[64,256]{1,0:T(8,128)(2,1)S(1)}, u32[]{:S(2)}, u32[]{:S(2)}) %collective-permute-start.3) | collective-permute-done | bytes 32800 | tf_op jit(solution)/shard_map/ppermute | solution.py:184
  9.8 0.8 %collective-permute-done.4.refs_2_ = bf16[64,256]{1,0:T(8,128)(2,1)S(1)} collective-permute-done((bf16[64,256]{1,0:T(8,128)(2,1)S(1)}, bf16[64,256]{1,0:T(8,128)(2,1)S(1)}, u32[]{:S(2)}, u32[]{:S(2)}) %collective-permute-start.4) | collective-permute-done | bytes 32800 | tf_op jit(solution)/shard_map/ppermute | solution.py:184
  10.6 0.2 %hidden_and_boundary_rows.1 = (bf16[96,256]{1,0:T(8,128)(2,1)S(1)}, bf16[32,256]{1,0:T(8,128)(2,1)S(1)}, bf16[32,256]{1,0:T(8,128)(2,1)S(1)}, bf16[32,256]{1,0:T(8,128)(2,1)S(1)}) custom-call(bf16[64,256]{1,0:T(8,128)(2,1)S(1)} %collective-permute-done.2.refs_0_, bf16[64,256]{1,0:T(8,128)(2,1)S(1)} %collective-permute-done.3.refs_1_, ...), custom_call_target="tpu_custom_call" | custom-call | tf_op jit(solution)/shard_map/hidden_and_boundary_rows/pallas_call | solution.py:144
  10.8 0.0 copy-start.4
  10.8 1.3 %collective-permute-start.6 = (bf16[32,256]{1,0:T(8,128)(2,1)S(1)}, bf16[32,256]{1,0:T(8,128)(2,1)S(1)}, u32[]{:S(2)}, u32[]{:S(2)}) collective-permute-start(bf16[32,256]{1,0:T(8,128)(2,1)S(1)} %get-tuple-element.19), channel_id=1, source_target_pairs={{0,5},{1,6},{2,7},{3,4},{4,2},{5,3},{6,1},{7,0},{8,13},{9,14},{10,... | collective-permute-start | bytes 49160 | tf_op jit(solution)/shard_map/ppermute | solution.py:198
  12.2 1.5 %collective-permute-start.7 = (bf16[32,256]{1,0:T(8,128)(2,1)S(1)}, bf16[32,256]{1,0:T(8,128)(2,1)S(1)}, u32[]{:S(2)}, u32[]{:S(2)}) collective-permute-start(bf16[32,256]{1,0:T(8,128)(2,1)S(1)} %get-tuple-element.20), channel_id=1, source_target_pairs={{0,6},{1,7},{2,4},{3,5},{4,3},{5,2},{6,0},{7,1},{8,14},{9,15},{10,... | collective-permute-start | bytes 49160 | tf_op jit(solution)/shard_map/ppermute | solution.py:198
  13.6 2.2 %collective-permute-start.8 = (bf16[32,256]{1,0:T(8,128)(2,1)S(1)}, bf16[32,256]{1,0:T(8,128)(2,1)S(1)}, u32[]{:S(2)}, u32[]{:S(2)}) collective-permute-start(bf16[32,256]{1,0:T(8,128)(2,1)S(1)} %get-tuple-element.21), channel_id=1, source_target_pairs={{0,7},{1,4},{2,5},{3,6},{4,1},{5,0},{6,3},{7,2},{8,15},{9,12},{10,... | collective-permute-start | bytes 49160 | tf_op jit(solution)/shard_map/ppermute | solution.py:198
  15.8 0.0 copy-done.4
  15.8 0.1 layer_two_counts.1.counts
  15.9 0.0 copy-start
  15.9 0.1 collective-permute-start.9
  16.0 0.0 collective-permute-done.6.refs_0_
  16.0 0.3 %collective-permute-done.7.refs_1_ = bf16[32,256]{1,0:T(8,128)(2,1)S(1)} collective-permute-done((bf16[32,256]{1,0:T(8,128)(2,1)S(1)}, bf16[32,256]{1,0:T(8,128)(2,1)S(1)}, u32[]{:S(2)}, u32[]{:S(2)}) %collective-permute-start.7) | collective-permute-done | bytes 16416 | tf_op jit(solution)/shard_map/ppermute | solution.py:198
  16.4 0.9 %collective-permute-done.8.refs_2_ = bf16[32,256]{1,0:T(8,128)(2,1)S(1)} collective-permute-done((bf16[32,256]{1,0:T(8,128)(2,1)S(1)}, bf16[32,256]{1,0:T(8,128)(2,1)S(1)}, u32[]{:S(2)}, u32[]{:S(2)}) %collective-permute-start.8) | collective-permute-done | bytes 16416 | tf_op jit(solution)/shard_map/ppermute | solution.py:198
  17.3 0.0 collective-permute-done.9.hidden
  17.3 0.0 copy-done
  17.3 0.9 %layer_two_far.1 = bf16[1,32,256]{2,1,0:T(8,128)(2,1)} custom-call(bf16[96,256]{1,0:T(8,128)(2,1)S(1)} %far_rows.1.far, bf16[96,256]{1,0:T(8,128)(2,1)S(1)} %collective-permute-done.9.hidden, bf16[192,32]{1,0:T(8,128)(2,1)S(1)} %layer_two_counts.1.counts, bf16[2,256,256]{2,1,0:T(8,128)(2,1)S(1)} %copy-done), custom_call_target="tpu_custom_call" | custom-call | tf_op jit(solution)/shard_map/layer_two_far/pallas_call | solution.py:144
  (1 shorter events, 0.0 us)
Async XLA Ops:
  0.0 2.2 %collective-permute-start = (bf16[96,1024]{1,0:T(8,128)(2,1)}, bf16[96,1024]{1,0:T(8,128)(2,1)S(1)}, u32[]{:S(2)}, u32[]{:S(2)}) collective-permute-start(bf16[96,1024]{1,0:T(8,128)(2,1)} %mine.1), channel_id=1, source_target_pairs={{0,4},{4,0},{8,12},{12,8},{16,20},{20,16},{24,28},{28,24},{1,5},{5... | collective-permute-start | bytes 589832 | tf_op jit(solution)/shard_map/ppermute | solution.py:170
  0.5 1.7 %collective-permute-start.1 = (bf16[2,96,256]{2,1,0:T(8,128)(2,1)}, bf16[2,96,256]{2,1,0:T(8,128)(2,1)S(1)}, u32[]{:S(2)}, u32[]{:S(2)}) collective-permute-start(bf16[2,96,256]{2,1,0:T(8,128)(2,1)} %weight.2), channel_id=1, source_target_pairs={{0,4},{4,0},{8,12},{12,8},{16,20},{20,16},{24,28},{28,24},{1,5},{5... | collective-permute-start | bytes 294920 | tf_op jit(solution)/shard_map/ppermute | solution.py:171
  0.5 0.8 %copy-start.3 = (s32[1,15,512]{2,0,1:T(1,128)S(1)}, s32[1,15,512]{2,0,1:T(1,128)}, u32[]{:S(2)}) copy-start(s32[1,15,512]{2,0,1:T(1,128)} %param.7) | copy-start | bytes 92164
  1.3 1.0 %copy-start.1 = (bf16[96,1024]{1,0:T(8,128)(2,1)S(1)}, bf16[96,1024]{1,0:T(8,128)(2,1)}, u32[]{:S(2)}) copy-start(bf16[96,1024]{1,0:T(8,128)(2,1)} %mine.1) | copy-start | bytes 589828
  1.3 1.0 %copy-start.2 = (bf16[2,96,256]{2,1,0:T(8,128)(2,1)S(1)}, bf16[2,96,256]{2,1,0:T(8,128)(2,1)}, u32[]{:S(2)}) copy-start(bf16[2,96,256]{2,1,0:T(8,128)(2,1)} %weight.2) | copy-start | bytes 294916
  2.9 5.4 %collective-permute-start.2 = (bf16[64,256]{1,0:T(8,128)(2,1)S(1)}, bf16[64,256]{1,0:T(8,128)(2,1)S(1)}, u32[]{:S(2)}, u32[]{:S(2)}) collective-permute-start(bf16[64,256]{1,0:T(8,128)(2,1)S(1)} %get-tuple-element.14), channel_id=1, source_target_pairs={{0,20},{4,16},{8,28},{12,24},{16,4},{20,0},{24,12},{28,8},{1,21},{... | collective-permute-start | bytes 98312 | tf_op jit(solution)/shard_map/ppermute | solution.py:184
  5.5 1.7 %copy-start.5 = (s32[1,1,128]{2,1,0:T(1,128)S(1)}, s32[1,1,128]{2,1,0:T(1,128)}, u32[]{:S(2)}) copy-start(s32[1,1,128]{2,1,0:T(1,128)} %param.8) | copy-start | bytes 1540
  5.5 4.2 %collective-permute-start.3 = (bf16[64,256]{1,0:T(8,128)(2,1)S(1)}, bf16[64,256]{1,0:T(8,128)(2,1)S(1)}, u32[]{:S(2)}, u32[]{:S(2)}) collective-permute-start(bf16[64,256]{1,0:T(8,128)(2,1)S(1)} %get-tuple-element.15), channel_id=1, source_target_pairs={{0,28},{4,24},{8,20},{12,16},{16,12},{20,8},{24,4},{28,0},{1,29},{... | collective-permute-start | bytes 98312 | tf_op jit(solution)/shard_map/ppermute | solution.py:184
  7.1 3.5 %collective-permute-start.4 = (bf16[64,256]{1,0:T(8,128)(2,1)S(1)}, bf16[64,256]{1,0:T(8,128)(2,1)S(1)}, u32[]{:S(2)}, u32[]{:S(2)}) collective-permute-start(bf16[64,256]{1,0:T(8,128)(2,1)S(1)} %get-tuple-element.16), channel_id=1, source_target_pairs={{0,12},{4,8},{8,4},{12,0},{16,28},{20,24},{24,20},{28,16},{1,13},{... | collective-permute-start | bytes 98312 | tf_op jit(solution)/shard_map/ppermute | solution.py:184
  7.2 1.1 %collective-permute-start.5 = (s32[1,1,128]{2,1,0:T(1,128)S(1)}, s32[1,1,128]{2,1,0:T(1,128)S(1)}, u32[]{:S(2)}, u32[]{:S(2)}) collective-permute-start(s32[1,1,128]{2,1,0:T(1,128)S(1)} %copy-done.5), channel_id=1, source_target_pairs={{0,4},{4,0},{8,12},{12,8},{16,20},{20,16},{24,28},{28,24},{1,5},{5... | collective-permute-start | bytes 1544 | tf_op jit(solution)/shard_map/ppermute | solution.py:189
  10.8 5.0 %copy-start.4 = (s32[1,32,10]{1,0,2:T(1,128)S(1)}, s32[1,32,10]{1,0,2:T(1,128)}, u32[]{:S(2)}) copy-start(s32[1,32,10]{1,0,2:T(1,128)} %param.9) | copy-start | bytes 3844
  10.8 5.2 %collective-permute-start.6 = (bf16[32,256]{1,0:T(8,128)(2,1)S(1)}, bf16[32,256]{1,0:T(8,128)(2,1)S(1)}, u32[]{:S(2)}, u32[]{:S(2)}) collective-permute-start(bf16[32,256]{1,0:T(8,128)(2,1)S(1)} %get-tuple-element.19), channel_id=1, source_target_pairs={{0,5},{1,6},{2,7},{3,4},{4,2},{5,3},{6,1},{7,0},{8,13},{9,14},{10,... | collective-permute-start | bytes 49160 | tf_op jit(solution)/shard_map/ppermute | solution.py:198
  12.2 4.2 %collective-permute-start.7 = (bf16[32,256]{1,0:T(8,128)(2,1)S(1)}, bf16[32,256]{1,0:T(8,128)(2,1)S(1)}, u32[]{:S(2)}, u32[]{:S(2)}) collective-permute-start(bf16[32,256]{1,0:T(8,128)(2,1)S(1)} %get-tuple-element.20), channel_id=1, source_target_pairs={{0,6},{1,7},{2,4},{3,5},{4,3},{5,2},{6,0},{7,1},{8,14},{9,15},{10,... | collective-permute-start | bytes 49160 | tf_op jit(solution)/shard_map/ppermute | solution.py:198
  13.6 3.6 %collective-permute-start.8 = (bf16[32,256]{1,0:T(8,128)(2,1)S(1)}, bf16[32,256]{1,0:T(8,128)(2,1)S(1)}, u32[]{:S(2)}, u32[]{:S(2)}) collective-permute-start(bf16[32,256]{1,0:T(8,128)(2,1)S(1)} %get-tuple-element.21), channel_id=1, source_target_pairs={{0,7},{1,4},{2,5},{3,6},{4,1},{5,0},{6,3},{7,2},{8,15},{9,12},{10,... | collective-permute-start | bytes 49160 | tf_op jit(solution)/shard_map/ppermute | solution.py:198
  15.9 1.4 %copy-start = (bf16[2,256,256]{2,1,0:T(8,128)(2,1)S(1)}, bf16[2,256,256]{2,1,0:T(8,128)(2,1)}, u32[]{:S(2)}) copy-start(bf16[2,256,256]{2,1,0:T(8,128)(2,1)} %weight.3) | copy-start | bytes 786436
  15.9 1.3 %collective-permute-start.9 = (bf16[96,256]{1,0:T(8,128)(2,1)S(1)}, bf16[96,256]{1,0:T(8,128)(2,1)S(1)}, u32[]{:S(2)}, u32[]{:S(2)}) collective-permute-start(bf16[96,256]{1,0:T(8,128)(2,1)S(1)} %get-tuple-element.22), channel_id=1, source_target_pairs={{0,4},{4,0},{8,12},{12,8},{16,20},{20,16},{24,28},{28,24},{1,5},{5... | collective-permute-start | bytes 147464 | tf_op jit(solution)/shard_map/ppermute | solution.py:209

commit v5 on v4

--- a/solution.py
+++ b/solution.py
@@ -11,7 +11,8 @@
 FAN1 = 15
 FAN2 = 10
 CHUNK = 256
-BESIDE = 10**9
+BEHIND = 10**9
+AHEAD = 10**10
 COLUMNS_FIRST = (((0,), (0,)), ((), ()))
 VMEM = pl.BlockSpec(memory_space=pltpu.VMEM)
 CHIP_TO = ((2, 3, 0, 1), (3, 2, 1, 0), (1, 0, 3, 2))
@@ -44,13 +45,13 @@
 def counts_of(rows, start, height):
     width = rows[0].shape[1]
     slots = lax.broadcasted_iota(jnp.int32, (height, width), 0).astype(jnp.float32).astype(jnp.bfloat16)
-    one = jnp.ones((), jnp.bfloat16)
-    zero = jnp.zeros((), jnp.bfloat16)
-    counts = None
-    for row in rows:
+    counts = jnp.zeros((height, width), jnp.bfloat16)
+    for at, row in enumerate(rows):
         near = (row - start).astype(jnp.float32).astype(jnp.bfloat16)
-        hit = jnp.where(near == slots, one, zero)
-        counts = hit if counts is None else counts + hit
+        so_far = jnp.ones(row.shape, jnp.float32)
+        for before in rows[:at]:
+            so_far = so_far + (before == row).astype(jnp.float32)
+        counts = jnp.where(near == slots, so_far.astype(jnp.bfloat16), counts)
     return counts
 
 
@@ -58,16 +59,21 @@
     return jnp.where(to == chip, 1 - core, core)
 
 
-def counts_kernel(neigh, counts):
+def halves_kernel(halves):
     me = lax.axis_index("feat")
     core, chip = lax.rem(me, 2), lax.div(me, 2)
+    for to in range(halves.shape[0]):
+        halves[pl.ds(to, 1), :] = jnp.broadcast_to(half_of(to, chip, core), (1, halves.shape[1]))
+
+
+def counts_kernel(halves, neigh, counts):
     index = neigh[:, 0, :]
     lane = lax.broadcasted_iota(jnp.int32, (index.shape[0], 128), 1)
     groups = []
     for at in range(0, index.shape[1] // 128, 2):
         a, b = (index[:, 128 * to : 128 * (to + 1)] for to in (at, at + 1))
-        first = jnp.where(half_of(at, chip, core) == 0, a, pltpu.roll(a, 64, 1))
-        second = jnp.where(half_of(at + 1, chip, core) == 0, pltpu.roll(b, 64, 1), b)
+        first = jnp.where(halves[pl.ds(at, 1), :] == 0, a, pltpu.roll(a, 64, 1))
+        second = jnp.where(halves[pl.ds(at + 1, 1), :] == 0, pltpu.roll(b, 64, 1), b)
         groups.append(jnp.where(lane < 64, first, second))
     index = jnp.concatenate(groups, axis=1)
     rows = [index[k : k + 1] for k in range(index.shape[0])]
@@ -96,34 +102,41 @@
             sent[at - 1][...] = pre.astype(jnp.bfloat16)
 
 
-def rows_kernel(*refs):
-    partials, kept, boundary, hidden, sent, picked = refs[:-7], refs[-7], refs[-6], refs[-5], refs[-4:-1], refs[-1]
+def turned(slots):
+    size = slots.shape[0]
+    same = lax.broadcasted_iota(jnp.int32, (size, size), 0) == lax.broadcasted_iota(jnp.int32, (size, size), 1)
+    return f32_dot_columns(slots, jnp.where(same, 1.0, 0.0).astype(jnp.bfloat16)).astype(jnp.bfloat16)
+
+
+def picks_kernel(share, boundary, neigh, chosen, counts, scratch):
     me = lax.axis_index("dom")
     core = lax.rem(lax.axis_index("feat"), 2)
+    scratch[...] = turned(counts_of([boundary[0]], 0, chosen.shape[1]))
+    places = [me]
+    sources = [me]
+    for tables in DOM_TO:
+        places.append(jnp.where(core == 0, look_up(tables[0], me), look_up(tables[1], me)))
+        sources.append(jnp.where(core == 0, look_up(inverse(tables[1]), me), look_up(inverse(tables[0]), me)))
+    for at, place in enumerate(places):
+        chosen[pl.ds(at * share, share), :] = scratch[pl.ds(pl.multiple_of(place * share, share), share), :]
+    rows = [neigh[k] for k in range(neigh.shape[0])]
+    local = chosen.shape[1]
+    parts = [counts_of(rows, 0, local)] + [counts_of(rows, local + source * share, share) for source in sources]
+    counts[...] = turned(jnp.concatenate(parts, axis=0))
+
+
+def rows_kernel(*refs):
+    partials, kept, chosen, hidden, sent = refs[:-6], refs[-6], refs[-5], refs[-4], refs[-3:]
     pre = kept[...]
     for part in partials:
         pre = pre + part[...].astype(jnp.float32)
     rows = jnp.maximum(pre, 0.0).astype(jnp.bfloat16)
     local, share = rows.shape[0], sent[0].shape[0]
-    picked[...] = f32_dot_columns(counts_of([boundary[0]], 0, local), rows).astype(jnp.bfloat16)
     hidden[pl.ds(0, local), :] = rows
-    hidden[pl.ds(local, share), :] = picked[pl.ds(pl.multiple_of(me * share, share), share), :]
-    for tables, to in zip(DOM_TO, sent):
-        place = jnp.where(core == 0, look_up(tables[0], me), look_up(tables[1], me))
-        to[...] = picked[pl.ds(pl.multiple_of(place * share, share), share), :]
-
-
-def slots_kernel(share, neigh, counts):
-    me = lax.axis_index("dom")
-    core = lax.rem(lax.axis_index("feat"), 2)
-    rows = [neigh[k] for k in range(neigh.shape[0])]
-    local = counts.shape[0] - (len(DOM_TO) + 1) * share
-    counts[pl.ds(0, local), :] = counts_of(rows, 0, local)
-    sources = [me]
-    for tables in DOM_TO:
-        sources.append(jnp.where(core == 0, look_up(inverse(tables[1]), me), look_up(inverse(tables[0]), me)))
-    for at, source in enumerate(sources):
-        counts[pl.ds(local + at * share, share), :] = counts_of(rows, local + source * share, share)
+    picked = f32_dot(chosen[...], rows).astype(jnp.bfloat16)
+    hidden[pl.ds(local, share), :] = picked[:share]
+    for at, to in enumerate(sent):
+        to[...] = picked[(at + 1) * share : (at + 2) * share]
 
 
 def join_kernel(*refs):
@@ -134,7 +147,7 @@
 
 def far_kernel(far, hidden, counts, weight, out):
     table = jnp.concatenate([hidden[...], far[...]], axis=0)
-    agg = (f32_dot_columns(counts[...], table) / FAN2).astype(jnp.bfloat16)
+    agg = (f32_dot(counts[...], table) / FAN2).astype(jnp.bfloat16)
     base = f32_dot(hidden[pl.ds(0, out.shape[1]), :], weight[0])
     out[0] = jnp.maximum(base + f32_dot(agg, weight[1]), 0.0).astype(jnp.bfloat16)
 
@@ -167,10 +180,16 @@
     shape = jax.ShapeDtypeStruct
     bf16, f32 = jnp.bfloat16, jnp.float32
 
+    halves = call(
+        halves_kernel, shape((feat_count // 2, 128), jnp.int32), [], "halves_of_chips", flops=AHEAD
+    )
+    their_weight = lax.ppermute(weight_one, "feat", apart_by(feat_count, 1))
     theirs = lax.ppermute(features, "feat", apart_by(feat_count, 1))
-    their_weight = lax.ppermute(weight_one, "feat", apart_by(feat_count, 1))
     counts = call(
-        counts_kernel, shape((features.shape[1], nodes // 2), bf16), [neigh_one.transpose(1, 0, 2)], "layer_one_counts"
+        counts_kernel,
+        shape((features.shape[1], nodes // 2), bf16),
+        [halves, neigh_one.transpose(1, 0, 2)],
+        "layer_one_counts",
     )
     chips = feat_count // 2
     kept, *sent = call(
@@ -187,12 +206,18 @@
     swap = apart_by(feat_count, 1)
     held, _ = lax.optimization_barrier((boundary, sent[0]))
     their_boundary = lax.ppermute(held, "feat", swap)
+    chosen, counts_two = call(
+        functools.partial(picks_kernel, share),
+        (shape((share * dom_count, local), bf16), shape((out_rows, local + share * dom_count), bf16)),
+        [their_boundary, neigh_two.transpose(2, 0, 1)],
+        "boundary_and_layer_two_counts",
+        scratch=[pltpu.VMEM((share * dom_count, local), bf16)],
+    )
     hidden, *sent = call(
         rows_kernel,
         (shape((local + share, width), bf16),) + (shape((share, width), bf16),) * (dom_count - 1),
-        [*partials, kept, their_boundary],
+        [*partials, kept, chosen],
         "hidden_and_boundary_rows",
-        scratch=[pltpu.VMEM((share * dom_count, width), bf16)],
     )
     incoming = [
         lax.ppermute(
@@ -207,14 +232,7 @@
         for tables, rows in zip(DOM_TO, sent)
     ]
     hidden = lax.ppermute(hidden, "feat", swap)
-    counts_two = call(
-        functools.partial(slots_kernel, share),
-        shape((local + share * dom_count, out_rows), bf16),
-        [neigh_two.transpose(2, 0, 1)],
-        "layer_two_counts",
-        flops=BESIDE,
-    )
-    far = call(join_kernel, shape((share * len(incoming), width), bf16), incoming, "far_rows", flops=BESIDE)
+    far = call(join_kernel, shape((share * len(incoming), width), bf16), incoming, "far_rows", flops=BEHIND)
     return call(
         far_kernel,
         shape((1, out_rows, weight_two.shape[2]), bf16),

time: 18.5 us -> 17.9 us (0.968)
  local copies, waits for them, and re-layouts: 0.8 us -> 0.49 us
    ppermute x3, waiting for transfers between devices: 2.26 us -> 1.6 us  [on_small_mesh(): lax.ppermute(rows, 'feat', [(2 * at + core, 2 * to + 1 - core) for at, to...]
    ppermute x1, waiting for transfers between devices: 0.01 us -> 0.5 us  [on_small_mesh(): theirs = lax.ppermute(features, 'feat', apart_by(feat_count, 1))]
    ppermute x1, starting transfers between devices: 0.06 us -> 0.45 us  [on_small_mesh(): their_weight = lax.ppermute(weight_one, 'feat', apart_by(feat_count, 1))]
    ppermute x1, starting transfers between devices: 0.45 us -> 0.06 us  [on_small_mesh(): theirs = lax.ppermute(features, 'feat', apart_by(feat_count, 1))]
    unnamed x12, local copies, waits for them, and re-layouts: 0.8 us -> 0.49 us
    ppermute x3, starting transfers between devices: 4.3 us -> 4.03 us  [on_small_mesh(): lax.ppermute(rows, 'feat', [(2 * at + core, 2 * to + 1 - core) for at, to...]
    ppermute x3, starting transfers between devices: 5 us -> 5.25 us  [on_small_mesh(): lax.ppermute(rows, ('feat', 'dom'), [(feat * dom_count + at, (feat ^ 1) *...]
    pallas_call x6 -> x7, Pallas kernels: 2.75 us -> 2.63 us  [call(): pl.pallas_call(kernel, out_shape=outs, in_specs=[VMEM] * len(operands), o...]
  transfers between devices with their start and end apart: 10 -> 10, of which waited for: 5 -> 7; matrix products, arithmetic and copies ran while one was open for 0% -> 0% of each run, Pallas kernels for 6% -> 5%
where the time goes in v5:
time: 17.9 us; the launch traced here: 17.8 us
  starting transfers between devices  9.95 us (56%)
  waiting for transfers between devices  4.63 us (26%)
  Pallas kernels  2.63 us (15%)
  local copies, waits for them, and re-layouts  0.49 us (3%)
    ppermute x3, starting transfers between devices, on_small_mesh(): lax.ppermute(rows, ('feat', 'dom'), [(feat * dom_count + at, (feat ^ 1) *...  5.25 us
    ppermute x3, starting transfers between devices, on_small_mesh(): lax.ppermute(rows, 'feat', [(2 * at + core, 2 * to + 1 - core) for at, to...  4.03 us
    pallas_call x7, Pallas kernels, call(): pl.pallas_call(kernel, out_shape=outs, in_specs=[VMEM] * len(operands), o...  2.63 us
    ppermute x3, waiting for transfers between devices, on_small_mesh(): lax.ppermute(rows, 'feat', [(2 * at + core, 2 * to + 1 - core) for at, to...  1.6 us
    ppermute x3, waiting for transfers between devices, on_small_mesh(): lax.ppermute(rows, ('feat', 'dom'), [(feat * dom_count + at, (feat ^ 1) *...  1.43 us
    ppermute x1, waiting for transfers between devices, on_small_mesh(): their_boundary = lax.ppermute(held, 'feat', swap)  0.97 us
    ppermute x1, waiting for transfers between devices, on_small_mesh(): theirs = lax.ppermute(features, 'feat', apart_by(feat_count, 1))  0.5 us
    unnamed x12, local copies, waits for them, and re-layouts  0.49 us
  transfers between devices with their start and end apart: 10, of which 7 were waited for; matrix products, arithmetic and copies ran while one was open for 0% of the time, Pallas kernels for 5%

profile of v5, /device:TPU:0, one launch (start us, length us, event | category | flops | bytes accessed | tf_op | source)
XLA Modules:
  0.0 17.8 jit_solution(18370916411302305141)
XLA Ops:
  0.0 0.0 copy-start.3
  0.0 0.5 %collective-permute-start.1 = (bf16[2,96,256]{2,1,0:T(8,128)(2,1)}, bf16[2,96,256]{2,1,0:T(8,128)(2,1)S(1)}, u32[]{:S(2)}, u32[]{:S(2)}) collective-permute-start(bf16[2,96,256]{2,1,0:T(8,128)(2,1)} %weight.2), channel_id=1, source_target_pairs={{0,4},{4,0},{8,12},{12,8},{16,20},{20,16},{24,28},{28,24},{1,5},{5... | collective-permute-start | bytes 294920 | tf_op jit(solution)/shard_map/ppermute | solution.py:186
  0.5 0.1 collective-permute-start
  0.5 0.2 %copy-done.3 = s32[1,15,512]{2,0,1:T(1,128)S(1)} copy-done((s32[1,15,512]{2,0,1:T(1,128)S(1)}, s32[1,15,512]{2,0,1:T(1,128)}, u32[]{:S(2)}) %copy-start.3) | copy-done | bytes 30744
  0.8 0.0 copy-start.1
  0.8 0.0 copy-start.2
  0.8 0.7 %layer_one_counts.1.counts = bf16[1024,256]{1,0:T(8,128)(2,1)S(1)} custom-call(s32[4,128]{1,0:T(4,128)S(1)} %halves_of_chips.1.halves, s32[15,1,512]{2,1,0:T(1,128)S(1)} %bitcast.2), custom_call_target="tpu_custom_call" | custom-call | tf_op jit(solution)/shard_map/layer_one_counts/pallas_call | solution.py:157
  1.5 0.1 collective-permute-done.1.their_weight
  1.6 0.5 %collective-permute-done.theirs = bf16[96,1024]{1,0:T(8,128)(2,1)S(1)} collective-permute-done((bf16[96,1024]{1,0:T(8,128)(2,1)}, bf16[96,1024]{1,0:T(8,128)(2,1)S(1)}, u32[]{:S(2)}, u32[]{:S(2)}) %collective-permute-start) | collective-permute-done | bytes 196640 | tf_op jit(solution)/shard_map/ppermute | solution.py:187
  2.1 0.0 copy-done.1
  2.1 0.0 copy-done.2
  2.1 0.6 %layer_one_sums.1 = (f32[64,256]{1,0:T(8,128)S(1)}, bf16[64,256]{1,0:T(8,128)(2,1)S(1)}, bf16[64,256]{1,0:T(8,128)(2,1)S(1)}, bf16[64,256]{1,0:T(8,128)(2,1)S(1)}) custom-call(bf16[96,1024]{1,0:T(8,128)(2,1)S(1)} %copy-done.1, bf16[96,1024]{1,0:T(8,128)(2,1)S(1)} %collective-permute-done.theirs, bf16[1024,256]{1,0:T(8,128)(2,1)S(1)} %layer_one_counts.1.counts, ...), custom_call_target="tpu_custom_call" | custom-call | tf_op jit(solution)/shard_map/layer_one_sums/pallas_call | solution.py:157
  2.8 0.0 copy-start.4
  2.8 3.6 %collective-permute-start.3 = (bf16[64,256]{1,0:T(8,128)(2,1)S(1)}, bf16[64,256]{1,0:T(8,128)(2,1)S(1)}, u32[]{:S(2)}, u32[]{:S(2)}) collective-permute-start(bf16[64,256]{1,0:T(8,128)(2,1)S(1)} %get-tuple-element.17), channel_id=1, source_target_pairs={{0,28},{4,24},{8,20},{12,16},{16,12},{20,8},{24,4},{28,0},{1,29},{... | collective-permute-start | bytes 98312 | tf_op jit(solution)/shard_map/ppermute | solution.py:203
  6.4 0.0 copy-start.5
  6.4 0.3 %collective-permute-start.4 = (bf16[64,256]{1,0:T(8,128)(2,1)S(1)}, bf16[64,256]{1,0:T(8,128)(2,1)S(1)}, u32[]{:S(2)}, u32[]{:S(2)}) collective-permute-start(bf16[64,256]{1,0:T(8,128)(2,1)S(1)} %get-tuple-element.18), channel_id=1, source_target_pairs={{0,12},{4,8},{8,4},{12,0},{16,28},{20,24},{24,20},{28,16},{1,13},{... | collective-permute-start | bytes 98312 | tf_op jit(solution)/shard_map/ppermute | solution.py:203
  6.7 0.1 collective-permute-start.2
  6.8 0.2 %copy-done.5 = s32[1,1,128]{2,1,0:T(1,128)S(1)} copy-done((s32[1,1,128]{2,1,0:T(1,128)S(1)}, s32[1,1,128]{2,1,0:T(1,128)}, u32[]{:S(2)}) %copy-start.5) | copy-done | bytes 536
  7.0 0.2 collective-permute-start.5
  7.2 1.0 %collective-permute-done.5.boundary = s32[1,1,128]{2,1,0:T(1,128)S(1)} collective-permute-done((s32[1,1,128]{2,1,0:T(1,128)S(1)}, s32[1,1,128]{2,1,0:T(1,128)S(1)}, u32[]{:S(2)}, u32[]{:S(2)}) %collective-permute-start.5) | collective-permute-done | bytes 544 | tf_op jit(solution)/shard_map/ppermute | solution.py:208
  8.2 0.0 copy-done.4
  8.2 0.2 %boundary_and_layer_two_counts.1 = (bf16[128,64]{1,0:T(8,128)(2,1)S(1)}, bf16[32,192]{1,0:T(8,128)(2,1)S(1)}) custom-call(s32[1,1,128]{2,1,0:T(1,128)S(1)} %collective-permute-done.5.boundary, s32[10,1,32]{2,1,0:T(1,128)S(1)} %bitcast.3), custom_call_target="tpu_custom_call" | custom-call | tf_op jit(solution)/shard_map/boundary_and_layer_two_counts/pallas_call | solution.py:157
  8.4 0.0 collective-permute-done.3.refs_1_
  8.4 1.3 %collective-permute-done.4.refs_2_ = bf16[64,256]{1,0:T(8,128)(2,1)S(1)} collective-permute-done((bf16[64,256]{1,0:T(8,128)(2,1)S(1)}, bf16[64,256]{1,0:T(8,128)(2,1)S(1)}, u32[]{:S(2)}, u32[]{:S(2)}) %collective-permute-start.4) | collective-permute-done | bytes 32800 | tf_op jit(solution)/shard_map/ppermute | solution.py:203
  9.7 0.3 %collective-permute-done.2.refs_0_ = bf16[64,256]{1,0:T(8,128)(2,1)S(1)} collective-permute-done((bf16[64,256]{1,0:T(8,128)(2,1)S(1)}, bf16[64,256]{1,0:T(8,128)(2,1)S(1)}, u32[]{:S(2)}, u32[]{:S(2)}) %collective-permute-start.2) | collective-permute-done | bytes 32800 | tf_op jit(solution)/shard_map/ppermute | solution.py:203
  10.0 0.1 hidden_and_boundary_rows.1
  10.2 1.6 %collective-permute-start.6 = (bf16[32,256]{1,0:T(8,128)(2,1)S(1)}, bf16[32,256]{1,0:T(8,128)(2,1)S(1)}, u32[]{:S(2)}, u32[]{:S(2)}) collective-permute-start(bf16[32,256]{1,0:T(8,128)(2,1)S(1)} %get-tuple-element.22), channel_id=1, source_target_pairs={{0,5},{1,6},{2,7},{3,4},{4,2},{5,3},{6,1},{7,0},{8,13},{9,14},{10,... | collective-permute-start | bytes 49160 | tf_op jit(solution)/shard_map/ppermute | solution.py:223
  11.8 1.2 %collective-permute-start.7 = (bf16[32,256]{1,0:T(8,128)(2,1)S(1)}, bf16[32,256]{1,0:T(8,128)(2,1)S(1)}, u32[]{:S(2)}, u32[]{:S(2)}) collective-permute-start(bf16[32,256]{1,0:T(8,128)(2,1)S(1)} %get-tuple-element.23), channel_id=1, source_target_pairs={{0,6},{1,7},{2,4},{3,5},{4,3},{5,2},{6,0},{7,1},{8,14},{9,15},{10,... | collective-permute-start | bytes 49160 | tf_op jit(solution)/shard_map/ppermute | solution.py:223
  13.0 2.4 %collective-permute-start.8 = (bf16[32,256]{1,0:T(8,128)(2,1)S(1)}, bf16[32,256]{1,0:T(8,128)(2,1)S(1)}, u32[]{:S(2)}, u32[]{:S(2)}) collective-permute-start(bf16[32,256]{1,0:T(8,128)(2,1)S(1)} %get-tuple-element.24), channel_id=1, source_target_pairs={{0,7},{1,4},{2,5},{3,6},{4,1},{5,0},{6,3},{7,2},{8,15},{9,12},{10,... | collective-permute-start | bytes 49160 | tf_op jit(solution)/shard_map/ppermute | solution.py:223
  15.4 0.0 copy-start
  15.4 0.0 collective-permute-start.9
  15.4 0.0 collective-permute-done.6.refs_0_
  15.4 0.5 %collective-permute-done.7.refs_1_ = bf16[32,256]{1,0:T(8,128)(2,1)S(1)} collective-permute-done((bf16[32,256]{1,0:T(8,128)(2,1)S(1)}, bf16[32,256]{1,0:T(8,128)(2,1)S(1)}, u32[]{:S(2)}, u32[]{:S(2)}) %collective-permute-start.7) | collective-permute-done | bytes 16416 | tf_op jit(solution)/shard_map/ppermute | solution.py:223
  15.9 1.0 %collective-permute-done.8.refs_2_ = bf16[32,256]{1,0:T(8,128)(2,1)S(1)} collective-permute-done((bf16[32,256]{1,0:T(8,128)(2,1)S(1)}, bf16[32,256]{1,0:T(8,128)(2,1)S(1)}, u32[]{:S(2)}, u32[]{:S(2)}) %collective-permute-start.8) | collective-permute-done | bytes 16416 | tf_op jit(solution)/shard_map/ppermute | solution.py:223
  16.9 0.0 collective-permute-done.9.hidden
  16.9 0.0 copy-done
  16.9 0.9 %layer_two_far.1 = bf16[1,32,256]{2,1,0:T(8,128)(2,1)} custom-call(bf16[96,256]{1,0:T(8,128)(2,1)S(1)} %far_rows.1.far, bf16[96,256]{1,0:T(8,128)(2,1)S(1)} %collective-permute-done.9.hidden, bf16[32,192]{1,0:T(8,128)(2,1)S(1)} %get-tuple-element.26.counts, bf16[2,256,256]{2,1,0:T(8,128)(2,1)S(1)} %copy-done), custom_call_target="tpu_custom_call" | custom-call | tf_op jit(solution)/shard_map/layer_two_far/pallas_call | solution.py:157
  (2 shorter events, 0.0 us)
Async XLA Ops:
  0.0 0.8 %copy-start.3 = (s32[1,15,512]{2,0,1:T(1,128)S(1)}, s32[1,15,512]{2,0,1:T(1,128)}, u32[]{:S(2)}) copy-start(s32[1,15,512]{2,0,1:T(1,128)} %param.7) | copy-start | bytes 92164
  0.0 1.6 %collective-permute-start.1 = (bf16[2,96,256]{2,1,0:T(8,128)(2,1)}, bf16[2,96,256]{2,1,0:T(8,128)(2,1)S(1)}, u32[]{:S(2)}, u32[]{:S(2)}) collective-permute-start(bf16[2,96,256]{2,1,0:T(8,128)(2,1)} %weight.2), channel_id=1, source_target_pairs={{0,4},{4,0},{8,12},{12,8},{16,20},{20,16},{24,28},{28,24},{1,5},{5... | collective-permute-start | bytes 294920 | tf_op jit(solution)/shard_map/ppermute | solution.py:186
  0.5 1.7 %collective-permute-start = (bf16[96,1024]{1,0:T(8,128)(2,1)}, bf16[96,1024]{1,0:T(8,128)(2,1)S(1)}, u32[]{:S(2)}, u32[]{:S(2)}) collective-permute-start(bf16[96,1024]{1,0:T(8,128)(2,1)} %mine.1), channel_id=1, source_target_pairs={{0,4},{4,0},{8,12},{12,8},{16,20},{20,16},{24,28},{28,24},{1,5},{5... | collective-permute-start | bytes 589832 | tf_op jit(solution)/shard_map/ppermute | solution.py:187
  0.8 1.4 %copy-start.1 = (bf16[96,1024]{1,0:T(8,128)(2,1)S(1)}, bf16[96,1024]{1,0:T(8,128)(2,1)}, u32[]{:S(2)}) copy-start(bf16[96,1024]{1,0:T(8,128)(2,1)} %mine.1) | copy-start | bytes 589828
  0.8 1.4 %copy-start.2 = (bf16[2,96,256]{2,1,0:T(8,128)(2,1)S(1)}, bf16[2,96,256]{2,1,0:T(8,128)(2,1)}, u32[]{:S(2)}) copy-start(bf16[2,96,256]{2,1,0:T(8,128)(2,1)} %weight.2) | copy-start | bytes 294916
  2.8 5.4 %copy-start.4 = (s32[1,32,10]{1,0,2:T(1,128)S(1)}, s32[1,32,10]{1,0,2:T(1,128)}, u32[]{:S(2)}) copy-start(s32[1,32,10]{1,0,2:T(1,128)} %param.9) | copy-start | bytes 3844
  2.8 5.7 %collective-permute-start.3 = (bf16[64,256]{1,0:T(8,128)(2,1)S(1)}, bf16[64,256]{1,0:T(8,128)(2,1)S(1)}, u32[]{:S(2)}, u32[]{:S(2)}) collective-permute-start(bf16[64,256]{1,0:T(8,128)(2,1)S(1)} %get-tuple-element.17), channel_id=1, source_target_pairs={{0,28},{4,24},{8,20},{12,16},{16,12},{20,8},{24,4},{28,0},{1,29},{... | collective-permute-start | bytes 98312 | tf_op jit(solution)/shard_map/ppermute | solution.py:203
  6.4 0.7 %copy-start.5 = (s32[1,1,128]{2,1,0:T(1,128)S(1)}, s32[1,1,128]{2,1,0:T(1,128)}, u32[]{:S(2)}) copy-start(s32[1,1,128]{2,1,0:T(1,128)} %param.8) | copy-start | bytes 1540
  6.4 3.4 %collective-permute-start.4 = (bf16[64,256]{1,0:T(8,128)(2,1)S(1)}, bf16[64,256]{1,0:T(8,128)(2,1)S(1)}, u32[]{:S(2)}, u32[]{:S(2)}) collective-permute-start(bf16[64,256]{1,0:T(8,128)(2,1)S(1)} %get-tuple-element.18), channel_id=1, source_target_pairs={{0,12},{4,8},{8,4},{12,0},{16,28},{20,24},{24,20},{28,16},{1,13},{... | collective-permute-start | bytes 98312 | tf_op jit(solution)/shard_map/ppermute | solution.py:203
  6.7 3.3 %collective-permute-start.2 = (bf16[64,256]{1,0:T(8,128)(2,1)S(1)}, bf16[64,256]{1,0:T(8,128)(2,1)S(1)}, u32[]{:S(2)}, u32[]{:S(2)}) collective-permute-start(bf16[64,256]{1,0:T(8,128)(2,1)S(1)} %get-tuple-element.16), channel_id=1, source_target_pairs={{0,20},{4,16},{8,28},{12,24},{16,4},{20,0},{24,12},{28,8},{1,21},{... | collective-permute-start | bytes 98312 | tf_op jit(solution)/shard_map/ppermute | solution.py:203
  7.0 1.1 %collective-permute-start.5 = (s32[1,1,128]{2,1,0:T(1,128)S(1)}, s32[1,1,128]{2,1,0:T(1,128)S(1)}, u32[]{:S(2)}, u32[]{:S(2)}) collective-permute-start(s32[1,1,128]{2,1,0:T(1,128)S(1)} %copy-done.5), channel_id=1, source_target_pairs={{0,4},{4,0},{8,12},{12,8},{16,20},{20,16},{24,28},{28,24},{1,5},{5... | collective-permute-start | bytes 1544 | tf_op jit(solution)/shard_map/ppermute | solution.py:208
  10.2 5.3 %collective-permute-start.6 = (bf16[32,256]{1,0:T(8,128)(2,1)S(1)}, bf16[32,256]{1,0:T(8,128)(2,1)S(1)}, u32[]{:S(2)}, u32[]{:S(2)}) collective-permute-start(bf16[32,256]{1,0:T(8,128)(2,1)S(1)} %get-tuple-element.22), channel_id=1, source_target_pairs={{0,5},{1,6},{2,7},{3,4},{4,2},{5,3},{6,1},{7,0},{8,13},{9,14},{10,... | collective-permute-start | bytes 49160 | tf_op jit(solution)/shard_map/ppermute | solution.py:223
  11.8 4.1 %collective-permute-start.7 = (bf16[32,256]{1,0:T(8,128)(2,1)S(1)}, bf16[32,256]{1,0:T(8,128)(2,1)S(1)}, u32[]{:S(2)}, u32[]{:S(2)}) collective-permute-start(bf16[32,256]{1,0:T(8,128)(2,1)S(1)} %get-tuple-element.23), channel_id=1, source_target_pairs={{0,6},{1,7},{2,4},{3,5},{4,3},{5,2},{6,0},{7,1},{8,14},{9,15},{10,... | collective-permute-start | bytes 49160 | tf_op jit(solution)/shard_map/ppermute | solution.py:223
  13.0 3.9 %collective-permute-start.8 = (bf16[32,256]{1,0:T(8,128)(2,1)S(1)}, bf16[32,256]{1,0:T(8,128)(2,1)S(1)}, u32[]{:S(2)}, u32[]{:S(2)}) collective-permute-start(bf16[32,256]{1,0:T(8,128)(2,1)S(1)} %get-tuple-element.24), channel_id=1, source_target_pairs={{0,7},{1,4},{2,5},{3,6},{4,1},{5,0},{6,3},{7,2},{8,15},{9,12},{10,... | collective-permute-start | bytes 49160 | tf_op jit(solution)/shard_map/ppermute | solution.py:223
  15.4 1.5 %copy-start = (bf16[2,256,256]{2,1,0:T(8,128)(2,1)S(1)}, bf16[2,256,256]{2,1,0:T(8,128)(2,1)}, u32[]{:S(2)}) copy-start(bf16[2,256,256]{2,1,0:T(8,128)(2,1)} %weight.3) | copy-start | bytes 786436
  15.4 1.4 %collective-permute-start.9 = (bf16[96,256]{1,0:T(8,128)(2,1)S(1)}, bf16[96,256]{1,0:T(8,128)(2,1)S(1)}, u32[]{:S(2)}, u32[]{:S(2)}) collective-permute-start(bf16[96,256]{1,0:T(8,128)(2,1)S(1)} %get-tuple-element.25), channel_id=1, source_target_pairs={{0,4},{4,0},{8,12},{12,8},{16,20},{20,16},{24,28},{28,24},{1,5},{5... | collective-permute-start | bytes 147464 | tf_op jit(solution)/shard_map/ppermute | solution.py:234

commit v6 on v5

--- a/solution.py
+++ b/solution.py
@@ -12,13 +12,13 @@
 FAN2 = 10
 CHUNK = 256
 BEHIND = 10**9
-AHEAD = 10**10
+AHEAD = 2 * 10**9
 COLUMNS_FIRST = (((0,), (0,)), ((), ()))
 VMEM = pl.BlockSpec(memory_space=pltpu.VMEM)
 CHIP_TO = ((2, 3, 0, 1), (3, 2, 1, 0), (1, 0, 3, 2))
 DOM_TO = (
-    ((1, 2, 3, 0), (2, 3, 1, 0)),
-    ((2, 3, 0, 1), (3, 2, 0, 1)),
+    ((1, 2, 3, 0), (2, 3, 0, 1)),
+    ((2, 3, 0, 1), (3, 2, 1, 0)),
     ((3, 0, 1, 2), (1, 0, 3, 2)),
 )
 

time: 17.9 us -> 17.8 us (level)
    ppermute x1, waiting for transfers between devices: 0.5 us -> 0.01 us  [on_small_mesh(): theirs = lax.ppermute(features, 'feat', apart_by(feat_count, 1))]
    ppermute x1, starting transfers between devices: 0.45 us -> 0.06 us  [on_small_mesh(): their_weight = lax.ppermute(weight_one, 'feat', apart_by(feat_count, 1))]
    ppermute x1, starting transfers between devices: 0.06 us -> 0.45 us  [on_small_mesh(): theirs = lax.ppermute(features, 'feat', apart_by(feat_count, 1))]
    ppermute x1, waiting for transfers between devices: 0.13 us -> 0.48 us  [on_small_mesh(): their_weight = lax.ppermute(weight_one, 'feat', apart_by(feat_count, 1))]
    ppermute x3, starting transfers between devices: 5.25 us -> 5.01 us  [on_small_mesh(): lax.ppermute(rows, ('feat', 'dom'), [(feat * dom_count + at, (feat ^ 1) *...]
  transfers between devices with their start and end apart: 10 -> 10, of which waited for: 7 -> 5; matrix products, arithmetic and copies ran while one was open for 0% -> 0% of each run, Pallas kernels for 5% -> 6%
where the time goes in v6:
time: 17.8 us; the launch traced here: 17.5 us
  starting transfers between devices  9.97 us (56%)
  waiting for transfers between devices  4.49 us (25%)
  Pallas kernels  2.63 us (15%)
  local copies, waits for them, and re-layouts  0.36 us (2%)
    ppermute x3, starting transfers between devices, on_small_mesh(): lax.ppermute(rows, ('feat', 'dom'), [(feat * dom_count + at, (feat ^ 1) *...  5.01 us
    ppermute x3, starting transfers between devices, on_small_mesh(): lax.ppermute(rows, 'feat', [(2 * at + core, 2 * to + 1 - core) for at, to...  4.16 us
    pallas_call x7, Pallas kernels, call(): pl.pallas_call(kernel, out_shape=outs, in_specs=[VMEM] * len(operands), o...  2.63 us
    ppermute x3, waiting for transfers between devices, on_small_mesh(): lax.ppermute(rows, 'feat', [(2 * at + core, 2 * to + 1 - core) for at, to...  1.73 us
    ppermute x3, waiting for transfers between devices, on_small_mesh(): lax.ppermute(rows, ('feat', 'dom'), [(feat * dom_count + at, (feat ^ 1) *...  1.43 us
    ppermute x1, waiting for transfers between devices, on_small_mesh(): their_boundary = lax.ppermute(held, 'feat', swap)  0.84 us
    ppermute x1, waiting for transfers between devices, on_small_mesh(): their_weight = lax.ppermute(weight_one, 'feat', apart_by(feat_count, 1))  0.48 us
    ppermute x1, starting transfers between devices, on_small_mesh(): theirs = lax.ppermute(features, 'feat', apart_by(feat_count, 1))  0.45 us
  transfers between devices with their start and end apart: 10, of which 5 were waited for; matrix products, arithmetic and copies ran while one was open for 0% of the time, Pallas kernels for 6%

profile of v6, /device:TPU:0, one launch (start us, length us, event | category | flops | bytes accessed | tf_op | source)
XLA Modules:
  0.0 17.5 jit_solution(18182504835325186422)
XLA Ops:
  0.0 0.0 copy-start.3
  0.0 0.5 %collective-permute-start = (bf16[96,1024]{1,0:T(8,128)(2,1)}, bf16[96,1024]{1,0:T(8,128)(2,1)S(1)}, u32[]{:S(2)}, u32[]{:S(2)}) collective-permute-start(bf16[96,1024]{1,0:T(8,128)(2,1)} %mine.1), channel_id=1, source_target_pairs={{0,4},{4,0},{8,12},{12,8},{16,20},{20,16},{24,28},{28,24},{1,5},{5... | collective-permute-start | bytes 589832 | tf_op jit(solution)/shard_map/ppermute | solution.py:187
  0.5 0.1 collective-permute-start.1
  0.5 0.2 %copy-done.3 = s32[1,15,512]{2,0,1:T(1,128)S(1)} copy-done((s32[1,15,512]{2,0,1:T(1,128)S(1)}, s32[1,15,512]{2,0,1:T(1,128)}, u32[]{:S(2)}) %copy-start.3) | copy-done | bytes 30744
  0.8 0.0 copy-start.1
  0.8 0.0 copy-start.2
  0.8 0.7 %layer_one_counts.1.counts = bf16[1024,256]{1,0:T(8,128)(2,1)S(1)} custom-call(s32[4,128]{1,0:T(4,128)S(1)} %halves_of_chips.1.halves, s32[15,1,512]{2,1,0:T(1,128)S(1)} %bitcast.2), custom_call_target="tpu_custom_call" | custom-call | tf_op jit(solution)/shard_map/layer_one_counts/pallas_call | solution.py:157
  1.5 0.5 %collective-permute-done.1.their_weight = bf16[2,96,256]{2,1,0:T(8,128)(2,1)S(1)} collective-permute-done((bf16[2,96,256]{2,1,0:T(8,128)(2,1)}, bf16[2,96,256]{2,1,0:T(8,128)(2,1)S(1)}, u32[]{:S(2)}, u32[]{:S(2)}) %collective-permute-start.1) | collective-permute-done | bytes 98336 | tf_op jit(solution)/shard_map/ppermute | solution.py:186
  2.0 0.0 collective-permute-done.theirs
  2.0 0.0 copy-done.1
  2.0 0.0 copy-done.2
  2.0 0.6 %layer_one_sums.1 = (f32[64,256]{1,0:T(8,128)S(1)}, bf16[64,256]{1,0:T(8,128)(2,1)S(1)}, bf16[64,256]{1,0:T(8,128)(2,1)S(1)}, bf16[64,256]{1,0:T(8,128)(2,1)S(1)}) custom-call(bf16[96,1024]{1,0:T(8,128)(2,1)S(1)} %copy-done.1, bf16[96,1024]{1,0:T(8,128)(2,1)S(1)} %collective-permute-done.theirs, bf16[1024,256]{1,0:T(8,128)(2,1)S(1)} %layer_one_counts.1.counts, ...), custom_call_target="tpu_custom_call" | custom-call | tf_op jit(solution)/shard_map/layer_one_sums/pallas_call | solution.py:157
  2.6 0.0 copy-start.4
  2.6 3.6 %collective-permute-start.3 = (bf16[64,256]{1,0:T(8,128)(2,1)S(1)}, bf16[64,256]{1,0:T(8,128)(2,1)S(1)}, u32[]{:S(2)}, u32[]{:S(2)}) collective-permute-start(bf16[64,256]{1,0:T(8,128)(2,1)S(1)} %get-tuple-element.17), channel_id=1, source_target_pairs={{0,28},{4,24},{8,20},{12,16},{16,12},{20,8},{24,4},{28,0},{1,29},{... | collective-permute-start | bytes 98312 | tf_op jit(solution)/shard_map/ppermute | solution.py:203
  6.3 0.0 copy-start.5
  6.3 0.4 %collective-permute-start.4 = (bf16[64,256]{1,0:T(8,128)(2,1)S(1)}, bf16[64,256]{1,0:T(8,128)(2,1)S(1)}, u32[]{:S(2)}, u32[]{:S(2)}) collective-permute-start(bf16[64,256]{1,0:T(8,128)(2,1)S(1)} %get-tuple-element.18), channel_id=1, source_target_pairs={{0,12},{4,8},{8,4},{12,0},{16,28},{20,24},{24,20},{28,16},{1,13},{... | collective-permute-start | bytes 98312 | tf_op jit(solution)/shard_map/ppermute | solution.py:203
  6.7 0.1 collective-permute-start.2
  6.8 0.1 copy-done.5
  6.9 0.3 %collective-permute-start.5 = (s32[1,1,128]{2,1,0:T(1,128)S(1)}, s32[1,1,128]{2,1,0:T(1,128)S(1)}, u32[]{:S(2)}, u32[]{:S(2)}) collective-permute-start(s32[1,1,128]{2,1,0:T(1,128)S(1)} %copy-done.5), channel_id=1, source_target_pairs={{0,4},{4,0},{8,12},{12,8},{16,20},{20,16},{24,28},{28,24},{1,5},{5... | collective-permute-start | bytes 1544 | tf_op jit(solution)/shard_map/ppermute | solution.py:208
  7.2 0.8 %collective-permute-done.5.boundary = s32[1,1,128]{2,1,0:T(1,128)S(1)} collective-permute-done((s32[1,1,128]{2,1,0:T(1,128)S(1)}, s32[1,1,128]{2,1,0:T(1,128)S(1)}, u32[]{:S(2)}, u32[]{:S(2)}) %collective-permute-start.5) | collective-permute-done | bytes 544 | tf_op jit(solution)/shard_map/ppermute | solution.py:208
  8.0 0.0 copy-done.4
  8.0 0.2 %boundary_and_layer_two_counts.1 = (bf16[128,64]{1,0:T(8,128)(2,1)S(1)}, bf16[32,192]{1,0:T(8,128)(2,1)S(1)}) custom-call(s32[1,1,128]{2,1,0:T(1,128)S(1)} %collective-permute-done.5.boundary, s32[10,1,32]{2,1,0:T(1,128)S(1)} %bitcast.3), custom_call_target="tpu_custom_call" | custom-call | tf_op jit(solution)/shard_map/boundary_and_layer_two_counts/pallas_call | solution.py:157
  8.3 0.0 collective-permute-done.3.refs_1_
  8.3 1.3 %collective-permute-done.4.refs_2_ = bf16[64,256]{1,0:T(8,128)(2,1)S(1)} collective-permute-done((bf16[64,256]{1,0:T(8,128)(2,1)S(1)}, bf16[64,256]{1,0:T(8,128)(2,1)S(1)}, u32[]{:S(2)}, u32[]{:S(2)}) %collective-permute-start.4) | collective-permute-done | bytes 32800 | tf_op jit(solution)/shard_map/ppermute | solution.py:203
  9.6 0.4 %collective-permute-done.2.refs_0_ = bf16[64,256]{1,0:T(8,128)(2,1)S(1)} collective-permute-done((bf16[64,256]{1,0:T(8,128)(2,1)S(1)}, bf16[64,256]{1,0:T(8,128)(2,1)S(1)}, u32[]{:S(2)}, u32[]{:S(2)}) %collective-permute-start.2) | collective-permute-done | bytes 32800 | tf_op jit(solution)/shard_map/ppermute | solution.py:203
  10.0 0.1 hidden_and_boundary_rows.1
  10.2 1.5 %collective-permute-start.6 = (bf16[32,256]{1,0:T(8,128)(2,1)S(1)}, bf16[32,256]{1,0:T(8,128)(2,1)S(1)}, u32[]{:S(2)}, u32[]{:S(2)}) collective-permute-start(bf16[32,256]{1,0:T(8,128)(2,1)S(1)} %get-tuple-element.22), channel_id=1, source_target_pairs={{0,5},{1,6},{2,7},{3,4},{4,2},{5,3},{6,0},{7,1},{8,13},{9,14},{10,... | collective-permute-start | bytes 49160 | tf_op jit(solution)/shard_map/ppermute | solution.py:223
  11.6 1.2 %collective-permute-start.7 = (bf16[32,256]{1,0:T(8,128)(2,1)S(1)}, bf16[32,256]{1,0:T(8,128)(2,1)S(1)}, u32[]{:S(2)}, u32[]{:S(2)}) collective-permute-start(bf16[32,256]{1,0:T(8,128)(2,1)S(1)} %get-tuple-element.23), channel_id=1, source_target_pairs={{0,6},{1,7},{2,4},{3,5},{4,3},{5,2},{6,1},{7,0},{8,14},{9,15},{10,... | collective-permute-start | bytes 49160 | tf_op jit(solution)/shard_map/ppermute | solution.py:223
  12.9 2.3 %collective-permute-start.8 = (bf16[32,256]{1,0:T(8,128)(2,1)S(1)}, bf16[32,256]{1,0:T(8,128)(2,1)S(1)}, u32[]{:S(2)}, u32[]{:S(2)}) collective-permute-start(bf16[32,256]{1,0:T(8,128)(2,1)S(1)} %get-tuple-element.24), channel_id=1, source_target_pairs={{0,7},{1,4},{2,5},{3,6},{4,1},{5,0},{6,3},{7,2},{8,15},{9,12},{10,... | collective-permute-start | bytes 49160 | tf_op jit(solution)/shard_map/ppermute | solution.py:223
  15.2 0.0 copy-start
  15.2 0.0 collective-permute-start.9
  15.2 0.0 collective-permute-done.6.refs_0_
  15.2 1.4 %collective-permute-done.7.refs_1_ = bf16[32,256]{1,0:T(8,128)(2,1)S(1)} collective-permute-done((bf16[32,256]{1,0:T(8,128)(2,1)S(1)}, bf16[32,256]{1,0:T(8,128)(2,1)S(1)}, u32[]{:S(2)}, u32[]{:S(2)}) %collective-permute-start.7) | collective-permute-done | bytes 16416 | tf_op jit(solution)/shard_map/ppermute | solution.py:223
  16.6 0.0 collective-permute-done.8.refs_2_
  16.6 0.0 collective-permute-done.9.hidden
  16.6 0.0 copy-done
  16.6 0.9 %layer_two_far.1 = bf16[1,32,256]{2,1,0:T(8,128)(2,1)} custom-call(bf16[96,256]{1,0:T(8,128)(2,1)S(1)} %far_rows.1.far, bf16[96,256]{1,0:T(8,128)(2,1)S(1)} %collective-permute-done.9.hidden, bf16[32,192]{1,0:T(8,128)(2,1)S(1)} %get-tuple-element.26.counts, bf16[2,256,256]{2,1,0:T(8,128)(2,1)S(1)} %copy-done), custom_call_target="tpu_custom_call" | custom-call | tf_op jit(solution)/shard_map/layer_two_far/pallas_call | solution.py:157
  (2 shorter events, 0.0 us)
Async XLA Ops:
  0.0 0.8 %copy-start.3 = (s32[1,15,512]{2,0,1:T(1,128)S(1)}, s32[1,15,512]{2,0,1:T(1,128)}, u32[]{:S(2)}) copy-start(s32[1,15,512]{2,0,1:T(1,128)} %param.7) | copy-start | bytes 92164
  0.0 2.0 %collective-permute-start = (bf16[96,1024]{1,0:T(8,128)(2,1)}, bf16[96,1024]{1,0:T(8,128)(2,1)S(1)}, u32[]{:S(2)}, u32[]{:S(2)}) collective-permute-start(bf16[96,1024]{1,0:T(8,128)(2,1)} %mine.1), channel_id=1, source_target_pairs={{0,4},{4,0},{8,12},{12,8},{16,20},{20,16},{24,28},{28,24},{1,5},{5... | collective-permute-start | bytes 589832 | tf_op jit(solution)/shard_map/ppermute | solution.py:187
  0.5 1.5 %collective-permute-start.1 = (bf16[2,96,256]{2,1,0:T(8,128)(2,1)}, bf16[2,96,256]{2,1,0:T(8,128)(2,1)S(1)}, u32[]{:S(2)}, u32[]{:S(2)}) collective-permute-start(bf16[2,96,256]{2,1,0:T(8,128)(2,1)} %weight.2), channel_id=1, source_target_pairs={{0,4},{4,0},{8,12},{12,8},{16,20},{20,16},{24,28},{28,24},{1,5},{5... | collective-permute-start | bytes 294920 | tf_op jit(solution)/shard_map/ppermute | solution.py:186
  0.8 1.2 %copy-start.1 = (bf16[96,1024]{1,0:T(8,128)(2,1)S(1)}, bf16[96,1024]{1,0:T(8,128)(2,1)}, u32[]{:S(2)}) copy-start(bf16[96,1024]{1,0:T(8,128)(2,1)} %mine.1) | copy-start | bytes 589828
  0.8 1.2 %copy-start.2 = (bf16[2,96,256]{2,1,0:T(8,128)(2,1)S(1)}, bf16[2,96,256]{2,1,0:T(8,128)(2,1)}, u32[]{:S(2)}) copy-start(bf16[2,96,256]{2,1,0:T(8,128)(2,1)} %weight.2) | copy-start | bytes 294916
  2.6 5.4 %copy-start.4 = (s32[1,32,10]{1,0,2:T(1,128)S(1)}, s32[1,32,10]{1,0,2:T(1,128)}, u32[]{:S(2)}) copy-start(s32[1,32,10]{1,0,2:T(1,128)} %param.9) | copy-start | bytes 3844
  2.6 5.7 %collective-permute-start.3 = (bf16[64,256]{1,0:T(8,128)(2,1)S(1)}, bf16[64,256]{1,0:T(8,128)(2,1)S(1)}, u32[]{:S(2)}, u32[]{:S(2)}) collective-permute-start(bf16[64,256]{1,0:T(8,128)(2,1)S(1)} %get-tuple-element.17), channel_id=1, source_target_pairs={{0,28},{4,24},{8,20},{12,16},{16,12},{20,8},{24,4},{28,0},{1,29},{... | collective-permute-start | bytes 98312 | tf_op jit(solution)/shard_map/ppermute | solution.py:203
  6.3 0.7 %copy-start.5 = (s32[1,1,128]{2,1,0:T(1,128)S(1)}, s32[1,1,128]{2,1,0:T(1,128)}, u32[]{:S(2)}) copy-start(s32[1,1,128]{2,1,0:T(1,128)} %param.8) | copy-start | bytes 1540
  6.3 3.3 %collective-permute-start.4 = (bf16[64,256]{1,0:T(8,128)(2,1)S(1)}, bf16[64,256]{1,0:T(8,128)(2,1)S(1)}, u32[]{:S(2)}, u32[]{:S(2)}) collective-permute-start(bf16[64,256]{1,0:T(8,128)(2,1)S(1)} %get-tuple-element.18), channel_id=1, source_target_pairs={{0,12},{4,8},{8,4},{12,0},{16,28},{20,24},{24,20},{28,16},{1,13},{... | collective-permute-start | bytes 98312 | tf_op jit(solution)/shard_map/ppermute | solution.py:203
  6.7 3.3 %collective-permute-start.2 = (bf16[64,256]{1,0:T(8,128)(2,1)S(1)}, bf16[64,256]{1,0:T(8,128)(2,1)S(1)}, u32[]{:S(2)}, u32[]{:S(2)}) collective-permute-start(bf16[64,256]{1,0:T(8,128)(2,1)S(1)} %get-tuple-element.16), channel_id=1, source_target_pairs={{0,20},{4,16},{8,28},{12,24},{16,4},{20,0},{24,12},{28,8},{1,21},{... | collective-permute-start | bytes 98312 | tf_op jit(solution)/shard_map/ppermute | solution.py:203
  6.9 1.1 %collective-permute-start.5 = (s32[1,1,128]{2,1,0:T(1,128)S(1)}, s32[1,1,128]{2,1,0:T(1,128)S(1)}, u32[]{:S(2)}, u32[]{:S(2)}) collective-permute-start(s32[1,1,128]{2,1,0:T(1,128)S(1)} %copy-done.5), channel_id=1, source_target_pairs={{0,4},{4,0},{8,12},{12,8},{16,20},{20,16},{24,28},{28,24},{1,5},{5... | collective-permute-start | bytes 1544 | tf_op jit(solution)/shard_map/ppermute | solution.py:208
  10.2 5.0 %collective-permute-start.6 = (bf16[32,256]{1,0:T(8,128)(2,1)S(1)}, bf16[32,256]{1,0:T(8,128)(2,1)S(1)}, u32[]{:S(2)}, u32[]{:S(2)}) collective-permute-start(bf16[32,256]{1,0:T(8,128)(2,1)S(1)} %get-tuple-element.22), channel_id=1, source_target_pairs={{0,5},{1,6},{2,7},{3,4},{4,2},{5,3},{6,0},{7,1},{8,13},{9,14},{10,... | collective-permute-start | bytes 49160 | tf_op jit(solution)/shard_map/ppermute | solution.py:223
  11.6 5.0 %collective-permute-start.7 = (bf16[32,256]{1,0:T(8,128)(2,1)S(1)}, bf16[32,256]{1,0:T(8,128)(2,1)S(1)}, u32[]{:S(2)}, u32[]{:S(2)}) collective-permute-start(bf16[32,256]{1,0:T(8,128)(2,1)S(1)} %get-tuple-element.23), channel_id=1, source_target_pairs={{0,6},{1,7},{2,4},{3,5},{4,3},{5,2},{6,1},{7,0},{8,14},{9,15},{10,... | collective-permute-start | bytes 49160 | tf_op jit(solution)/shard_map/ppermute | solution.py:223
  12.9 3.8 %collective-permute-start.8 = (bf16[32,256]{1,0:T(8,128)(2,1)S(1)}, bf16[32,256]{1,0:T(8,128)(2,1)S(1)}, u32[]{:S(2)}, u32[]{:S(2)}) collective-permute-start(bf16[32,256]{1,0:T(8,128)(2,1)S(1)} %get-tuple-element.24), channel_id=1, source_target_pairs={{0,7},{1,4},{2,5},{3,6},{4,1},{5,0},{6,3},{7,2},{8,15},{9,12},{10,... | collective-permute-start | bytes 49160 | tf_op jit(solution)/shard_map/ppermute | solution.py:223
  15.2 1.5 %copy-start = (bf16[2,256,256]{2,1,0:T(8,128)(2,1)S(1)}, bf16[2,256,256]{2,1,0:T(8,128)(2,1)}, u32[]{:S(2)}) copy-start(bf16[2,256,256]{2,1,0:T(8,128)(2,1)} %weight.3) | copy-start | bytes 786436
  15.2 1.4 %collective-permute-start.9 = (bf16[96,256]{1,0:T(8,128)(2,1)S(1)}, bf16[96,256]{1,0:T(8,128)(2,1)S(1)}, u32[]{:S(2)}, u32[]{:S(2)}) collective-permute-start(bf16[96,256]{1,0:T(8,128)(2,1)S(1)} %get-tuple-element.25), channel_id=1, source_target_pairs={{0,4},{4,0},{8,12},{12,8},{16,20},{20,16},{24,28},{28,24},{1,5},{5... | collective-permute-start | bytes 147464 | tf_op jit(solution)/shard_map/ppermute | solution.py:234

commit v7 on v6

--- a/solution.py
+++ b/solution.py
@@ -145,8 +145,8 @@
         rows[pl.ds(at * part.shape[0], part.shape[0]), :] = part[...]
 
 
-def far_kernel(far, hidden, counts, weight, out):
-    table = jnp.concatenate([hidden[...], far[...]], axis=0)
+def far_kernel(far, last, hidden, counts, weight, out):
+    table = jnp.concatenate([hidden[...], far[...], last[...]], axis=0)
     agg = (f32_dot(counts[...], table) / FAN2).astype(jnp.bfloat16)
     base = f32_dot(hidden[pl.ds(0, out.shape[1]), :], weight[0])
     out[0] = jnp.maximum(base + f32_dot(agg, weight[1]), 0.0).astype(jnp.bfloat16)
@@ -232,11 +232,11 @@
         for tables, rows in zip(DOM_TO, sent)
     ]
     hidden = lax.ppermute(hidden, "feat", swap)
-    far = call(join_kernel, shape((share * len(incoming), width), bf16), incoming, "far_rows", flops=BEHIND)
+    far = call(join_kernel, shape((share * (len(incoming) - 1), width), bf16), incoming[:-1], "far_rows", flops=BEHIND)
     return call(
         far_kernel,
         shape((1, out_rows, weight_two.shape[2]), bf16),
-        [far, hidden, counts_two, weight_two],
+        [far, incoming[-1], hidden, counts_two, weight_two],
         "layer_two_far",
     )
 

time: 17.8 us -> 17.8 us (level)
  no operation moved by 1% of the time
where the time goes in v7:
time: 17.8 us; the launch traced here: 17.5 us
  starting transfers between devices  9.97 us (56%)
  waiting for transfers between devices  4.49 us (25%)
  Pallas kernels  2.63 us (15%)
  local copies, waits for them, and re-layouts  0.36 us (2%)
    ppermute x3, starting transfers between devices, on_small_mesh(): lax.ppermute(rows, ('feat', 'dom'), [(feat * dom_count + at, (feat ^ 1) *...  5.01 us
    ppermute x3, starting transfers between devices, on_small_mesh(): lax.ppermute(rows, 'feat', [(2 * at + core, 2 * to + 1 - core) for at, to...  4.16 us
    pallas_call x7, Pallas kernels, call(): pl.pallas_call(kernel, out_shape=outs, in_specs=[VMEM] * len(operands), o...  2.63 us
    ppermute x3, waiting for transfers between devices, on_small_mesh(): lax.ppermute(rows, 'feat', [(2 * at + core, 2 * to + 1 - core) for at, to...  1.73 us
    ppermute x3, waiting for transfers between devices, on_small_mesh(): lax.ppermute(rows, ('feat', 'dom'), [(feat * dom_count + at, (feat ^ 1) *...  1.43 us
    ppermute x1, waiting for transfers between devices, on_small_mesh(): their_boundary = lax.ppermute(held, 'feat', swap)  0.84 us
    ppermute x1, waiting for transfers between devices, on_small_mesh(): their_weight = lax.ppermute(weight_one, 'feat', apart_by(feat_count, 1))  0.48 us
    ppermute x1, starting transfers between devices, on_small_mesh(): theirs = lax.ppermute(features, 'feat', apart_by(feat_count, 1))  0.45 us
  transfers between devices with their start and end apart: 10, of which 5 were waited for; matrix products, arithmetic and copies ran while one was open for 0% of the time, Pallas kernels for 6%

profile of v7, /device:TPU:0, one launch (start us, length us, event | category | flops | bytes accessed | tf_op | source)
XLA Modules:
  0.0 17.5 jit_solution(49383333285620579)
XLA Ops:
  0.0 0.0 copy-start.3
  0.0 0.5 %collective-permute-start = (bf16[96,1024]{1,0:T(8,128)(2,1)}, bf16[96,1024]{1,0:T(8,128)(2,1)S(1)}, u32[]{:S(2)}, u32[]{:S(2)}) collective-permute-start(bf16[96,1024]{1,0:T(8,128)(2,1)} %mine.1), channel_id=1, source_target_pairs={{0,4},{4,0},{8,12},{12,8},{16,20},{20,16},{24,28},{28,24},{1,5},{5... | collective-permute-start | bytes 589832 | tf_op jit(solution)/shard_map/ppermute | solution.py:187
  0.5 0.1 collective-permute-start.1
  0.5 0.2 %copy-done.3 = s32[1,15,512]{2,0,1:T(1,128)S(1)} copy-done((s32[1,15,512]{2,0,1:T(1,128)S(1)}, s32[1,15,512]{2,0,1:T(1,128)}, u32[]{:S(2)}) %copy-start.3) | copy-done | bytes 30744
  0.8 0.0 copy-start.1
  0.8 0.0 copy-start.2
  0.8 0.7 %layer_one_counts.1.counts = bf16[1024,256]{1,0:T(8,128)(2,1)S(1)} custom-call(s32[4,128]{1,0:T(4,128)S(1)} %halves_of_chips.1.halves, s32[15,1,512]{2,1,0:T(1,128)S(1)} %bitcast.2), custom_call_target="tpu_custom_call" | custom-call | tf_op jit(solution)/shard_map/layer_one_counts/pallas_call | solution.py:157
  1.5 0.5 %collective-permute-done.1.their_weight = bf16[2,96,256]{2,1,0:T(8,128)(2,1)S(1)} collective-permute-done((bf16[2,96,256]{2,1,0:T(8,128)(2,1)}, bf16[2,96,256]{2,1,0:T(8,128)(2,1)S(1)}, u32[]{:S(2)}, u32[]{:S(2)}) %collective-permute-start.1) | collective-permute-done | bytes 98336 | tf_op jit(solution)/shard_map/ppermute | solution.py:186
  2.0 0.0 collective-permute-done.theirs
  2.0 0.0 copy-done.1
  2.0 0.0 copy-done.2
  2.0 0.6 %layer_one_sums.1 = (f32[64,256]{1,0:T(8,128)S(1)}, bf16[64,256]{1,0:T(8,128)(2,1)S(1)}, bf16[64,256]{1,0:T(8,128)(2,1)S(1)}, bf16[64,256]{1,0:T(8,128)(2,1)S(1)}) custom-call(bf16[96,1024]{1,0:T(8,128)(2,1)S(1)} %copy-done.1, bf16[96,1024]{1,0:T(8,128)(2,1)S(1)} %collective-permute-done.theirs, bf16[1024,256]{1,0:T(8,128)(2,1)S(1)} %layer_one_counts.1.counts, ...), custom_call_target="tpu_custom_call" | custom-call | tf_op jit(solution)/shard_map/layer_one_sums/pallas_call | solution.py:157
  2.6 0.0 copy-start.4
  2.6 3.6 %collective-permute-start.3 = (bf16[64,256]{1,0:T(8,128)(2,1)S(1)}, bf16[64,256]{1,0:T(8,128)(2,1)S(1)}, u32[]{:S(2)}, u32[]{:S(2)}) collective-permute-start(bf16[64,256]{1,0:T(8,128)(2,1)S(1)} %get-tuple-element.17), channel_id=1, source_target_pairs={{0,28},{4,24},{8,20},{12,16},{16,12},{20,8},{24,4},{28,0},{1,29},{... | collective-permute-start | bytes 98312 | tf_op jit(solution)/shard_map/ppermute | solution.py:203
  6.3 0.0 copy-start.5
  6.3 0.4 %collective-permute-start.4 = (bf16[64,256]{1,0:T(8,128)(2,1)S(1)}, bf16[64,256]{1,0:T(8,128)(2,1)S(1)}, u32[]{:S(2)}, u32[]{:S(2)}) collective-permute-start(bf16[64,256]{1,0:T(8,128)(2,1)S(1)} %get-tuple-element.18), channel_id=1, source_target_pairs={{0,12},{4,8},{8,4},{12,0},{16,28},{20,24},{24,20},{28,16},{1,13},{... | collective-permute-start | bytes 98312 | tf_op jit(solution)/shard_map/ppermute | solution.py:203
  6.7 0.1 collective-permute-start.2
  6.8 0.1 copy-done.5
  6.9 0.3 %collective-permute-start.5 = (s32[1,1,128]{2,1,0:T(1,128)S(1)}, s32[1,1,128]{2,1,0:T(1,128)S(1)}, u32[]{:S(2)}, u32[]{:S(2)}) collective-permute-start(s32[1,1,128]{2,1,0:T(1,128)S(1)} %copy-done.5), channel_id=1, source_target_pairs={{0,4},{4,0},{8,12},{12,8},{16,20},{20,16},{24,28},{28,24},{1,5},{5... | collective-permute-start | bytes 1544 | tf_op jit(solution)/shard_map/ppermute | solution.py:208
  7.2 0.8 %collective-permute-done.5.boundary = s32[1,1,128]{2,1,0:T(1,128)S(1)} collective-permute-done((s32[1,1,128]{2,1,0:T(1,128)S(1)}, s32[1,1,128]{2,1,0:T(1,128)S(1)}, u32[]{:S(2)}, u32[]{:S(2)}) %collective-permute-start.5) | collective-permute-done | bytes 544 | tf_op jit(solution)/shard_map/ppermute | solution.py:208
  8.0 0.0 copy-done.4
  8.0 0.2 %boundary_and_layer_two_counts.1 = (bf16[128,64]{1,0:T(8,128)(2,1)S(1)}, bf16[32,192]{1,0:T(8,128)(2,1)S(1)}) custom-call(s32[1,1,128]{2,1,0:T(1,128)S(1)} %collective-permute-done.5.boundary, s32[10,1,32]{2,1,0:T(1,128)S(1)} %bitcast.3), custom_call_target="tpu_custom_call" | custom-call | tf_op jit(solution)/shard_map/boundary_and_layer_two_counts/pallas_call | solution.py:157
  8.3 0.0 collective-permute-done.3.refs_1_
  8.3 1.3 %collective-permute-done.4.refs_2_ = bf16[64,256]{1,0:T(8,128)(2,1)S(1)} collective-permute-done((bf16[64,256]{1,0:T(8,128)(2,1)S(1)}, bf16[64,256]{1,0:T(8,128)(2,1)S(1)}, u32[]{:S(2)}, u32[]{:S(2)}) %collective-permute-start.4) | collective-permute-done | bytes 32800 | tf_op jit(solution)/shard_map/ppermute | solution.py:203
  9.6 0.4 %collective-permute-done.2.refs_0_ = bf16[64,256]{1,0:T(8,128)(2,1)S(1)} collective-permute-done((bf16[64,256]{1,0:T(8,128)(2,1)S(1)}, bf16[64,256]{1,0:T(8,128)(2,1)S(1)}, u32[]{:S(2)}, u32[]{:S(2)}) %collective-permute-start.2) | collective-permute-done | bytes 32800 | tf_op jit(solution)/shard_map/ppermute | solution.py:203
  10.0 0.1 hidden_and_boundary_rows.1
  10.2 1.5 %collective-permute-start.6 = (bf16[32,256]{1,0:T(8,128)(2,1)S(1)}, bf16[32,256]{1,0:T(8,128)(2,1)S(1)}, u32[]{:S(2)}, u32[]{:S(2)}) collective-permute-start(bf16[32,256]{1,0:T(8,128)(2,1)S(1)} %get-tuple-element.22), channel_id=1, source_target_pairs={{0,5},{1,6},{2,7},{3,4},{4,2},{5,3},{6,0},{7,1},{8,13},{9,14},{10,... | collective-permute-start | bytes 49160 | tf_op jit(solution)/shard_map/ppermute | solution.py:223
  11.6 1.2 %collective-permute-start.7 = (bf16[32,256]{1,0:T(8,128)(2,1)S(1)}, bf16[32,256]{1,0:T(8,128)(2,1)S(1)}, u32[]{:S(2)}, u32[]{:S(2)}) collective-permute-start(bf16[32,256]{1,0:T(8,128)(2,1)S(1)} %get-tuple-element.23), channel_id=1, source_target_pairs={{0,6},{1,7},{2,4},{3,5},{4,3},{5,2},{6,1},{7,0},{8,14},{9,15},{10,... | collective-permute-start | bytes 49160 | tf_op jit(solution)/shard_map/ppermute | solution.py:223
  12.9 2.3 %collective-permute-start.8 = (bf16[32,256]{1,0:T(8,128)(2,1)S(1)}, bf16[32,256]{1,0:T(8,128)(2,1)S(1)}, u32[]{:S(2)}, u32[]{:S(2)}) collective-permute-start(bf16[32,256]{1,0:T(8,128)(2,1)S(1)} %get-tuple-element.24), channel_id=1, source_target_pairs={{0,7},{1,4},{2,5},{3,6},{4,1},{5,0},{6,3},{7,2},{8,15},{9,12},{10,... | collective-permute-start | bytes 49160 | tf_op jit(solution)/shard_map/ppermute | solution.py:223
  15.2 0.0 copy-start
  15.2 0.0 collective-permute-start.9
  15.2 0.0 collective-permute-done.6.refs_0_
  15.2 1.4 %collective-permute-done.7.refs_1_ = bf16[32,256]{1,0:T(8,128)(2,1)S(1)} collective-permute-done((bf16[32,256]{1,0:T(8,128)(2,1)S(1)}, bf16[32,256]{1,0:T(8,128)(2,1)S(1)}, u32[]{:S(2)}, u32[]{:S(2)}) %collective-permute-start.7) | collective-permute-done | bytes 16416 | tf_op jit(solution)/shard_map/ppermute | solution.py:223
  16.6 0.0 collective-permute-done.8.last
  16.6 0.0 collective-permute-done.9.hidden
  16.6 0.0 copy-done
  16.6 0.9 %layer_two_far.1 = bf16[1,32,256]{2,1,0:T(8,128)(2,1)} custom-call(bf16[64,256]{1,0:T(8,128)(2,1)S(1)} %far_rows.1.far, bf16[32,256]{1,0:T(8,128)(2,1)S(1)} %collective-permute-done.8.last, bf16[96,256]{1,0:T(8,128)(2,1)S(1)} %collective-permute-done.9.hidden, bf16[32,192]{1,0:T(8,128)(2,1)S(1)} %get-tuple-element.26.counts, bf16[2,256,256]{2,1,0:T(8,128)(2,1)S(1)} %copy-done), custom_call_target="tpu_custom_call" | custom-call | tf_op jit(solution)/shard_map/layer_two_far/pallas_call | solution.py:157
  (2 shorter events, 0.0 us)
Async XLA Ops:
  0.0 0.8 %copy-start.3 = (s32[1,15,512]{2,0,1:T(1,128)S(1)}, s32[1,15,512]{2,0,1:T(1,128)}, u32[]{:S(2)}) copy-start(s32[1,15,512]{2,0,1:T(1,128)} %param.7) | copy-start | bytes 92164
  0.0 2.0 %collective-permute-start = (bf16[96,1024]{1,0:T(8,128)(2,1)}, bf16[96,1024]{1,0:T(8,128)(2,1)S(1)}, u32[]{:S(2)}, u32[]{:S(2)}) collective-permute-start(bf16[96,1024]{1,0:T(8,128)(2,1)} %mine.1), channel_id=1, source_target_pairs={{0,4},{4,0},{8,12},{12,8},{16,20},{20,16},{24,28},{28,24},{1,5},{5... | collective-permute-start | bytes 589832 | tf_op jit(solution)/shard_map/ppermute | solution.py:187
  0.5 1.5 %collective-permute-start.1 = (bf16[2,96,256]{2,1,0:T(8,128)(2,1)}, bf16[2,96,256]{2,1,0:T(8,128)(2,1)S(1)}, u32[]{:S(2)}, u32[]{:S(2)}) collective-permute-start(bf16[2,96,256]{2,1,0:T(8,128)(2,1)} %weight.2), channel_id=1, source_target_pairs={{0,4},{4,0},{8,12},{12,8},{16,20},{20,16},{24,28},{28,24},{1,5},{5... | collective-permute-start | bytes 294920 | tf_op jit(solution)/shard_map/ppermute | solution.py:186
  0.8 1.2 %copy-start.1 = (bf16[96,1024]{1,0:T(8,128)(2,1)S(1)}, bf16[96,1024]{1,0:T(8,128)(2,1)}, u32[]{:S(2)}) copy-start(bf16[96,1024]{1,0:T(8,128)(2,1)} %mine.1) | copy-start | bytes 589828
  0.8 1.2 %copy-start.2 = (bf16[2,96,256]{2,1,0:T(8,128)(2,1)S(1)}, bf16[2,96,256]{2,1,0:T(8,128)(2,1)}, u32[]{:S(2)}) copy-start(bf16[2,96,256]{2,1,0:T(8,128)(2,1)} %weight.2) | copy-start | bytes 294916
  2.6 5.4 %copy-start.4 = (s32[1,32,10]{1,0,2:T(1,128)S(1)}, s32[1,32,10]{1,0,2:T(1,128)}, u32[]{:S(2)}) copy-start(s32[1,32,10]{1,0,2:T(1,128)} %param.9) | copy-start | bytes 3844
  2.6 5.7 %collective-permute-start.3 = (bf16[64,256]{1,0:T(8,128)(2,1)S(1)}, bf16[64,256]{1,0:T(8,128)(2,1)S(1)}, u32[]{:S(2)}, u32[]{:S(2)}) collective-permute-start(bf16[64,256]{1,0:T(8,128)(2,1)S(1)} %get-tuple-element.17), channel_id=1, source_target_pairs={{0,28},{4,24},{8,20},{12,16},{16,12},{20,8},{24,4},{28,0},{1,29},{... | collective-permute-start | bytes 98312 | tf_op jit(solution)/shard_map/ppermute | solution.py:203
  6.3 0.7 %copy-start.5 = (s32[1,1,128]{2,1,0:T(1,128)S(1)}, s32[1,1,128]{2,1,0:T(1,128)}, u32[]{:S(2)}) copy-start(s32[1,1,128]{2,1,0:T(1,128)} %param.8) | copy-start | bytes 1540
  6.3 3.3 %collective-permute-start.4 = (bf16[64,256]{1,0:T(8,128)(2,1)S(1)}, bf16[64,256]{1,0:T(8,128)(2,1)S(1)}, u32[]{:S(2)}, u32[]{:S(2)}) collective-permute-start(bf16[64,256]{1,0:T(8,128)(2,1)S(1)} %get-tuple-element.18), channel_id=1, source_target_pairs={{0,12},{4,8},{8,4},{12,0},{16,28},{20,24},{24,20},{28,16},{1,13},{... | collective-permute-start | bytes 98312 | tf_op jit(solution)/shard_map/ppermute | solution.py:203
  6.7 3.3 %collective-permute-start.2 = (bf16[64,256]{1,0:T(8,128)(2,1)S(1)}, bf16[64,256]{1,0:T(8,128)(2,1)S(1)}, u32[]{:S(2)}, u32[]{:S(2)}) collective-permute-start(bf16[64,256]{1,0:T(8,128)(2,1)S(1)} %get-tuple-element.16), channel_id=1, source_target_pairs={{0,20},{4,16},{8,28},{12,24},{16,4},{20,0},{24,12},{28,8},{1,21},{... | collective-permute-start | bytes 98312 | tf_op jit(solution)/shard_map/ppermute | solution.py:203
  6.9 1.1 %collective-permute-start.5 = (s32[1,1,128]{2,1,0:T(1,128)S(1)}, s32[1,1,128]{2,1,0:T(1,128)S(1)}, u32[]{:S(2)}, u32[]{:S(2)}) collective-permute-start(s32[1,1,128]{2,1,0:T(1,128)S(1)} %copy-done.5), channel_id=1, source_target_pairs={{0,4},{4,0},{8,12},{12,8},{16,20},{20,16},{24,28},{28,24},{1,5},{5... | collective-permute-start | bytes 1544 | tf_op jit(solution)/shard_map/ppermute | solution.py:208
  10.2 5.0 %collective-permute-start.6 = (bf16[32,256]{1,0:T(8,128)(2,1)S(1)}, bf16[32,256]{1,0:T(8,128)(2,1)S(1)}, u32[]{:S(2)}, u32[]{:S(2)}) collective-permute-start(bf16[32,256]{1,0:T(8,128)(2,1)S(1)} %get-tuple-element.22), channel_id=1, source_target_pairs={{0,5},{1,6},{2,7},{3,4},{4,2},{5,3},{6,0},{7,1},{8,13},{9,14},{10,... | collective-permute-start | bytes 49160 | tf_op jit(solution)/shard_map/ppermute | solution.py:223
  11.6 5.0 %collective-permute-start.7 = (bf16[32,256]{1,0:T(8,128)(2,1)S(1)}, bf16[32,256]{1,0:T(8,128)(2,1)S(1)}, u32[]{:S(2)}, u32[]{:S(2)}) collective-permute-start(bf16[32,256]{1,0:T(8,128)(2,1)S(1)} %get-tuple-element.23), channel_id=1, source_target_pairs={{0,6},{1,7},{2,4},{3,5},{4,3},{5,2},{6,1},{7,0},{8,14},{9,15},{10,... | collective-permute-start | bytes 49160 | tf_op jit(solution)/shard_map/ppermute | solution.py:223
  12.9 3.8 %collective-permute-start.8 = (bf16[32,256]{1,0:T(8,128)(2,1)S(1)}, bf16[32,256]{1,0:T(8,128)(2,1)S(1)}, u32[]{:S(2)}, u32[]{:S(2)}) collective-permute-start(bf16[32,256]{1,0:T(8,128)(2,1)S(1)} %get-tuple-element.24), channel_id=1, source_target_pairs={{0,7},{1,4},{2,5},{3,6},{4,1},{5,0},{6,3},{7,2},{8,15},{9,12},{10,... | collective-permute-start | bytes 49160 | tf_op jit(solution)/shard_map/ppermute | solution.py:223
  15.2 1.4 %copy-start = (bf16[2,256,256]{2,1,0:T(8,128)(2,1)S(1)}, bf16[2,256,256]{2,1,0:T(8,128)(2,1)}, u32[]{:S(2)}) copy-start(bf16[2,256,256]{2,1,0:T(8,128)(2,1)} %weight.3) | copy-start | bytes 786436
  15.2 1.4 %collective-permute-start.9 = (bf16[96,256]{1,0:T(8,128)(2,1)S(1)}, bf16[96,256]{1,0:T(8,128)(2,1)S(1)}, u32[]{:S(2)}, u32[]{:S(2)}) collective-permute-start(bf16[96,256]{1,0:T(8,128)(2,1)S(1)} %get-tuple-element.25), channel_id=1, source_target_pairs={{0,4},{4,0},{8,12},{12,8},{16,20},{20,16},{24,28},{28,24},{1,5},{5... | collective-permute-start | bytes 147464 | tf_op jit(solution)/shard_map/ppermute | solution.py:234

commit v8 on v7

--- a/solution.py
+++ b/solution.py
@@ -15,7 +15,7 @@
 AHEAD = 2 * 10**9
 COLUMNS_FIRST = (((0,), (0,)), ((), ()))
 VMEM = pl.BlockSpec(memory_space=pltpu.VMEM)
-CHIP_TO = ((2, 3, 0, 1), (3, 2, 1, 0), (1, 0, 3, 2))
+CHIP_TO = ((1, 0, 3, 2), (3, 2, 1, 0), (2, 3, 0, 1))
 DOM_TO = (
     ((1, 2, 3, 0), (2, 3, 0, 1)),
     ((2, 3, 0, 1), (3, 2, 1, 0)),

time: 17.8 us -> 17.8 us (level)
  no operation moved by 1% of the time
where the time goes in v8:
time: 17.8 us; the launch traced here: 17.5 us
  starting transfers between devices  9.97 us (56%)
  waiting for transfers between devices  4.46 us (25%)
  Pallas kernels  2.63 us (15%)
  local copies, waits for them, and re-layouts  0.36 us (2%)
    ppermute x3, starting transfers between devices, on_small_mesh(): lax.ppermute(rows, ('feat', 'dom'), [(feat * dom_count + at, (feat ^ 1) *...  5.01 us
    ppermute x3, starting transfers between devices, on_small_mesh(): lax.ppermute(rows, 'feat', [(2 * at + core, 2 * to + 1 - core) for at, to...  4.16 us
    pallas_call x7, Pallas kernels, call(): pl.pallas_call(kernel, out_shape=outs, in_specs=[VMEM] * len(operands), o...  2.63 us
    ppermute x3, waiting for transfers between devices, on_small_mesh(): lax.ppermute(rows, 'feat', [(2 * at + core, 2 * to + 1 - core) for at, to...  1.7 us
    ppermute x3, waiting for transfers between devices, on_small_mesh(): lax.ppermute(rows, ('feat', 'dom'), [(feat * dom_count + at, (feat ^ 1) *...  1.43 us
    ppermute x1, waiting for transfers between devices, on_small_mesh(): their_boundary = lax.ppermute(held, 'feat', swap)  0.84 us
    ppermute x1, waiting for transfers between devices, on_small_mesh(): their_weight = lax.ppermute(weight_one, 'feat', apart_by(feat_count, 1))  0.48 us
    ppermute x1, starting transfers between devices, on_small_mesh(): theirs = lax.ppermute(features, 'feat', apart_by(feat_count, 1))  0.45 us
  transfers between devices with their start and end apart: 10, of which 5 were waited for; matrix products, arithmetic and copies ran while one was open for 0% of the time, Pallas kernels for 6%

profile of v8, /device:TPU:0, one launch (start us, length us, event | category | flops | bytes accessed | tf_op | source)
XLA Modules:
  0.0 17.5 jit_solution(3579890226909225957)
XLA Ops:
  0.0 0.0 copy-start.3
  0.0 0.5 %collective-permute-start = (bf16[96,1024]{1,0:T(8,128)(2,1)}, bf16[96,1024]{1,0:T(8,128)(2,1)S(1)}, u32[]{:S(2)}, u32[]{:S(2)}) collective-permute-start(bf16[96,1024]{1,0:T(8,128)(2,1)} %mine.1), channel_id=1, source_target_pairs={{0,4},{4,0},{8,12},{12,8},{16,20},{20,16},{24,28},{28,24},{1,5},{5... | collective-permute-start | bytes 589832 | tf_op jit(solution)/shard_map/ppermute | solution.py:187
  0.5 0.1 collective-permute-start.1
  0.5 0.2 %copy-done.3 = s32[1,15,512]{2,0,1:T(1,128)S(1)} copy-done((s32[1,15,512]{2,0,1:T(1,128)S(1)}, s32[1,15,512]{2,0,1:T(1,128)}, u32[]{:S(2)}) %copy-start.3) | copy-done | bytes 30744
  0.8 0.0 copy-start.1
  0.8 0.0 copy-start.2
  0.8 0.7 %layer_one_counts.1.counts = bf16[1024,256]{1,0:T(8,128)(2,1)S(1)} custom-call(s32[4,128]{1,0:T(4,128)S(1)} %halves_of_chips.1.halves, s32[15,1,512]{2,1,0:T(1,128)S(1)} %bitcast.2), custom_call_target="tpu_custom_call" | custom-call | tf_op jit(solution)/shard_map/layer_one_counts/pallas_call | solution.py:157
  1.5 0.5 %collective-permute-done.1.their_weight = bf16[2,96,256]{2,1,0:T(8,128)(2,1)S(1)} collective-permute-done((bf16[2,96,256]{2,1,0:T(8,128)(2,1)}, bf16[2,96,256]{2,1,0:T(8,128)(2,1)S(1)}, u32[]{:S(2)}, u32[]{:S(2)}) %collective-permute-start.1) | collective-permute-done | bytes 98336 | tf_op jit(solution)/shard_map/ppermute | solution.py:186
  2.0 0.0 collective-permute-done.theirs
  2.0 0.0 copy-done.1
  2.0 0.0 copy-done.2
  2.0 0.6 %layer_one_sums.1 = (f32[64,256]{1,0:T(8,128)S(1)}, bf16[64,256]{1,0:T(8,128)(2,1)S(1)}, bf16[64,256]{1,0:T(8,128)(2,1)S(1)}, bf16[64,256]{1,0:T(8,128)(2,1)S(1)}) custom-call(bf16[96,1024]{1,0:T(8,128)(2,1)S(1)} %copy-done.1, bf16[96,1024]{1,0:T(8,128)(2,1)S(1)} %collective-permute-done.theirs, bf16[1024,256]{1,0:T(8,128)(2,1)S(1)} %layer_one_counts.1.counts, ...), custom_call_target="tpu_custom_call" | custom-call | tf_op jit(solution)/shard_map/layer_one_sums/pallas_call | solution.py:157
  2.6 0.0 copy-start.4
  2.6 3.6 %collective-permute-start.3 = (bf16[64,256]{1,0:T(8,128)(2,1)S(1)}, bf16[64,256]{1,0:T(8,128)(2,1)S(1)}, u32[]{:S(2)}, u32[]{:S(2)}) collective-permute-start(bf16[64,256]{1,0:T(8,128)(2,1)S(1)} %get-tuple-element.17), channel_id=1, source_target_pairs={{0,28},{4,24},{8,20},{12,16},{16,12},{20,8},{24,4},{28,0},{1,29},{... | collective-permute-start | bytes 98312 | tf_op jit(solution)/shard_map/ppermute | solution.py:203
  6.3 0.0 copy-start.5
  6.3 0.4 %collective-permute-start.4 = (bf16[64,256]{1,0:T(8,128)(2,1)S(1)}, bf16[64,256]{1,0:T(8,128)(2,1)S(1)}, u32[]{:S(2)}, u32[]{:S(2)}) collective-permute-start(bf16[64,256]{1,0:T(8,128)(2,1)S(1)} %get-tuple-element.18), channel_id=1, source_target_pairs={{0,20},{4,16},{8,28},{12,24},{16,4},{20,0},{24,12},{28,8},{1,21},{... | collective-permute-start | bytes 98312 | tf_op jit(solution)/shard_map/ppermute | solution.py:203
  6.6 0.1 collective-permute-start.2
  6.8 0.1 copy-done.5
  6.9 0.3 %collective-permute-start.5 = (s32[1,1,128]{2,1,0:T(1,128)S(1)}, s32[1,1,128]{2,1,0:T(1,128)S(1)}, u32[]{:S(2)}, u32[]{:S(2)}) collective-permute-start(s32[1,1,128]{2,1,0:T(1,128)S(1)} %copy-done.5), channel_id=1, source_target_pairs={{0,4},{4,0},{8,12},{12,8},{16,20},{20,16},{24,28},{28,24},{1,5},{5... | collective-permute-start | bytes 1544 | tf_op jit(solution)/shard_map/ppermute | solution.py:208
  7.2 0.8 %collective-permute-done.5.boundary = s32[1,1,128]{2,1,0:T(1,128)S(1)} collective-permute-done((s32[1,1,128]{2,1,0:T(1,128)S(1)}, s32[1,1,128]{2,1,0:T(1,128)S(1)}, u32[]{:S(2)}, u32[]{:S(2)}) %collective-permute-start.5) | collective-permute-done | bytes 544 | tf_op jit(solution)/shard_map/ppermute | solution.py:208
  8.0 0.0 copy-done.4
  8.0 0.2 %boundary_and_layer_two_counts.1 = (bf16[128,64]{1,0:T(8,128)(2,1)S(1)}, bf16[32,192]{1,0:T(8,128)(2,1)S(1)}) custom-call(s32[1,1,128]{2,1,0:T(1,128)S(1)} %collective-permute-done.5.boundary, s32[10,1,32]{2,1,0:T(1,128)S(1)} %bitcast.3), custom_call_target="tpu_custom_call" | custom-call | tf_op jit(solution)/shard_map/boundary_and_layer_two_counts/pallas_call | solution.py:157
  8.3 0.0 collective-permute-done.3.refs_1_
  8.3 1.3 %collective-permute-done.4.refs_2_ = bf16[64,256]{1,0:T(8,128)(2,1)S(1)} collective-permute-done((bf16[64,256]{1,0:T(8,128)(2,1)S(1)}, bf16[64,256]{1,0:T(8,128)(2,1)S(1)}, u32[]{:S(2)}, u32[]{:S(2)}) %collective-permute-start.4) | collective-permute-done | bytes 32800 | tf_op jit(solution)/shard_map/ppermute | solution.py:203
  9.6 0.4 %collective-permute-done.2.refs_0_ = bf16[64,256]{1,0:T(8,128)(2,1)S(1)} collective-permute-done((bf16[64,256]{1,0:T(8,128)(2,1)S(1)}, bf16[64,256]{1,0:T(8,128)(2,1)S(1)}, u32[]{:S(2)}, u32[]{:S(2)}) %collective-permute-start.2) | collective-permute-done | bytes 32800 | tf_op jit(solution)/shard_map/ppermute | solution.py:203
  10.0 0.1 hidden_and_boundary_rows.1
  10.1 1.5 %collective-permute-start.6 = (bf16[32,256]{1,0:T(8,128)(2,1)S(1)}, bf16[32,256]{1,0:T(8,128)(2,1)S(1)}, u32[]{:S(2)}, u32[]{:S(2)}) collective-permute-start(bf16[32,256]{1,0:T(8,128)(2,1)S(1)} %get-tuple-element.22), channel_id=1, source_target_pairs={{0,5},{1,6},{2,7},{3,4},{4,2},{5,3},{6,0},{7,1},{8,13},{9,14},{10,... | collective-permute-start | bytes 49160 | tf_op jit(solution)/shard_map/ppermute | solution.py:223
  11.6 1.2 %collective-permute-start.7 = (bf16[32,256]{1,0:T(8,128)(2,1)S(1)}, bf16[32,256]{1,0:T(8,128)(2,1)S(1)}, u32[]{:S(2)}, u32[]{:S(2)}) collective-permute-start(bf16[32,256]{1,0:T(8,128)(2,1)S(1)} %get-tuple-element.23), channel_id=1, source_target_pairs={{0,6},{1,7},{2,4},{3,5},{4,3},{5,2},{6,1},{7,0},{8,14},{9,15},{10,... | collective-permute-start | bytes 49160 | tf_op jit(solution)/shard_map/ppermute | solution.py:223
  12.8 2.3 %collective-permute-start.8 = (bf16[32,256]{1,0:T(8,128)(2,1)S(1)}, bf16[32,256]{1,0:T(8,128)(2,1)S(1)}, u32[]{:S(2)}, u32[]{:S(2)}) collective-permute-start(bf16[32,256]{1,0:T(8,128)(2,1)S(1)} %get-tuple-element.24), channel_id=1, source_target_pairs={{0,7},{1,4},{2,5},{3,6},{4,1},{5,0},{6,3},{7,2},{8,15},{9,12},{10,... | collective-permute-start | bytes 49160 | tf_op jit(solution)/shard_map/ppermute | solution.py:223
  15.2 0.0 copy-start
  15.2 0.0 collective-permute-start.9
  15.2 0.0 collective-permute-done.6.refs_0_
  15.2 1.4 %collective-permute-done.7.refs_1_ = bf16[32,256]{1,0:T(8,128)(2,1)S(1)} collective-permute-done((bf16[32,256]{1,0:T(8,128)(2,1)S(1)}, bf16[32,256]{1,0:T(8,128)(2,1)S(1)}, u32[]{:S(2)}, u32[]{:S(2)}) %collective-permute-start.7) | collective-permute-done | bytes 16416 | tf_op jit(solution)/shard_map/ppermute | solution.py:223
  16.6 0.0 collective-permute-done.8.last
  16.6 0.0 collective-permute-done.9.hidden
  16.6 0.0 copy-done
  16.6 0.9 %layer_two_far.1 = bf16[1,32,256]{2,1,0:T(8,128)(2,1)} custom-call(bf16[64,256]{1,0:T(8,128)(2,1)S(1)} %far_rows.1.far, bf16[32,256]{1,0:T(8,128)(2,1)S(1)} %collective-permute-done.8.last, bf16[96,256]{1,0:T(8,128)(2,1)S(1)} %collective-permute-done.9.hidden, bf16[32,192]{1,0:T(8,128)(2,1)S(1)} %get-tuple-element.26.counts, bf16[2,256,256]{2,1,0:T(8,128)(2,1)S(1)} %copy-done), custom_call_target="tpu_custom_call" | custom-call | tf_op jit(solution)/shard_map/layer_two_far/pallas_call | solution.py:157
  (2 shorter events, 0.0 us)
Async XLA Ops:
  0.0 0.8 %copy-start.3 = (s32[1,15,512]{2,0,1:T(1,128)S(1)}, s32[1,15,512]{2,0,1:T(1,128)}, u32[]{:S(2)}) copy-start(s32[1,15,512]{2,0,1:T(1,128)} %param.7) | copy-start | bytes 92164
  0.0 2.0 %collective-permute-start = (bf16[96,1024]{1,0:T(8,128)(2,1)}, bf16[96,1024]{1,0:T(8,128)(2,1)S(1)}, u32[]{:S(2)}, u32[]{:S(2)}) collective-permute-start(bf16[96,1024]{1,0:T(8,128)(2,1)} %mine.1), channel_id=1, source_target_pairs={{0,4},{4,0},{8,12},{12,8},{16,20},{20,16},{24,28},{28,24},{1,5},{5... | collective-permute-start | bytes 589832 | tf_op jit(solution)/shard_map/ppermute | solution.py:187
  0.5 1.5 %collective-permute-start.1 = (bf16[2,96,256]{2,1,0:T(8,128)(2,1)}, bf16[2,96,256]{2,1,0:T(8,128)(2,1)S(1)}, u32[]{:S(2)}, u32[]{:S(2)}) collective-permute-start(bf16[2,96,256]{2,1,0:T(8,128)(2,1)} %weight.2), channel_id=1, source_target_pairs={{0,4},{4,0},{8,12},{12,8},{16,20},{20,16},{24,28},{28,24},{1,5},{5... | collective-permute-start | bytes 294920 | tf_op jit(solution)/shard_map/ppermute | solution.py:186
  0.8 1.2 %copy-start.1 = (bf16[96,1024]{1,0:T(8,128)(2,1)S(1)}, bf16[96,1024]{1,0:T(8,128)(2,1)}, u32[]{:S(2)}) copy-start(bf16[96,1024]{1,0:T(8,128)(2,1)} %mine.1) | copy-start | bytes 589828
  0.8 1.2 %copy-start.2 = (bf16[2,96,256]{2,1,0:T(8,128)(2,1)S(1)}, bf16[2,96,256]{2,1,0:T(8,128)(2,1)}, u32[]{:S(2)}) copy-start(bf16[2,96,256]{2,1,0:T(8,128)(2,1)} %weight.2) | copy-start | bytes 294916
  2.6 5.4 %copy-start.4 = (s32[1,32,10]{1,0,2:T(1,128)S(1)}, s32[1,32,10]{1,0,2:T(1,128)}, u32[]{:S(2)}) copy-start(s32[1,32,10]{1,0,2:T(1,128)} %param.9) | copy-start | bytes 3844
  2.6 5.7 %collective-permute-start.3 = (bf16[64,256]{1,0:T(8,128)(2,1)S(1)}, bf16[64,256]{1,0:T(8,128)(2,1)S(1)}, u32[]{:S(2)}, u32[]{:S(2)}) collective-permute-start(bf16[64,256]{1,0:T(8,128)(2,1)S(1)} %get-tuple-element.17), channel_id=1, source_target_pairs={{0,28},{4,24},{8,20},{12,16},{16,12},{20,8},{24,4},{28,0},{1,29},{... | collective-permute-start | bytes 98312 | tf_op jit(solution)/shard_map/ppermute | solution.py:203
  6.3 0.7 %copy-start.5 = (s32[1,1,128]{2,1,0:T(1,128)S(1)}, s32[1,1,128]{2,1,0:T(1,128)}, u32[]{:S(2)}) copy-start(s32[1,1,128]{2,1,0:T(1,128)} %param.8) | copy-start | bytes 1540
  6.3 3.3 %collective-permute-start.4 = (bf16[64,256]{1,0:T(8,128)(2,1)S(1)}, bf16[64,256]{1,0:T(8,128)(2,1)S(1)}, u32[]{:S(2)}, u32[]{:S(2)}) collective-permute-start(bf16[64,256]{1,0:T(8,128)(2,1)S(1)} %get-tuple-element.18), channel_id=1, source_target_pairs={{0,20},{4,16},{8,28},{12,24},{16,4},{20,0},{24,12},{28,8},{1,21},{... | collective-permute-start | bytes 98312 | tf_op jit(solution)/shard_map/ppermute | solution.py:203
  6.6 3.3 %collective-permute-start.2 = (bf16[64,256]{1,0:T(8,128)(2,1)S(1)}, bf16[64,256]{1,0:T(8,128)(2,1)S(1)}, u32[]{:S(2)}, u32[]{:S(2)}) collective-permute-start(bf16[64,256]{1,0:T(8,128)(2,1)S(1)} %get-tuple-element.16), channel_id=1, source_target_pairs={{0,12},{4,8},{8,4},{12,0},{16,28},{20,24},{24,20},{28,16},{1,13},{... | collective-permute-start | bytes 98312 | tf_op jit(solution)/shard_map/ppermute | solution.py:203
  6.9 1.1 %collective-permute-start.5 = (s32[1,1,128]{2,1,0:T(1,128)S(1)}, s32[1,1,128]{2,1,0:T(1,128)S(1)}, u32[]{:S(2)}, u32[]{:S(2)}) collective-permute-start(s32[1,1,128]{2,1,0:T(1,128)S(1)} %copy-done.5), channel_id=1, source_target_pairs={{0,4},{4,0},{8,12},{12,8},{16,20},{20,16},{24,28},{28,24},{1,5},{5... | collective-permute-start | bytes 1544 | tf_op jit(solution)/shard_map/ppermute | solution.py:208
  10.1 5.0 %collective-permute-start.6 = (bf16[32,256]{1,0:T(8,128)(2,1)S(1)}, bf16[32,256]{1,0:T(8,128)(2,1)S(1)}, u32[]{:S(2)}, u32[]{:S(2)}) collective-permute-start(bf16[32,256]{1,0:T(8,128)(2,1)S(1)} %get-tuple-element.22), channel_id=1, source_target_pairs={{0,5},{1,6},{2,7},{3,4},{4,2},{5,3},{6,0},{7,1},{8,13},{9,14},{10,... | collective-permute-start | bytes 49160 | tf_op jit(solution)/shard_map/ppermute | solution.py:223
  11.6 5.0 %collective-permute-start.7 = (bf16[32,256]{1,0:T(8,128)(2,1)S(1)}, bf16[32,256]{1,0:T(8,128)(2,1)S(1)}, u32[]{:S(2)}, u32[]{:S(2)}) collective-permute-start(bf16[32,256]{1,0:T(8,128)(2,1)S(1)} %get-tuple-element.23), channel_id=1, source_target_pairs={{0,6},{1,7},{2,4},{3,5},{4,3},{5,2},{6,1},{7,0},{8,14},{9,15},{10,... | collective-permute-start | bytes 49160 | tf_op jit(solution)/shard_map/ppermute | solution.py:223
  12.8 3.8 %collective-permute-start.8 = (bf16[32,256]{1,0:T(8,128)(2,1)S(1)}, bf16[32,256]{1,0:T(8,128)(2,1)S(1)}, u32[]{:S(2)}, u32[]{:S(2)}) collective-permute-start(bf16[32,256]{1,0:T(8,128)(2,1)S(1)} %get-tuple-element.24), channel_id=1, source_target_pairs={{0,7},{1,4},{2,5},{3,6},{4,1},{5,0},{6,3},{7,2},{8,15},{9,12},{10,... | collective-permute-start | bytes 49160 | tf_op jit(solution)/shard_map/ppermute | solution.py:223
  15.2 1.4 %copy-start = (bf16[2,256,256]{2,1,0:T(8,128)(2,1)S(1)}, bf16[2,256,256]{2,1,0:T(8,128)(2,1)}, u32[]{:S(2)}) copy-start(bf16[2,256,256]{2,1,0:T(8,128)(2,1)} %weight.3) | copy-start | bytes 786436
  15.2 1.4 %collective-permute-start.9 = (bf16[96,256]{1,0:T(8,128)(2,1)S(1)}, bf16[96,256]{1,0:T(8,128)(2,1)S(1)}, u32[]{:S(2)}, u32[]{:S(2)}) collective-permute-start(bf16[96,256]{1,0:T(8,128)(2,1)S(1)} %get-tuple-element.25), channel_id=1, source_target_pairs={{0,4},{4,0},{8,12},{12,8},{16,20},{20,16},{24,28},{28,24},{1,5},{5... | collective-permute-start | bytes 147464 | tf_op jit(solution)/shard_map/ppermute | solution.py:234

commit v9 on v8

--- a/solution.py
+++ b/solution.py
@@ -15,10 +15,10 @@
 AHEAD = 2 * 10**9
 COLUMNS_FIRST = (((0,), (0,)), ((), ()))
 VMEM = pl.BlockSpec(memory_space=pltpu.VMEM)
-CHIP_TO = ((1, 0, 3, 2), (3, 2, 1, 0), (2, 3, 0, 1))
+CHIP_TO = ((3, 2, 1, 0), (1, 3, 0, 2), (2, 0, 3, 1))
 DOM_TO = (
-    ((1, 2, 3, 0), (2, 3, 0, 1)),
-    ((2, 3, 0, 1), (3, 2, 1, 0)),
+    ((1, 2, 3, 0), (2, 3, 1, 0)),
+    ((2, 3, 0, 1), (3, 2, 0, 1)),
     ((3, 0, 1, 2), (1, 0, 3, 2)),
 )
 

time: 17.8 us -> 17.7 us (level)
  starting transfers between devices: 9.97 us -> 11.6 us
  waiting for transfers between devices: 4.46 us -> 3.01 us
    ppermute x3, waiting for transfers between devices: 1.7 us -> 0.25 us  [on_small_mesh(): lax.ppermute(rows, 'feat', [(2 * at + core, 2 * to + 1 - core) for at, to...]
    ppermute x3, starting transfers between devices: 4.16 us -> 5.35 us  [on_small_mesh(): lax.ppermute(rows, 'feat', [(2 * at + core, 2 * to + 1 - core) for at, to...]
    ppermute x3, starting transfers between devices: 5.01 us -> 5.44 us  [on_small_mesh(): lax.ppermute(rows, ('feat', 'dom'), [(feat * dom_count + at, (feat ^ 1) *...]
where the time goes in v9:
time: 17.7 us; the launch traced here: 17.5 us
  starting transfers between devices  11.6 us (66%)
  waiting for transfers between devices  3.01 us (17%)
  Pallas kernels  2.63 us (15%)
  local copies, waits for them, and re-layouts  0.25 us (1%)
    ppermute x3, starting transfers between devices, on_small_mesh(): lax.ppermute(rows, ('feat', 'dom'), [(feat * dom_count + at, (feat ^ 1) *...  5.44 us
    ppermute x3, starting transfers between devices, on_small_mesh(): lax.ppermute(rows, 'feat', [(2 * at + core, 2 * to + 1 - core) for at, to...  5.35 us
    pallas_call x7, Pallas kernels, call(): pl.pallas_call(kernel, out_shape=outs, in_specs=[VMEM] * len(operands), o...  2.63 us
    ppermute x3, waiting for transfers between devices, on_small_mesh(): lax.ppermute(rows, ('feat', 'dom'), [(feat * dom_count + at, (feat ^ 1) *...  1.43 us
    ppermute x1, waiting for transfers between devices, on_small_mesh(): their_boundary = lax.ppermute(held, 'feat', swap)  0.84 us
    ppermute x1, waiting for transfers between devices, on_small_mesh(): their_weight = lax.ppermute(weight_one, 'feat', apart_by(feat_count, 1))  0.48 us
    ppermute x1, starting transfers between devices, on_small_mesh(): theirs = lax.ppermute(features, 'feat', apart_by(feat_count, 1))  0.45 us
  transfers between devices with their start and end apart: 10, of which 5 were waited for; matrix products, arithmetic and copies ran while one was open for 0% of the time, Pallas kernels for 6%

profile of v9, /device:TPU:0, one launch (start us, length us, event | category | flops | bytes accessed | tf_op | source)
XLA Modules:
  0.0 17.5 jit_solution(3112073996271383208)
XLA Ops:
  0.0 0.0 copy-start.3
  0.0 0.5 %collective-permute-start = (bf16[96,1024]{1,0:T(8,128)(2,1)}, bf16[96,1024]{1,0:T(8,128)(2,1)S(1)}, u32[]{:S(2)}, u32[]{:S(2)}) collective-permute-start(bf16[96,1024]{1,0:T(8,128)(2,1)} %mine.1), channel_id=1, source_target_pairs={{0,4},{4,0},{8,12},{12,8},{16,20},{20,16},{24,28},{28,24},{1,5},{5... | collective-permute-start | bytes 589832 | tf_op jit(solution)/shard_map/ppermute | solution.py:187
  0.5 0.1 collective-permute-start.1
  0.5 0.2 %copy-done.3 = s32[1,15,512]{2,0,1:T(1,128)S(1)} copy-done((s32[1,15,512]{2,0,1:T(1,128)S(1)}, s32[1,15,512]{2,0,1:T(1,128)}, u32[]{:S(2)}) %copy-start.3) | copy-done | bytes 30744
  0.8 0.0 copy-start.1
  0.8 0.0 copy-start.2
  0.8 0.7 %layer_one_counts.1.counts = bf16[1024,256]{1,0:T(8,128)(2,1)S(1)} custom-call(s32[4,128]{1,0:T(4,128)S(1)} %halves_of_chips.1.halves, s32[15,1,512]{2,1,0:T(1,128)S(1)} %bitcast.2), custom_call_target="tpu_custom_call" | custom-call | tf_op jit(solution)/shard_map/layer_one_counts/pallas_call | solution.py:157
  1.5 0.5 %collective-permute-done.1.their_weight = bf16[2,96,256]{2,1,0:T(8,128)(2,1)S(1)} collective-permute-done((bf16[2,96,256]{2,1,0:T(8,128)(2,1)}, bf16[2,96,256]{2,1,0:T(8,128)(2,1)S(1)}, u32[]{:S(2)}, u32[]{:S(2)}) %collective-permute-start.1) | collective-permute-done | bytes 98336 | tf_op jit(solution)/shard_map/ppermute | solution.py:186
  2.0 0.0 collective-permute-done.theirs
  2.0 0.0 copy-done.1
  2.0 0.0 copy-done.2
  2.0 0.6 %layer_one_sums.1 = (f32[64,256]{1,0:T(8,128)S(1)}, bf16[64,256]{1,0:T(8,128)(2,1)S(1)}, bf16[64,256]{1,0:T(8,128)(2,1)S(1)}, bf16[64,256]{1,0:T(8,128)(2,1)S(1)}) custom-call(bf16[96,1024]{1,0:T(8,128)(2,1)S(1)} %copy-done.1, bf16[96,1024]{1,0:T(8,128)(2,1)S(1)} %collective-permute-done.theirs, bf16[1024,256]{1,0:T(8,128)(2,1)S(1)} %layer_one_counts.1.counts, ...), custom_call_target="tpu_custom_call" | custom-call | tf_op jit(solution)/shard_map/layer_one_sums/pallas_call | solution.py:157
  2.6 0.0 copy-start.4
  2.6 2.7 %collective-permute-start.3 = (bf16[64,256]{1,0:T(8,128)(2,1)S(1)}, bf16[64,256]{1,0:T(8,128)(2,1)S(1)}, u32[]{:S(2)}, u32[]{:S(2)}) collective-permute-start(bf16[64,256]{1,0:T(8,128)(2,1)S(1)} %get-tuple-element.17), channel_id=1, source_target_pairs={{0,12},{4,8},{8,28},{12,24},{16,4},{20,0},{24,20},{28,16},{1,13},{... | collective-permute-start | bytes 98312 | tf_op jit(solution)/shard_map/ppermute | solution.py:203
  5.3 0.0 copy-start.5
  5.3 0.1 collective-permute-start.4
  5.4 2.6 %collective-permute-start.2 = (bf16[64,256]{1,0:T(8,128)(2,1)S(1)}, bf16[64,256]{1,0:T(8,128)(2,1)S(1)}, u32[]{:S(2)}, u32[]{:S(2)}) collective-permute-start(bf16[64,256]{1,0:T(8,128)(2,1)S(1)} %get-tuple-element.16), channel_id=1, source_target_pairs={{0,28},{4,24},{8,20},{12,16},{16,12},{20,8},{24,4},{28,0},{1,29},{... | collective-permute-start | bytes 98312 | tf_op jit(solution)/shard_map/ppermute | solution.py:203
  8.0 0.0 copy-done.5
  8.0 0.3 %collective-permute-start.5 = (s32[1,1,128]{2,1,0:T(1,128)S(1)}, s32[1,1,128]{2,1,0:T(1,128)S(1)}, u32[]{:S(2)}, u32[]{:S(2)}) collective-permute-start(s32[1,1,128]{2,1,0:T(1,128)S(1)} %copy-done.5), channel_id=1, source_target_pairs={{0,4},{4,0},{8,12},{12,8},{16,20},{20,16},{24,28},{28,24},{1,5},{5... | collective-permute-start | bytes 1544 | tf_op jit(solution)/shard_map/ppermute | solution.py:208
  8.3 0.8 %collective-permute-done.5.boundary = s32[1,1,128]{2,1,0:T(1,128)S(1)} collective-permute-done((s32[1,1,128]{2,1,0:T(1,128)S(1)}, s32[1,1,128]{2,1,0:T(1,128)S(1)}, u32[]{:S(2)}, u32[]{:S(2)}) %collective-permute-start.5) | collective-permute-done | bytes 544 | tf_op jit(solution)/shard_map/ppermute | solution.py:208
  9.1 0.0 copy-done.4
  9.1 0.2 %boundary_and_layer_two_counts.1 = (bf16[128,64]{1,0:T(8,128)(2,1)S(1)}, bf16[32,192]{1,0:T(8,128)(2,1)S(1)}) custom-call(s32[1,1,128]{2,1,0:T(1,128)S(1)} %collective-permute-done.5.boundary, s32[10,1,32]{2,1,0:T(1,128)S(1)} %bitcast.3), custom_call_target="tpu_custom_call" | custom-call | tf_op jit(solution)/shard_map/boundary_and_layer_two_counts/pallas_call | solution.py:157
  9.4 0.0 collective-permute-done.3.refs_1_
  9.4 0.0 collective-permute-done.4.refs_2_
  9.4 0.2 %collective-permute-done.2.refs_0_ = bf16[64,256]{1,0:T(8,128)(2,1)S(1)} collective-permute-done((bf16[64,256]{1,0:T(8,128)(2,1)S(1)}, bf16[64,256]{1,0:T(8,128)(2,1)S(1)}, u32[]{:S(2)}, u32[]{:S(2)}) %collective-permute-start.2) | collective-permute-done | bytes 32800 | tf_op jit(solution)/shard_map/ppermute | solution.py:203
  9.6 0.1 hidden_and_boundary_rows.1
  9.8 1.8 %collective-permute-start.6 = (bf16[32,256]{1,0:T(8,128)(2,1)S(1)}, bf16[32,256]{1,0:T(8,128)(2,1)S(1)}, u32[]{:S(2)}, u32[]{:S(2)}) collective-permute-start(bf16[32,256]{1,0:T(8,128)(2,1)S(1)} %get-tuple-element.22), channel_id=1, source_target_pairs={{0,5},{1,6},{2,7},{3,4},{4,2},{5,3},{6,1},{7,0},{8,13},{9,14},{10,... | collective-permute-start | bytes 49160 | tf_op jit(solution)/shard_map/ppermute | solution.py:223
  11.6 1.3 %collective-permute-start.7 = (bf16[32,256]{1,0:T(8,128)(2,1)S(1)}, bf16[32,256]{1,0:T(8,128)(2,1)S(1)}, u32[]{:S(2)}, u32[]{:S(2)}) collective-permute-start(bf16[32,256]{1,0:T(8,128)(2,1)S(1)} %get-tuple-element.23), channel_id=1, source_target_pairs={{0,6},{1,7},{2,4},{3,5},{4,3},{5,2},{6,0},{7,1},{8,14},{9,15},{10,... | collective-permute-start | bytes 49160 | tf_op jit(solution)/shard_map/ppermute | solution.py:223
  12.9 2.3 %collective-permute-start.8 = (bf16[32,256]{1,0:T(8,128)(2,1)S(1)}, bf16[32,256]{1,0:T(8,128)(2,1)S(1)}, u32[]{:S(2)}, u32[]{:S(2)}) collective-permute-start(bf16[32,256]{1,0:T(8,128)(2,1)S(1)} %get-tuple-element.24), channel_id=1, source_target_pairs={{0,7},{1,4},{2,5},{3,6},{4,1},{5,0},{6,3},{7,2},{8,15},{9,12},{10,... | collective-permute-start | bytes 49160 | tf_op jit(solution)/shard_map/ppermute | solution.py:223
  15.2 0.0 copy-start
  15.2 0.0 collective-permute-start.9
  15.2 0.0 collective-permute-done.6.refs_0_
  15.2 0.4 %collective-permute-done.7.refs_1_ = bf16[32,256]{1,0:T(8,128)(2,1)S(1)} collective-permute-done((bf16[32,256]{1,0:T(8,128)(2,1)S(1)}, bf16[32,256]{1,0:T(8,128)(2,1)S(1)}, u32[]{:S(2)}, u32[]{:S(2)}) %collective-permute-start.7) | collective-permute-done | bytes 16416 | tf_op jit(solution)/shard_map/ppermute | solution.py:223
  15.7 1.0 %collective-permute-done.8.last = bf16[32,256]{1,0:T(8,128)(2,1)S(1)} collective-permute-done((bf16[32,256]{1,0:T(8,128)(2,1)S(1)}, bf16[32,256]{1,0:T(8,128)(2,1)S(1)}, u32[]{:S(2)}, u32[]{:S(2)}) %collective-permute-start.8) | collective-permute-done | bytes 16416 | tf_op jit(solution)/shard_map/ppermute | solution.py:223
  16.7 0.0 collective-permute-done.9.hidden
  16.7 0.0 copy-done
  16.7 0.9 %layer_two_far.1 = bf16[1,32,256]{2,1,0:T(8,128)(2,1)} custom-call(bf16[64,256]{1,0:T(8,128)(2,1)S(1)} %far_rows.1.far, bf16[32,256]{1,0:T(8,128)(2,1)S(1)} %collective-permute-done.8.last, bf16[96,256]{1,0:T(8,128)(2,1)S(1)} %collective-permute-done.9.hidden, bf16[32,192]{1,0:T(8,128)(2,1)S(1)} %get-tuple-element.26.counts, bf16[2,256,256]{2,1,0:T(8,128)(2,1)S(1)} %copy-done), custom_call_target="tpu_custom_call" | custom-call | tf_op jit(solution)/shard_map/layer_two_far/pallas_call | solution.py:157
  (2 shorter events, 0.0 us)
Async XLA Ops:
  0.0 0.8 %copy-start.3 = (s32[1,15,512]{2,0,1:T(1,128)S(1)}, s32[1,15,512]{2,0,1:T(1,128)}, u32[]{:S(2)}) copy-start(s32[1,15,512]{2,0,1:T(1,128)} %param.7) | copy-start | bytes 92164
  0.0 2.0 %collective-permute-start = (bf16[96,1024]{1,0:T(8,128)(2,1)}, bf16[96,1024]{1,0:T(8,128)(2,1)S(1)}, u32[]{:S(2)}, u32[]{:S(2)}) collective-permute-start(bf16[96,1024]{1,0:T(8,128)(2,1)} %mine.1), channel_id=1, source_target_pairs={{0,4},{4,0},{8,12},{12,8},{16,20},{20,16},{24,28},{28,24},{1,5},{5... | collective-permute-start | bytes 589832 | tf_op jit(solution)/shard_map/ppermute | solution.py:187
  0.5 1.5 %collective-permute-start.1 = (bf16[2,96,256]{2,1,0:T(8,128)(2,1)}, bf16[2,96,256]{2,1,0:T(8,128)(2,1)S(1)}, u32[]{:S(2)}, u32[]{:S(2)}) collective-permute-start(bf16[2,96,256]{2,1,0:T(8,128)(2,1)} %weight.2), channel_id=1, source_target_pairs={{0,4},{4,0},{8,12},{12,8},{16,20},{20,16},{24,28},{28,24},{1,5},{5... | collective-permute-start | bytes 294920 | tf_op jit(solution)/shard_map/ppermute | solution.py:186
  0.8 1.2 %copy-start.1 = (bf16[96,1024]{1,0:T(8,128)(2,1)S(1)}, bf16[96,1024]{1,0:T(8,128)(2,1)}, u32[]{:S(2)}) copy-start(bf16[96,1024]{1,0:T(8,128)(2,1)} %mine.1) | copy-start | bytes 589828
  0.8 1.2 %copy-start.2 = (bf16[2,96,256]{2,1,0:T(8,128)(2,1)S(1)}, bf16[2,96,256]{2,1,0:T(8,128)(2,1)}, u32[]{:S(2)}) copy-start(bf16[2,96,256]{2,1,0:T(8,128)(2,1)} %weight.2) | copy-start | bytes 294916
  2.6 6.5 %copy-start.4 = (s32[1,32,10]{1,0,2:T(1,128)S(1)}, s32[1,32,10]{1,0,2:T(1,128)}, u32[]{:S(2)}) copy-start(s32[1,32,10]{1,0,2:T(1,128)} %param.9) | copy-start | bytes 3844
  2.6 6.7 %collective-permute-start.3 = (bf16[64,256]{1,0:T(8,128)(2,1)S(1)}, bf16[64,256]{1,0:T(8,128)(2,1)S(1)}, u32[]{:S(2)}, u32[]{:S(2)}) collective-permute-start(bf16[64,256]{1,0:T(8,128)(2,1)S(1)} %get-tuple-element.17), channel_id=1, source_target_pairs={{0,12},{4,8},{8,28},{12,24},{16,4},{20,0},{24,20},{28,16},{1,13},{... | collective-permute-start | bytes 98312 | tf_op jit(solution)/shard_map/ppermute | solution.py:203
  5.3 2.7 %copy-start.5 = (s32[1,1,128]{2,1,0:T(1,128)S(1)}, s32[1,1,128]{2,1,0:T(1,128)}, u32[]{:S(2)}) copy-start(s32[1,1,128]{2,1,0:T(1,128)} %param.8) | copy-start | bytes 1540
  5.3 4.1 %collective-permute-start.4 = (bf16[64,256]{1,0:T(8,128)(2,1)S(1)}, bf16[64,256]{1,0:T(8,128)(2,1)S(1)}, u32[]{:S(2)}, u32[]{:S(2)}) collective-permute-start(bf16[64,256]{1,0:T(8,128)(2,1)S(1)} %get-tuple-element.18), channel_id=1, source_target_pairs={{0,20},{4,16},{8,4},{12,0},{16,28},{20,24},{24,12},{28,8},{1,21},{... | collective-permute-start | bytes 98312 | tf_op jit(solution)/shard_map/ppermute | solution.py:203
  5.4 4.2 %collective-permute-start.2 = (bf16[64,256]{1,0:T(8,128)(2,1)S(1)}, bf16[64,256]{1,0:T(8,128)(2,1)S(1)}, u32[]{:S(2)}, u32[]{:S(2)}) collective-permute-start(bf16[64,256]{1,0:T(8,128)(2,1)S(1)} %get-tuple-element.16), channel_id=1, source_target_pairs={{0,28},{4,24},{8,20},{12,16},{16,12},{20,8},{24,4},{28,0},{1,29},{... | collective-permute-start | bytes 98312 | tf_op jit(solution)/shard_map/ppermute | solution.py:203
  8.0 1.1 %collective-permute-start.5 = (s32[1,1,128]{2,1,0:T(1,128)S(1)}, s32[1,1,128]{2,1,0:T(1,128)S(1)}, u32[]{:S(2)}, u32[]{:S(2)}) collective-permute-start(s32[1,1,128]{2,1,0:T(1,128)S(1)} %copy-done.5), channel_id=1, source_target_pairs={{0,4},{4,0},{8,12},{12,8},{16,20},{20,16},{24,28},{28,24},{1,5},{5... | collective-permute-start | bytes 1544 | tf_op jit(solution)/shard_map/ppermute | solution.py:208
  9.8 5.4 %collective-permute-start.6 = (bf16[32,256]{1,0:T(8,128)(2,1)S(1)}, bf16[32,256]{1,0:T(8,128)(2,1)S(1)}, u32[]{:S(2)}, u32[]{:S(2)}) collective-permute-start(bf16[32,256]{1,0:T(8,128)(2,1)S(1)} %get-tuple-element.22), channel_id=1, source_target_pairs={{0,5},{1,6},{2,7},{3,4},{4,2},{5,3},{6,1},{7,0},{8,13},{9,14},{10,... | collective-permute-start | bytes 49160 | tf_op jit(solution)/shard_map/ppermute | solution.py:223
  11.6 4.1 %collective-permute-start.7 = (bf16[32,256]{1,0:T(8,128)(2,1)S(1)}, bf16[32,256]{1,0:T(8,128)(2,1)S(1)}, u32[]{:S(2)}, u32[]{:S(2)}) collective-permute-start(bf16[32,256]{1,0:T(8,128)(2,1)S(1)} %get-tuple-element.23), channel_id=1, source_target_pairs={{0,6},{1,7},{2,4},{3,5},{4,3},{5,2},{6,0},{7,1},{8,14},{9,15},{10,... | collective-permute-start | bytes 49160 | tf_op jit(solution)/shard_map/ppermute | solution.py:223
  12.9 3.8 %collective-permute-start.8 = (bf16[32,256]{1,0:T(8,128)(2,1)S(1)}, bf16[32,256]{1,0:T(8,128)(2,1)S(1)}, u32[]{:S(2)}, u32[]{:S(2)}) collective-permute-start(bf16[32,256]{1,0:T(8,128)(2,1)S(1)} %get-tuple-element.24), channel_id=1, source_target_pairs={{0,7},{1,4},{2,5},{3,6},{4,1},{5,0},{6,3},{7,2},{8,15},{9,12},{10,... | collective-permute-start | bytes 49160 | tf_op jit(solution)/shard_map/ppermute | solution.py:223
  15.2 1.4 %copy-start = (bf16[2,256,256]{2,1,0:T(8,128)(2,1)S(1)}, bf16[2,256,256]{2,1,0:T(8,128)(2,1)}, u32[]{:S(2)}) copy-start(bf16[2,256,256]{2,1,0:T(8,128)(2,1)} %weight.3) | copy-start | bytes 786436
  15.2 1.4 %collective-permute-start.9 = (bf16[96,256]{1,0:T(8,128)(2,1)S(1)}, bf16[96,256]{1,0:T(8,128)(2,1)S(1)}, u32[]{:S(2)}, u32[]{:S(2)}) collective-permute-start(bf16[96,256]{1,0:T(8,128)(2,1)S(1)} %get-tuple-element.25), channel_id=1, source_target_pairs={{0,4},{4,0},{8,12},{12,8},{16,20},{20,16},{24,28},{28,24},{1,5},{5... | collective-permute-start | bytes 147464 | tf_op jit(solution)/shard_map/ppermute | solution.py:234
